TPU v7x, 32 devices: a whole 2x2x4 slice. The times are simulated.
32 devices in a mesh: grp: 4 (over y, x), dev: 8 (over z, core).
Axes of the slice: x: 2, y: 2, z: 4, core: 2. Of those that a mesh axis runs over, the one named last changes fastest.
Arguments:
- locations: float32 [32, 3, 256], P(('grp', 'dev')), may hold values from 0 to 1
- neighbours: int32 [32, 4], P(('grp', 'dev')), may hold values from -1 to 30, as said below
- observations: float32 [32, 8, 256], P(('grp', 'dev')), may hold values from -63 to 63
- noise_prec: float32 [32, 8, 256], P(('grp', 'dev')), may hold values from 0.5 to 4
Outputs:
- solution: float32 [32, 8, 256], P(('grp', 'dev'))
- residual: float32 [32, 8, 256], P(('grp', 'dev'))
Inputs may be any that keep to these rules, and one draw needn't show every extreme that they name: `neighbours`: row b holds b - 1 in slot 0 (-1 for block 0); in slot 1 a block drawn from the range from max(b - 1, 0) * 1 to b - 2, or -1 where that range is empty; in slots 2 and 3 two different blocks below min(8, max(b - 1, 0)), -1 in a slot where fewer exist. All listed blocks of a row differ.
All inputs are finite; a program needn't handle non-finite values.
Results may differ from a plain program's by a relative error of at most 0.0003.
Values sent between devices are 32-bit elements; how exact they have to be, the bound alone decides.
No kernel may reach another device: no remote copies, remote signals or barrier semaphores. Data moves between devices by JAX's collectives and lax.ppermute only.
A program may use at most 128 MiB of HBM per device.

v0:
```python
import math

import jax
import jax.numpy as jnp
from jax import lax
from jax.sharding import PartitionSpec as P

ITERS = 2


SCALE_LENGTH = 0.5
NUGGET = 0.5
SQRT_THREE = math.sqrt(3.0)
HIGHEST = lax.Precision.HIGHEST


def from_behind(block, axis, distance):
    devices = range(lax.axis_size(axis))
    route = [(i - distance, i) for i in devices if i - distance in devices]
    return lax.ppermute(block, axis, route)


def from_root(value, axis, source):
    kept = jnp.where(lax.axis_index(axis) == source, value, 0).astype(value.dtype)
    return lax.psum(kept, axis)


def kernel_factor(point_set, point_mask, own_size):
    offsets = point_set[:, :, None] - point_set[:, None, :]
    distance = jnp.sqrt(jnp.sum(offsets * offsets, axis=0))
    scaled = SQRT_THREE / SCALE_LENGTH * distance
    covariance = (1.0 + scaled) * jnp.exp(-scaled)
    order_size = point_set.shape[1]
    identity = jnp.eye(order_size, dtype=point_set.dtype)
    diagonal_term = NUGGET * point_mask + (1.0 - point_mask)
    covariance = (
        covariance * (point_mask[:, None] * point_mask[None, :]) + identity * diagonal_term[:, None]
    )
    factor_lower = jnp.linalg.cholesky(covariance)
    unit_tail = identity[:, order_size - own_size :]
    return lax.linalg.triangular_solve(
        factor_lower, unit_tail, left_side=True, lower=True, transpose_a=True
    )


def local(locations, neighbours, observations, noise_prec):
    blocks = locations.shape[0]
    points = locations.shape[2]
    fields = observations.shape[1]
    slot_count = neighbours.shape[1]
    coarse = blocks * lax.axis_size("dev")
    first_local = (lax.axis_index(("grp", "dev")) - 1) * blocks
    slot_live = (neighbours >= 0).astype(jnp.float32)
    near_ids = neighbours[:, :2] - first_local
    near_select = (
        near_ids[:, :, None] == jnp.arange(2 * blocks, dtype=jnp.int32)[None, None, :]
    ).astype(jnp.float32)
    near_select = near_select * slot_live[:, :2, None]
    coarse_select = (
        neighbours[:, 2:, None] == jnp.arange(coarse, dtype=jnp.int32)[None, None, :]
    ).astype(jnp.float32)
    owner_flag = (lax.axis_index("grp") == 0).astype(jnp.float32)

    def fetch(packed):
        before = from_behind(packed, ("grp", "dev"), 1)
        first_rows = from_root(packed, "grp", 0)
        coarse_rows = lax.all_gather(first_rows, "dev", axis=0, tiled=True)
        near_table = jnp.concatenate([before, packed], axis=0)
        near_rows = jnp.einsum("bsn,ncp->bcsp", near_select, near_table, precision=HIGHEST)
        coarse_picked = jnp.einsum("bsn,ncp->bcsp", coarse_select, coarse_rows, precision=HIGHEST)
        slot_rows = jnp.concatenate([near_rows, coarse_picked], axis=2)
        slot_rows = slot_rows.reshape(blocks, packed.shape[1], slot_count * points)
        return jnp.concatenate([slot_rows, packed], axis=2)

    gathered_first = fetch(jnp.concatenate([locations, observations], axis=1))
    point_sets = gathered_first[:, :3]
    point_mask = jnp.concatenate(
        [jnp.repeat(slot_live, points, axis=1), jnp.ones((blocks, points), jnp.float32)], axis=1
    )
    factors = lax.map(
        lambda pair: kernel_factor(pair[0], pair[1], points), (point_sets, point_mask)
    )

    def squared_norm(field):
        return lax.psum(jnp.sum(field * field, axis=(0, 2)), ("grp", "dev"))

    solution = jnp.zeros_like(observations)
    residual = observations
    direction = observations
    norm_now = squared_norm(residual)
    for iteration in range(ITERS):
        if iteration == 0:
            gathered = gathered_first[:, 3:]
        else:
            gathered = fetch(direction)
        weighted = jnp.einsum("bvk,bkp->bvp", gathered, factors, precision=HIGHEST)
        spread = jnp.einsum("bvp,bkp->bvk", weighted, factors, precision=HIGHEST)
        own_part = spread[:, :, slot_count * points :]
        slot_parts = spread[:, :, : slot_count * points].reshape(blocks, fields, slot_count, points)
        near_back = jnp.einsum(
            "bsn,bvsp->nvp", near_select, slot_parts[:, :, :2], precision=HIGHEST
        )
        coarse_back = jnp.einsum(
            "bsn,bvsp->nvp", coarse_select, slot_parts[:, :, 2:], precision=HIGHEST
        )
        returned = from_behind(near_back[:blocks], ("grp", "dev"), -1)
        group_rows = lax.psum_scatter(coarse_back, "dev", scatter_dimension=0, tiled=True)
        owned_rows = lax.psum(group_rows, "grp")
        image = (
            own_part
            + near_back[blocks:]
            + returned
            + owner_flag * owned_rows
            + noise_prec * direction
        )
        product = lax.psum(jnp.sum(direction * image, axis=(0, 2)), ("grp", "dev"))
        alpha = norm_now / product
        solution = solution + alpha[None, :, None] * direction
        residual = residual - alpha[None, :, None] * image
        if iteration + 1 < ITERS:
            norm_next = squared_norm(residual)
            direction = residual + (norm_next / norm_now)[None, :, None] * direction
            norm_now = norm_next
    return (solution, residual)


def solution(mesh):
    placed = (
        P(("grp", "dev"), None, None),
        P(("grp", "dev"), None),
        P(("grp", "dev"), None, None),
        P(("grp", "dev"), None, None),
    )
    return jax.shard_map(
        local,
        mesh=mesh,
        in_specs=placed,
        out_specs=(P(("grp", "dev"), None, None), P(("grp", "dev"), None, None)),
        check_vma=False,
    )
```

profile of v0, /device:TPU:0, one launch (start us, length us, event | category | flops | bytes accessed | tf_op | source)
XLA Modules:
  0.0 744.4 jit_solution(9757663607837852320)
XLA Ops:
  8.6 2.4 collective-permute-start
  11.5 3.2 fusion.4
  14.7 17.0 %psum.57 = f32[1,11,256]{2,0,1:T(1,128)S(1)} all-reduce(f32[1,11,256]{2,0,1:T(1,128)S(1)} %broadcast_select_fusion), channel_id=1, replica_groups=mesh['grp'=4,'dev'=8] {'grp'}, use_global_device_ids=true, to_apply=%region_2.3 | all-reduce | flops 2816 | bytes 22528 | tf_op jit(solution)/shard_map/psum | solution.py:25
  31.7 14.2 %all_gather.6 = f32[8,11,256]{2,1,0:T(8,128)S(1)} all-gather(f32[1,11,256]{2,1,0:T(8,128)S(1)} %copy.58), channel_id=1, replica_groups=mesh['grp'=4,'dev'=8] {'dev'}, dimensions={0}, use_global_device_ids=true | all-gather | bytes 101376 | tf_op jit(solution)/shard_map/all_gather | solution.py:67
  46.8 4.5 multiply_reduce_fusion
  51.4 8.2 %copy.60 = f32[1280,1280]{0,1:T(8,128)} copy(f32[1280,1280]{1,0:T(8,128)} %multiply_reduce_fusion) | data formatting | bytes 13107200 | tf_op jit(solution)/shard_map/while/body/eval_jaxpr/reduce_sum | solution.py:30
  59.5 8.4 %exponential_multiply_fusion = f32[1280,1280]{0,1:T(8,128)} fusion(f32[1280,1280]{0,1:T(8,128)} %copy.60), kind=kLoop, calls=%fused_computation.12 | loop fusion | flops 6553600 | bytes 13107200 | tf_op jit(solution)/shard_map/while/body/eval_jaxpr/mul | solution.py:32
  67.9 8.1 %copy.61 = f32[1280,1280]{1,0:T(8,128)} copy(f32[1280,1280]{0,1:T(8,128)} %exponential_multiply_fusion) | data formatting | bytes 13107200 | tf_op jit(solution)/shard_map/while/body/eval_jaxpr/mul | solution.py:32
  76.1 9.6 %fusion.2 = f32[1280,1280]{1,0:T(8,128)S(1)} fusion(f32[1280,1280]{1,0:T(8,128)} %copy.61, f32[1280]{0:T(1024)S(1)} %subtract_add_fusion, f32[1280]{0:T(1024)S(1)} %pad_reduce_fusion, f32[1280,1280]{0,1:T(8,128)} %copy.60), kind=kLoop, calls=%fused_computation.8 | loop fusion | flops 24576000 | bytes 19671040 | tf_op jit(solution)/shard_map/while/body/eval_jaxpr/jit(cholesky)/div | solution.py:39
  85.6 2.7 copy-done
  88.3 11.7 %cholesky.280 = f32[128,128]{1,0:T(8,128)S(1)} custom-call(f32[128,128]{1,0:T(8,128)S(1)} %cholesky.733), custom_call_target="Cholesky" | custom-call | tf_op jit(solution)/shard_map/while/body/eval_jaxpr/jit(cholesky)/cholesky | solution.py:39
  100.1 9.8 %custom-call.98 = f32[1,128,128]{1,2,0:T(8,128)S(1)} custom-call(f32[1,128,128]{2,1,0:T(8,128)S(1)} %get-tuple-element.68), custom_call_target="InvertDiagBlocksLowerTriangular" | custom-call | tf_op jit(solution)/shard_map/while/body/eval_jaxpr/jit(cholesky)/cholesky | solution.py:39
  109.9 3.1 cholesky.310
  113.0 2.5 constant_dynamic-update-slice_fusion.55
  117.2 11.7 %cholesky.303 = f32[128,128]{1,0:T(8,128)S(1)} custom-call(f32[128,128]{1,0:T(8,128)S(1)} %cholesky.737), custom_call_target="Cholesky" | custom-call | tf_op jit(solution)/shard_map/while/body/eval_jaxpr/jit(cholesky)/cholesky | solution.py:39
  129.6 10.2 %custom-call.99 = f32[1,128,128]{1,2,0:T(8,128)S(1)} custom-call(f32[1,128,128]{2,1,0:T(8,128)S(1)} %get-tuple-element.65), custom_call_target="InvertDiagBlocksLowerTriangular" | custom-call | tf_op jit(solution)/shard_map/while/body/eval_jaxpr/jit(cholesky)/cholesky | solution.py:39
  141.2 2.4 convolution_subtract_fusion.1
  143.6 11.7 %cholesky.328 = f32[128,128]{1,0:T(8,128)S(1)} custom-call(f32[128,128]{1,0:T(8,128)S(1)} %cholesky.742), custom_call_target="Cholesky" | custom-call | tf_op jit(solution)/shard_map/while/body/eval_jaxpr/jit(cholesky)/cholesky | solution.py:39
  156.6 9.8 %custom-call.100 = f32[1,128,128]{1,2,0:T(8,128)S(1)} custom-call(f32[1,128,128]{2,1,0:T(8,128)S(1)} %get-tuple-element.62), custom_call_target="InvertDiagBlocksLowerTriangular" | custom-call | tf_op jit(solution)/shard_map/while/body/eval_jaxpr/jit(cholesky)/cholesky | solution.py:39
  167.8 2.8 fusion.15
  170.6 11.9 %cholesky.599 = f32[128,128]{1,0:T(8,128)S(1)} custom-call(f32[128,128]{1,0:T(8,128)S(1)} %cholesky.747), custom_call_target="Cholesky" | custom-call | tf_op jit(solution)/shard_map/while/body/eval_jaxpr/jit(cholesky)/cholesky | solution.py:39
  183.8 9.8 %custom-call.101 = f32[1,128,128]{1,2,0:T(8,128)S(1)} custom-call(f32[1,128,128]{2,1,0:T(8,128)S(1)} %get-tuple-element.59), custom_call_target="InvertDiagBlocksLowerTriangular" | custom-call | tf_op jit(solution)/shard_map/while/body/eval_jaxpr/jit(cholesky)/cholesky | solution.py:39
  194.9 2.9 fusion.18
  197.9 11.7 %cholesky.618 = f32[128,128]{1,0:T(8,128)S(1)} custom-call(f32[128,128]{1,0:T(8,128)S(1)} %cholesky.752), custom_call_target="Cholesky" | custom-call | tf_op jit(solution)/shard_map/while/body/eval_jaxpr/jit(cholesky)/cholesky | solution.py:39
  210.9 10.0 %custom-call.102 = f32[1,128,128]{1,2,0:T(8,128)S(1)} custom-call(f32[1,128,128]{2,1,0:T(8,128)S(1)} %get-tuple-element.56), custom_call_target="InvertDiagBlocksLowerTriangular" | custom-call | tf_op jit(solution)/shard_map/while/body/eval_jaxpr/jit(cholesky)/cholesky | solution.py:39
  222.1 3.0 fusion.21
  225.2 11.7 %cholesky.638 = f32[128,128]{1,0:T(8,128)S(1)} custom-call(f32[128,128]{1,0:T(8,128)S(1)} %cholesky.757), custom_call_target="Cholesky" | custom-call | tf_op jit(solution)/shard_map/while/body/eval_jaxpr/jit(cholesky)/cholesky | solution.py:39
  238.2 9.8 %custom-call.103 = f32[1,128,128]{1,2,0:T(8,128)S(1)} custom-call(f32[1,128,128]{2,1,0:T(8,128)S(1)} %get-tuple-element.53), custom_call_target="InvertDiagBlocksLowerTriangular" | custom-call | tf_op jit(solution)/shard_map/while/body/eval_jaxpr/jit(cholesky)/cholesky | solution.py:39
  249.1 3.0 fusion.24
  252.1 12.1 %cholesky.658 = f32[128,128]{1,0:T(8,128)S(1)} custom-call(f32[128,128]{1,0:T(8,128)S(1)} %cholesky.762), custom_call_target="Cholesky" | custom-call | tf_op jit(solution)/shard_map/while/body/eval_jaxpr/jit(cholesky)/cholesky | solution.py:39
  265.5 9.8 %custom-call.104 = f32[1,128,128]{1,2,0:T(8,128)S(1)} custom-call(f32[1,128,128]{2,1,0:T(8,128)S(1)} %get-tuple-element.50), custom_call_target="InvertDiagBlocksLowerTriangular" | custom-call | tf_op jit(solution)/shard_map/while/body/eval_jaxpr/jit(cholesky)/cholesky | solution.py:39
  276.4 2.8 fusion.27
  279.2 11.7 %cholesky.678 = f32[128,128]{1,0:T(8,128)S(1)} custom-call(f32[128,128]{1,0:T(8,128)S(1)} %cholesky.767), custom_call_target="Cholesky" | custom-call | tf_op jit(solution)/shard_map/while/body/eval_jaxpr/jit(cholesky)/cholesky | solution.py:39
  292.2 10.0 %custom-call.105 = f32[1,128,128]{1,2,0:T(8,128)S(1)} custom-call(f32[1,128,128]{2,1,0:T(8,128)S(1)} %get-tuple-element.47), custom_call_target="InvertDiagBlocksLowerTriangular" | custom-call | tf_op jit(solution)/shard_map/while/body/eval_jaxpr/jit(cholesky)/cholesky | solution.py:39
  303.1 2.4 convolution_subtract_fusion.11
  305.5 11.7 %cholesky.698 = f32[128,128]{1,0:T(8,128)S(1)} custom-call(f32[128,128]{1,0:T(8,128)S(1)} %cholesky.772), custom_call_target="Cholesky" | custom-call | tf_op jit(solution)/shard_map/while/body/eval_jaxpr/jit(cholesky)/cholesky | solution.py:39
  318.5 9.8 %custom-call.106 = f32[1,128,128]{1,2,0:T(8,128)S(1)} custom-call(f32[1,128,128]{2,1,0:T(8,128)S(1)} %get-tuple-element.44), custom_call_target="InvertDiagBlocksLowerTriangular" | custom-call | tf_op jit(solution)/shard_map/while/body/eval_jaxpr/jit(cholesky)/cholesky | solution.py:39
  329.2 2.1 convolution_subtract_fusion.12
  331.3 11.7 %cholesky.716 = f32[128,128]{1,0:T(8,128)S(1)} custom-call(f32[128,128]{1,0:T(8,128)S(1)} %convolution_subtract_fusion.12), custom_call_target="Cholesky" | custom-call | tf_op jit(solution)/shard_map/while/body/eval_jaxpr/jit(cholesky)/cholesky | solution.py:39
  351.4 6.0 select_select_fusion
  357.4 34.9 %while.1 = (s32[]{:T(128)}, f32[1280,1280]{1,0:T(8,128)}, s32[10,2]{0,1:T(2,128)S(1)}, f32[10,128,128]{2,1,0:T(8,128)}, s32[]{:T(128)}) while((s32[]{:T(128)}, f32[1280,1280]{1,0:T(8,128)}, s32[10,2]{0,1:T(2,128)S(1)}, f32[10,128,128]{2,1,0:T(8,128)}, s32[]{:T(128)}) %tuple.61), condition=%wide.while_cond, body=%wide.while_body.sunk | while | flops 2 | bytes 132705 | solution.py:41
  358.0 2.9 bitcast_dynamic-update-slice_fusion.2
  361.5 2.9 bitcast_dynamic-update-slice_fusion.2
  365.0 2.9 bitcast_dynamic-update-slice_fusion.2
  368.5 2.9 bitcast_dynamic-update-slice_fusion.2
  372.0 2.9 bitcast_dynamic-update-slice_fusion.2
  375.5 2.9 bitcast_dynamic-update-slice_fusion.2
  379.0 2.9 bitcast_dynamic-update-slice_fusion.2
  382.5 2.9 bitcast_dynamic-update-slice_fusion.2
  386.0 2.9 bitcast_dynamic-update-slice_fusion.2
  389.5 2.8 bitcast_dynamic-update-slice_fusion.2
  392.3 99.0 %custom-call.107 = f32[10,128,128]{1,2,0:T(8,128)S(1)} custom-call(f32[10,128,128]{2,1,0:T(8,128)} %get-tuple-element.21), custom_call_target="InvertDiagBlocksLowerTriangular" | custom-call | tf_op jit(solution)/shard_map/while/body/eval_jaxpr/triangular_solve | solution.py:41
  502.8 2.0 convolution_subtract_fusion.10
  505.3 2.1 convolution_subtract_fusion.9
  507.8 2.3 convolution_subtract_fusion.8
  515.0 27.6 %reduce-scatter.3.cloned.1.call-done = f32[1,8,256]{2,1,0:T(8,128)} async-done(((f32[8,8,256]{2,1,0:T(8,128)}), f32[1,8,256]{2,1,0:T(8,128)}) %reduce-scatter.3.cloned.1.call-update) | async-done | bytes 8208 | tf_op jit(solution)/shard_map/reduce_scatter | solution.py:107
  542.7 10.1 %psum.58 = f32[1,8,256]{2,1,0:T(8,128)S(1)} all-reduce(f32[1,8,256]{2,1,0:T(8,128)} %reduce-scatter.3.cloned.1.call-done), channel_id=1, replica_groups=mesh['grp'=4,'dev'=8] {'grp'}, use_global_device_ids=true, to_apply=%region_25.26 | all-reduce | flops 2048 | bytes 16384 | tf_op jit(solution)/shard_map/psum | solution.py:108
  552.9 36.9 %all-reduce.2 = (f32[8]{0:T(128)S(1)}, f32[8]{0:T(128)S(1)}) all-reduce(f32[8]{0:T(128)S(1)} %get-tuple-element.23, f32[8]{0:T(128)S(1)} %get-tuple-element.22), channel_id=1, replica_groups=mesh['grp'=4,'dev'=8] {'grp','dev'}, use_global_device_ids=true, to_apply=%region_1.2 | all-reduce | flops 16 | bytes 128 | tf_op jit(solution)/shard_map/psum | solution.py:85
  590.0 41.7 %psum.60 = f32[8]{0:T(128)S(1)} all-reduce(f32[8]{0:T(128)S(1)} %multiply_reduce_fusion.2), channel_id=1, replica_groups=mesh['grp'=4,'dev'=8] {'grp','dev'}, use_global_device_ids=true, to_apply=%region_29.30 | all-reduce | flops 8 | bytes 64 | tf_op jit(solution)/shard_map/psum | solution.py:85
  633.1 11.4 %psum.61 = f32[1,8,256]{2,1,0:T(8,128)S(1)} all-reduce(f32[1,8,256]{2,1,0:T(8,128)S(1)} %get-tuple-element.36), channel_id=1, replica_groups=mesh['grp'=4,'dev'=8] {'grp'}, use_global_device_ids=true, to_apply=%region_30.31 | all-reduce | flops 2048 | bytes 16384 | tf_op jit(solution)/shard_map/psum | solution.py:25
  644.5 14.0 %all_gather.7 = f32[8,8,256]{2,1,0:T(8,128)S(1)} all-gather(f32[1,8,256]{2,1,0:T(8,128)S(1)} %psum.61), channel_id=1, replica_groups=mesh['grp'=4,'dev'=8] {'dev'}, dimensions={0}, use_global_device_ids=true | all-gather | bytes 73728 | tf_op jit(solution)/shard_map/all_gather | solution.py:67
  663.5 25.9 %reduce-scatter.5.cloned.1.call-done = f32[1,8,256]{2,1,0:T(8,128)} async-done(((f32[8,8,256]{2,1,0:T(8,128)}), f32[1,8,256]{2,1,0:T(8,128)}) %reduce-scatter.5.cloned.1.call-update) | async-done | bytes 8208 | tf_op jit(solution)/shard_map/reduce_scatter | solution.py:107
  689.3 10.1 %psum.62 = f32[1,8,256]{2,1,0:T(8,128)S(1)} all-reduce(f32[1,8,256]{2,1,0:T(8,128)} %reduce-scatter.5.cloned.1.call-done), channel_id=1, replica_groups=mesh['grp'=4,'dev'=8] {'grp'}, use_global_device_ids=true, to_apply=%region_32.33 | all-reduce | flops 2048 | bytes 16384 | tf_op jit(solution)/shard_map/psum | solution.py:108
  699.6 36.9 %psum.63 = f32[8]{0:T(128)S(1)} all-reduce(f32[8]{0:T(128)S(1)} %get-tuple-element.34), channel_id=1, replica_groups=mesh['grp'=4,'dev'=8] {'grp','dev'}, use_global_device_ids=true, to_apply=%region_34.35 | all-reduce | flops 8 | bytes 64 | tf_op jit(solution)/shard_map/psum | solution.py:116
  (183 shorter events, 56.0 us)
Async XLA Ops:
  7.2 7.5 %copy-start.3 = (s32[1,4]{1,0:T(1,128)S(1)}, s32[1,4]{1,0:T(1,128)}, u32[]{:S(2)}) copy-start(s32[1,4]{1,0:T(1,128)} %param.5) | copy-start | bytes 52
  7.2 535.5 %reduce-scatter.3.cloned.1.call-start = ((), (), s32[]{:S(2)}) async-start(), calls=%async_computation.2 | async-start | bytes 73728 | tf_op jit(solution)/shard_map/reduce_scatter | solution.py:107
  8.6 37.7 %collective-permute-start = (f32[1,11,256]{2,0,1:T(1,128)S(1)}, f32[1,11,256]{2,0,1:T(1,128)S(1)}, u32[]{:S(2)}, u32[]{:S(2)}) collective-permute-start(f32[1,11,256]{2,0,1:T(1,128)S(1)} %constant_dynamic-update-slice_fusion), channel_id=1, source_target_pairs={{0,1},{1,2},{2,3},{3,4},{4,5},{5,6},{6,7},{7,8},{8,9},{9,10},{10,1... | collective-permute-start | bytes 33800 | tf_op jit(solution)/shard_map/ppermute | solution.py:20
  85.6 2.7 copy-start
  505.2 47.6 %copy-start.1 = (f32[1,8,256]{2,1,0:T(8,128)S(1)}, f32[1,8,256]{2,1,0:T(8,128)}, u32[]{:S(2)}) copy-start(f32[1,8,256]{2,1,0:T(8,128)} %param.6) | copy-start | bytes 24580
  505.2 47.6 %copy-start.2 = (f32[1,8,256]{2,1,0:T(8,128)S(1)}, f32[1,8,256]{2,1,0:T(8,128)}, u32[]{:S(2)}) copy-start(f32[1,8,256]{2,1,0:T(8,128)} %param.7) | copy-start | bytes 24580
  513.3 176.0 %reduce-scatter.5.cloned.1.call-start = ((), (), s32[]{:S(2)}) async-start(), calls=%async_computation.3 | async-start | bytes 73728 | tf_op jit(solution)/shard_map/reduce_scatter | solution.py:107
  513.7 39.0 %collective-permute-start.1 = (f32[1,8,256]{2,1,0:T(8,128)S(1)}, f32[1,8,256]{2,1,0:T(8,128)S(1)}, u32[]{:S(2)}, u32[]{:S(2)}) collective-permute-start(f32[1,8,256]{2,1,0:T(8,128)S(1)} %copy.84), channel_id=1, source_target_pairs={{1,0},{2,1},{3,2},{4,3},{5,4},{6,5},{7,6},{8,7},{9,8},{10,9},{11,1... | collective-permute-start | bytes 24584 | tf_op jit(solution)/shard_map/ppermute | solution.py:20
  631.8 26.9 %collective-permute-start.2 = (f32[1,8,256]{2,1,0:T(8,128)S(1)}, f32[1,8,256]{2,1,0:T(8,128)S(1)}, u32[]{:S(2)}, u32[]{:S(2)}) collective-permute-start(f32[1,8,256]{2,1,0:T(8,128)S(1)} %get-tuple-element.37), channel_id=1, source_target_pairs={{0,1},{1,2},{2,3},{3,4},{4,5},{5,6},{6,7},{7,8},{8,9},{9,10},{10,1... | collective-permute-start | bytes 24584 | tf_op jit(solution)/shard_map/ppermute | solution.py:20
  662.2 37.3 %collective-permute-start.3 = (f32[1,8,256]{2,1,0:T(8,128)S(1)}, f32[1,8,256]{2,1,0:T(8,128)S(1)}, u32[]{:S(2)}, u32[]{:S(2)}) collective-permute-start(f32[1,8,256]{2,1,0:T(8,128)S(1)} %copy.88), channel_id=1, source_target_pairs={{1,0},{2,1},{3,2},{4,3},{5,4},{6,5},{7,6},{8,7},{9,8},{10,9},{11,1... | collective-permute-start | bytes 24584 | tf_op jit(solution)/shard_map/ppermute | solution.py:20
Sparse Core Ops, SparseCore 0:
  513.5 29.1 reduce-scatter.2
  661.9 27.3 reduce-scatter.4
where the time goes:
time: 755 us; the launch traced here: 744 us
  other arithmetic  351 us (46%)
  blocking collectives  192 us (25%)
  local copies, waits for them, and re-layouts  60.5 us (8%)
  matrix products  59 us (8%)
  waiting for transfers between devices  53.5 us (7%)
  between operations  21.9 us (3%)
    another operation x38, other arithmetic, kernel_factor(): factor_lower = jnp.linalg.cholesky(covariance)  218 us
    another operation x3, other arithmetic, kernel_factor(): lax.linalg.triangular_solve(factor_lower, unit_tail, left_side=True, lowe...  105 us
    psum x2, blocking collectives, squared_norm(): return lax.psum(jnp.sum(field * field, axis=(0, 2)), ('grp', 'dev'))  78.6 us
    reduce_scatter x2, waiting for transfers between devices, local(): lax.psum_scatter(coarse_back, 'dev', scatter_dimension=0, tiled=True)  53.5 us
    psum x1, blocking collectives, local(): product = lax.psum(jnp.sum(direction * image, axis=(0, 2)), ('grp', 'dev'))  36.9 us
    another operation x18, matrix products, kernel_factor(): factor_lower = jnp.linalg.cholesky(covariance)  34.9 us
    another operation x30, local copies, waits for them, and re-layouts  34.9 us
    psum x2, blocking collectives, from_root(): return lax.psum(kept, axis)  28.4 us
  transfers between devices with their start and end apart: 6, of which 2 were waited for; matrix products, arithmetic and copies ran while one was open for 1% of the time, Pallas kernels for 0%

commit v1 on v0

v1 whole, which is shorter than its diff:
```python
import functools
import math

import jax
import jax.numpy as jnp
from jax import lax
from jax.experimental import pallas as pl
from jax.experimental.pallas import tpu as pltpu
from jax.sharding import PartitionSpec as P

SCALE_LENGTH = 0.5
NUGGET = 0.5
SQRT_THREE = math.sqrt(3.0)
LANES = 128
HIGHEST = lax.Precision.HIGHEST
F32 = jnp.float32
NN = (((1,), (0,)), ((), ()))
NT = (((1,), (1,)), ((), ()))
AXES = ("grp", "dev")
VMEM_LIMIT = 48 * 1024 * 1024


def split(value):
    high = value.astype(jnp.bfloat16)
    return high, (value - high.astype(F32)).astype(jnp.bfloat16)


def dot(left, right, dims=NN, precision=None):
    return lax.dot_general(left, right, dims, precision=precision, preferred_element_type=F32)


def dot_three(left, right, dims=NN):
    return dot(left[0], right[0], dims) + (dot(left[0], right[1], dims) + dot(left[1], right[0], dims))


def inverse(matrix, beside=()):
    order = matrix.shape[0]
    rows = lax.broadcasted_iota(jnp.int32, (order, order), 0)
    columns = lax.broadcasted_iota(jnp.int32, (order, order), 1)
    identity = (rows == columns).astype(F32)
    start = 2.0 / (2.0 * NUGGET + order)
    least = start * NUGGET
    ahead = start * matrix
    guess = None
    beside = list(beside)
    while True:
        reached = least * (2.0 - least)
        centre = 2.0 / (1.0 + reached)
        least = centre * reached
        ahead_parts = split(ahead)
        if guess is None:
            guess = (centre * start) * (2.0 * identity - ahead)
        else:
            guess = centre * (2.0 * guess - dot_three(split(guess), ahead_parts))
        if beside:
            beside.pop(0)()
        if 1.0 - least < 1e-3:
            break
        ahead = centre * (2.0 * ahead - dot_three(ahead_parts, ahead_parts))
    for work in beside:
        work()
    error = identity - dot(matrix, guess, precision=HIGHEST)
    return guess + dot_three(split(guess), split(error))


def table_fields(entry, fields):
    return jnp.concatenate([entry[at : at + fields] for at in range(0, entry.shape[0] - 8, fields)], axis=1)


def table_places(entry, fields, pieces):
    first = fields * pieces
    return jnp.concatenate([entry[first + 4 * at : first + 4 * at + 4] for at in range(pieces)], axis=1)


def slot_list(slots):
    return [slot for slot in range(slots) if slot != 1]


def factor_kernel(sizes, nbr, me, table, noise, part, near_own, near_prev, back_out, last_out, blocks):
    fields, points, coarse, slots = sizes
    pieces = points // LANES
    used = slot_list(slots)
    count = len(used) + 1
    ids = [nbr[0, slot] for slot in used] + [me[0]]
    entries = [table[jnp.maximum(index, 0)] for index in ids]
    live = [(index >= 0).astype(F32) for index in ids]
    values = [table_fields(entry, fields) * alive for entry, alive in zip(entries, live)]
    places = [table_places(entry, fields, pieces) * (SQRT_THREE / SCALE_LENGTH) for entry in entries]
    turned = [jnp.transpose(jnp.concatenate([place, place], axis=0)) for place in places]
    rows_at_once = 64

    def build(i, j):
        across = places[j]
        alive = live[i] * live[j]
        for first in range(0, points, rows_at_once):
            down = turned[i][first : first + rows_at_once]
            total = None
            for k in range(3):
                offset = down[:, k : k + 1] - across[k : k + 1, :]
                total = offset * offset if total is None else total + offset * offset
            scaled = jnp.sqrt(total)
            value = (1.0 + scaled) * jnp.exp(-scaled) * alive
            if i == j:
                row = lax.broadcasted_iota(jnp.int32, value.shape, 0) + first
                column = lax.broadcasted_iota(jnp.int32, value.shape, 1)
                value = value + jnp.where(row == column, NUGGET * live[i] + (1.0 - live[i]), 0.0)
            blocks[i, j, first : first + rows_at_once, :] = value

    pairs = [(i, j) for i in range(count) for j in range(i + 1)]
    build(0, 0)
    later = [functools.partial(build, i, j) for i, j in pairs if (i, j) != (0, 0)]
    lower = {}
    last = None
    for k in range(count):
        middle = inverse(blocks[k, k], later if k == 0 else ())
        if k == count - 1:
            last = middle
            break
        side = {i: blocks[i, k] for i in range(k + 1, count)}
        for i in range(k + 1, count):
            lower[i, k] = dot(side[i], middle, precision=HIGHEST)
        side_parts = {i: split(side[i]) for i in side}
        for i in range(k + 1, count):
            left = split(lower[i, k])
            for j in range(k + 1, i + 1):
                blocks[i, j] = blocks[i, j] - dot_three(left, side_parts[j], NT)
    own = count - 1
    back = {}
    for k in range(own - 1, -1, -1):
        total = lower[own, k]
        for j in range(k + 1, own):
            total = total - dot_three(split(back[j]), split(lower[j, k]))
        back[k] = total
    for k in range(own):
        back_out[:, k * points : (k + 1) * points] = back[k]
    last_out[...] = last

    middle, spread, slot_parts = apply_block(values, back_out, last_out[...], points)
    own_part = spread + noise[0] * values[own]
    near_own[...] = own_part
    near_prev[...] = slot_parts[0]
    part[...] = jnp.zeros_like(part)
    part[coarse] = middle * spread + noise[0] * values[own] * values[own]
    add_coarse(part, coarse, ids, slot_parts, own_part)


def apply_block(values, back, last, points):
    own = len(values) - 1
    middle = values[own]
    for k in range(own):
        middle = middle - dot_three(split(values[k]), split(back[:, k * points : (k + 1) * points]), NT)
    spread = dot_three(split(middle), split(last))
    spread_parts = split(spread)
    slot_parts = [-dot_three(spread_parts, split(back[:, k * points : (k + 1) * points])) for k in range(own)]
    return middle, spread, slot_parts


def add_coarse(part, coarse, ids, slot_parts, own_part):
    for index, value in zip(ids, slot_parts + [own_part]):

        @pl.when((index >= 0) & (index < coarse))
        def _(index=index, value=value):
            part[index] = part[index] + value


def step_kernel(
    sizes, nbr, me, table, noise, summed, near_image, prev_image, back, last, sends, image_out, residual_out, ratio_out
):
    fields, points, coarse, slots = sizes
    pieces = points // LANES
    devices = table.shape[0]
    used = slot_list(slots)
    ids = [nbr[0, slot] for slot in used] + [me[0]]
    square = jnp.zeros((fields, points), F32)
    for block in range(devices):
        value = table_fields(table[block], fields)
        square = square + value * value
    norm_now = jnp.sum(square, axis=1, keepdims=True)
    product = jnp.sum(summed[coarse], axis=1, keepdims=True)
    alpha = norm_now / product
    observed, images = [], []
    for at, index in enumerate(ids):
        alive = (index >= 0).astype(F32)
        observed.append(table_fields(table[jnp.maximum(index, 0)], fields) * alive)
        image = summed[jnp.clip(index, 0, coarse - 1)]
        if at == len(ids) - 1:
            image = jnp.where(index < coarse, image, near_image[...])
        elif at == 0:
            image = jnp.where(index < coarse, image, prev_image[...])
        images.append(image * alive)
    values = [value - alpha * image for value, image in zip(observed, images)]
    middle, spread, slot_parts = apply_block(values, back, last[...], points)
    residual, image = values[-1], images[-1]
    own_part = spread + noise[0] * residual
    inner = jnp.sum(middle * spread + noise[0] * residual * residual, axis=1, keepdims=True)
    cross = jnp.sum(residual * image, axis=1, keepdims=True)
    square = jnp.sum(residual * residual, axis=1, keepdims=True)
    lane = lax.broadcasted_iota(jnp.int32, (fields, LANES), 1)
    scalars = jnp.where(lane == 0, inner, jnp.where(lane == 1, cross, jnp.where(lane == 2, square, 0.0)))
    clear = jnp.zeros((fields * pieces, LANES), F32)
    for block in range(devices):
        sends[block] = jnp.concatenate([clear, scalars], axis=0)
    for index, value in zip(ids, slot_parts + [own_part]):

        @pl.when(index >= 0)
        def _(index=index, value=value):
            for piece in range(pieces):
                sends[index, piece * fields : (piece + 1) * fields, :] = value[:, piece * LANES : (piece + 1) * LANES]

    image_out[...] = image
    residual_out[...] = residual
    ratio_out[...] = jnp.where(lane == 0, alpha, jnp.where(lane == 1, norm_now, product))


def finish_kernel(sizes, received, image, residual, ratios, observed, solution_out, residual_out):
    fields, points, coarse, slots = sizes
    pieces = points // LANES
    total = received[0]
    for block in range(1, received.shape[0]):
        total = total + received[block]
    spread = jnp.concatenate([total[at * fields : (at + 1) * fields] for at in range(pieces)], axis=1)
    scalars = total[pieces * fields :]
    alpha, norm_first, product_first = ratios[:, 0:1], ratios[:, 1:2], ratios[:, 2:3]
    inner, cross, norm_now = scalars[:, 0:1], scalars[:, 1:2], scalars[:, 2:3]
    beta = norm_now / norm_first
    product = inner + beta * (2.0 * cross + beta * product_first)
    step = norm_now / product
    direction = residual[...] + beta * observed[0]
    solution_out[0] = alpha * observed[0] + step * direction
    residual_out[0] = residual[...] - step * (spread + beta * image[...])


def call(kernel, sizes, outs, in_spaces, scratch=(), flops=0):
    return pl.pallas_call(
        functools.partial(kernel, sizes),
        out_shape=[jax.ShapeDtypeStruct(shape, F32) for shape in outs],
        in_specs=[pl.BlockSpec(memory_space=space) for space in in_spaces],
        out_specs=[pl.BlockSpec(memory_space=pltpu.VMEM)] * len(outs),
        scratch_shapes=list(scratch),
        compiler_params=pltpu.CompilerParams(vmem_limit_bytes=VMEM_LIMIT),
    )


def summed_over(value, axis):
    size = lax.axis_size(axis)
    if size & (size - 1):
        return lax.psum(value, axis)
    reach = 1
    while reach < size:
        value = value + lax.ppermute(value, axis, [(at, at ^ reach) for at in range(size)])
        reach *= 2
    return value


def local(locations, neighbours, observations, noise_prec):
    blocks, _, points = locations.shape
    fields = observations.shape[1]
    slots = neighbours.shape[1]
    assert blocks == 1
    pieces = points // LANES
    coarse = lax.axis_size("dev")
    devices = coarse * lax.axis_size("grp")
    sizes = (fields, points, coarse, slots)
    depth = (len(slot_list(slots))) * points
    me = lax.axis_index(AXES).astype(jnp.int32).reshape(1)
    smem, vmem = pltpu.SMEM, pltpu.VMEM

    def cut(rows):
        return rows.reshape(rows.shape[0], pieces, LANES).transpose(1, 0, 2).reshape(-1, LANES)

    packed = jnp.concatenate([cut(observations[0]), cut(jnp.pad(locations[0], ((0, 1), (0, 0))))], axis=0)
    table = lax.all_to_all(jnp.broadcast_to(packed, (devices,) + packed.shape), AXES, 0, 0, tiled=True)
    part, near_own, near_prev, back, last = call(
        factor_kernel,
        sizes,
        [(coarse + 1, fields, points), (fields, points), (fields, points), (points, depth), (points, points)],
        [smem, smem, vmem, vmem],
        [pltpu.VMEM((slots, slots, points, points), F32)],
    )(neighbours, me, table, noise_prec)
    near_image = near_own + lax.ppermute(near_prev, AXES, [(at, at - 1) for at in range(1, devices)])
    prev_image = lax.ppermute(near_image, AXES, [(at, at + 1) for at in range(devices - 1)])
    summed = summed_over(summed_over(part, "dev"), "grp")
    sends, image, residual, ratios = call(
        step_kernel,
        sizes,
        [(devices, 3 * fields, LANES), (fields, points), (fields, points), (fields, LANES)],
        [smem, smem] + [vmem] * 7,
    )(neighbours, me, table, noise_prec, summed, near_image, prev_image, back, last)
    received = lax.all_to_all(sends, AXES, 0, 0, tiled=True)
    return tuple(
        call(finish_kernel, sizes, [observations.shape] * 2, [vmem] * 5)(
            received, image, residual, ratios, observations
        )
    )


def solution(mesh):
    placed = (
        P(AXES, None, None),
        P(AXES, None),
        P(AXES, None, None),
        P(AXES, None, None),
    )
    return jax.shard_map(
        local,
        mesh=mesh,
        in_specs=placed,
        out_specs=(P(AXES, None, None), P(AXES, None, None)),
        check_vma=False,
    )
```

time: 755 us -> 89.5 us (0.12); the launches traced: 744 us -> 89.1 us
  other arithmetic: 351 us -> 0.06 us
  blocking collectives: 192 us -> 20.7 us
  matrix products: 59 us -> 0 us
  local copies, waits for them, and re-layouts: 60.5 us -> 2.19 us
  waiting for transfers between devices: 53.5 us -> 30.9 us
  Pallas kernels: 0 us -> 21.9 us
  between operations: 21.9 us -> 0.73 us
    another operation x41 -> x0, other arithmetic: 323 us -> none  [the longest x38 218 us: kernel_factor(): factor_lower = jnp.linalg.cholesky(covariance)]
    psum x7 -> x0, blocking collectives: 164 us -> none  [the longest x2 78.6 us: squared_norm(): return lax.psum(jnp.sum(field * field, axis=(0, 2)), ('grp', 'dev'))]
    reduce_scatter x2 -> x0, waiting for transfers between devices: 53.5 us -> none  [local(): lax.psum_scatter(coarse_back, 'dev', scatter_dimension=0, tiled=True)]
    another operation x37 -> x0, matrix products: 53.2 us -> none  [the longest x18 34.9 us: kernel_factor(): factor_lower = jnp.linalg.cholesky(covariance)]
    another operation x47 -> x0, local copies, waits for them, and re-layouts: 38.1 us -> none
    all_gather x2 -> x0, blocking collectives: 28.2 us -> none  [fetch(): coarse_rows = lax.all_gather(first_rows, 'dev', axis=0, tiled=True)]
    pallas_call x0 -> x3, Pallas kernels: none -> 21.9 us  [the longest x1 19.2 us: local(): call(factor_kernel, sizes, [(coarse + 1, fields, points), (fields, points...]
    all_to_all x0 -> x1, blocking collectives: none -> 20.7 us  [local(): received = lax.all_to_all(sends, AXES, 0, 0, tiled=True)]
  transfers between devices with their start and end apart: 6 -> 8, of which waited for: 2 -> 7; matrix products, arithmetic and copies ran while one was open for 1% -> 0% of each run, Pallas kernels for 0% -> 0%
where the time goes in v1:
time: 89.5 us; the launch traced here: 89.1 us
  waiting for transfers between devices  30.9 us (35%)
  Pallas kernels  21.9 us (24%)
  blocking collectives  20.7 us (23%)
  starting transfers between devices  12.8 us (14%)
  local copies, waits for them, and re-layouts  2.19 us (2%)
    all_to_all x1, blocking collectives, local(): received = lax.all_to_all(sends, AXES, 0, 0, tiled=True)  20.7 us
    pallas_call x1, Pallas kernels, local(): call(factor_kernel, sizes, [(coarse + 1, fields, points), (fields, points...  19.2 us
    ppermute x5, waiting for transfers between devices, summed_over(): lax.ppermute(value, axis, [(at, at ^ reach) for at in range(size)])  14.8 us
    all_to_all x1, waiting for transfers between devices, local(): lax.all_to_all(jnp.broadcast_to(packed, (devices,) + packed.shape), AXES,...  13.5 us
    all_to_all x1, starting transfers between devices, local(): lax.all_to_all(jnp.broadcast_to(packed, (devices,) + packed.shape), AXES,...  7.3 us
    ppermute x1, starting transfers between devices, local(): lax.ppermute(near_image, AXES, [(at, at + 1) for at in range(devices - 1)])  2.3 us
    ppermute x5, starting transfers between devices, summed_over(): lax.ppermute(value, axis, [(at, at ^ reach) for at in range(size)])  1.9 us
  transfers between devices with their start and end apart: 8, of which 7 were waited for; matrix products, arithmetic and copies ran while one was open for 0% of the time, Pallas kernels for 0%

profile of v1, /device:TPU:0, one launch (start us, length us, event | category | flops | bytes accessed | tf_op | source)
XLA Modules:
  0.0 89.1 jit_solution(7184625527646625596)
XLA Ops:
  0.6 0.7 copy.9
  1.3 0.0 copy-start.1
  1.4 0.7 copy-done.1
  2.0 0.8 broadcast_in_dim.3
  2.8 7.3 %all-to-all-start = ((f32[32,24,128]{2,1,0:T(8,128)}), f32[32,24,128]{2,1,0:T(8,128)S(1)}, u32[]{:S(2)}, u32[]{:S(2)}) async-start(f32[32,24,128]{2,1,0:T(8,128)} %broadcast_in_dim.3), calls=%async_computation | async-start | bytes 786432 | tf_op jit(solution)/shard_map/all_to_all | solution.py:272
  10.1 0.0 copy-start
  10.1 0.0 copy-start.2
  10.1 13.5 %all-to-all-done.table = f32[32,24,128]{2,1,0:T(8,128)S(1)} async-done(((f32[32,24,128]{2,1,0:T(8,128)}), f32[32,24,128]{2,1,0:T(8,128)S(1)}, u32[]{:S(2)}, u32[]{:S(2)}) %all-to-all-start) | async-done | bytes 393248 | tf_op jit(solution)/shard_map/all_to_all | solution.py:272
  23.7 0.0 copy-done
  23.7 0.0 copy-done.2
  23.7 19.2 %shard_map.59 = (f32[9,8,256]{2,1,0:T(8,128)S(1)}, f32[8,256]{1,0:T(8,128)S(1)}, f32[8,256]{1,0:T(8,128)S(1)}, f32[256,768]{1,0:T(8,128)S(1)}, f32[256,256]{1,0:T(8,128)S(1)}) custom-call(s32[1,4]{1,0:T(1,128)S(1)} %copy-done.2, s32[1]{0:T(128)} %bitcast.me, f32[32,24,128]{2,1,0:T(8,128)S(1)} %all-to-all-done.table, f32[1,8,256]{2,1,0:T(8,128)S(1)} %copy-done), custom_call_target="tpu_custom_call" | custom-call | tf_op jit(solution)/shard_map/pallas_call | solution.py:273
  42.9 0.1 collective-permute-start
  43.0 1.2 %collective-permute-done = f32[9,8,256]{2,1,0:T(8,128)S(1)} collective-permute-done((f32[9,8,256]{2,1,0:T(8,128)S(1)}, f32[9,8,256]{2,1,0:T(8,128)S(1)}, u32[]{:S(2)}, u32[]{:S(2)}) %collective-permute-start) | collective-permute-done | bytes 73760 | tf_op jit(solution)/shard_map/ppermute | solution.py:250
  44.2 0.1 collective-permute-start.1
  44.3 4.3 %collective-permute-done.1 = f32[9,8,256]{2,1,0:T(8,128)S(1)} collective-permute-done((f32[9,8,256]{2,1,0:T(8,128)S(1)}, f32[9,8,256]{2,1,0:T(8,128)S(1)}, u32[]{:S(2)}, u32[]{:S(2)}) %collective-permute-start.1) | collective-permute-done | bytes 73760 | tf_op jit(solution)/shard_map/ppermute | solution.py:250
  48.6 0.1 collective-permute-start.2
  48.7 5.7 %collective-permute-done.2 = f32[9,8,256]{2,1,0:T(8,128)S(1)} collective-permute-done((f32[9,8,256]{2,1,0:T(8,128)S(1)}, f32[9,8,256]{2,1,0:T(8,128)S(1)}, u32[]{:S(2)}, u32[]{:S(2)}) %collective-permute-start.2) | collective-permute-done | bytes 73760 | tf_op jit(solution)/shard_map/ppermute | solution.py:250
  54.5 0.8 collective-permute-start.3
  55.3 3.6 %collective-permute-done.3 = f32[9,8,256]{2,1,0:T(8,128)S(1)} collective-permute-done((f32[9,8,256]{2,1,0:T(8,128)S(1)}, f32[9,8,256]{2,1,0:T(8,128)S(1)}, u32[]{:S(2)}, u32[]{:S(2)}) %collective-permute-start.3) | collective-permute-done | bytes 73760 | tf_op jit(solution)/shard_map/ppermute | solution.py:250
  58.9 0.8 collective-permute-start.4
  59.7 1.3 %collective-permute-start.5 = (f32[8,256]{1,0:T(8,128)S(1)}, f32[8,256]{1,0:T(8,128)S(1)}, u32[]{:S(2)}, u32[]{:S(2)}) collective-permute-start(f32[8,256]{1,0:T(8,128)S(1)} %get-tuple-element.13), channel_id=1, source_target_pairs={{1,0},{2,1},{3,2},{4,3},{5,4},{6,5},{7,6},{8,7},{9,8},{10,9},{11,1... | collective-permute-start | bytes 24584 | tf_op jit(solution)/shard_map/ppermute | solution.py:280
  61.0 1.8 %collective-permute-done.5 = f32[8,256]{1,0:T(8,128)S(1)} collective-permute-done((f32[8,256]{1,0:T(8,128)S(1)}, f32[8,256]{1,0:T(8,128)S(1)}, u32[]{:S(2)}, u32[]{:S(2)}) %collective-permute-start.5) | collective-permute-done | bytes 8224 | tf_op jit(solution)/shard_map/ppermute | solution.py:280
  62.7 2.3 %collective-permute-start.6 = (f32[8,256]{1,0:T(8,128)S(1)}, f32[8,256]{1,0:T(8,128)S(1)}, u32[]{:S(2)}, u32[]{:S(2)}) collective-permute-start(f32[8,256]{1,0:T(8,128)S(1)} %add.29.near_image), channel_id=1, source_target_pairs={{0,1},{1,2},{2,3},{3,4},{4,5},{5,6},{6,7},{7,8},{8,9},{9,10},{10,1... | collective-permute-start | bytes 24584 | tf_op jit(solution)/shard_map/ppermute | solution.py:281
  65.1 0.0 collective-permute-done.4
  65.1 0.8 collective-permute-done.6.prev_image
  65.9 1.6 %shard_map.60 = (f32[32,24,128]{2,1,0:T(8,128)S(1)}, f32[8,256]{1,0:T(8,128)S(1)}, f32[8,256]{1,0:T(8,128)S(1)}, f32[8,128]{1,0:T(8,128)S(1)}) custom-call(s32[1,4]{1,0:T(1,128)S(1)} %copy-done.2, s32[1]{0:T(128)} %bitcast.me, f32[32,24,128]{2,1,0:T(8,128)S(1)} %all-to-all-done.table, f32[1,8,256]{2,1,0:T(8,128)S(1)} %copy-done, ...), custom_call_target="tpu_custom_call" | custom-call | tf_op jit(solution)/shard_map/pallas_call | solution.py:283
  67.4 20.7 %all_to_all.10.received = f32[32,24,128]{2,1,0:T(8,128)S(1)} all-to-all(f32[32,24,128]{2,1,0:T(8,128)S(1)} %get-tuple-element.16), channel_id=1, replica_groups=mesh['grp'=4,'dev'=8] {'grp','dev'}, dimensions={0} | all-to-all | bytes 786432 | tf_op jit(solution)/shard_map/all_to_all | solution.py:289
  88.1 1.0 %shard_map.61 = (f32[1,8,256]{2,1,0:T(8,128)}, f32[1,8,256]{2,1,0:T(8,128)}) custom-call(f32[32,24,128]{2,1,0:T(8,128)S(1)} %all_to_all.10.received, f32[8,256]{1,0:T(8,128)S(1)} %get-tuple-element.17.image, f32[8,256]{1,0:T(8,128)S(1)} %get-tuple-element.18.residual, f32[8,128]{1,0:T(8,128)S(1)} %get-tuple-element.19.ratios, f32[1,8,256]{2,1,0:T(8,128)S(1)} %copy-done.1), custom_call_target="tpu_custom_call" | custom-call | tf_op jit(solution)/shard_map/pallas_call | solution.py:291
  (10 shorter events, 0.1 us)
Async XLA Ops:
  1.3 0.7 copy-start.1
  2.8 20.8 %all-to-all-start = ((f32[32,24,128]{2,1,0:T(8,128)}), f32[32,24,128]{2,1,0:T(8,128)S(1)}, u32[]{:S(2)}, u32[]{:S(2)}) async-start(f32[32,24,128]{2,1,0:T(8,128)} %broadcast_in_dim.3), calls=%async_computation | async-start | bytes 786432 | tf_op jit(solution)/shard_map/all_to_all | solution.py:272
  10.1 13.5 %copy-start = (f32[1,8,256]{2,1,0:T(8,128)S(1)}, f32[1,8,256]{2,1,0:T(8,128)}, u32[]{:S(2)}) copy-start(f32[1,8,256]{2,1,0:T(8,128)} %noise.3) | copy-start | bytes 24580
  10.1 13.5 %copy-start.2 = (s32[1,4]{1,0:T(1,128)S(1)}, s32[1,4]{1,0:T(1,128)}, u32[]{:S(2)}) copy-start(s32[1,4]{1,0:T(1,128)} %nbr.3) | copy-start | bytes 52
  42.9 1.3 %collective-permute-start = (f32[9,8,256]{2,1,0:T(8,128)S(1)}, f32[9,8,256]{2,1,0:T(8,128)S(1)}, u32[]{:S(2)}, u32[]{:S(2)}) collective-permute-start(f32[9,8,256]{2,1,0:T(8,128)S(1)} %get-tuple-element.11), channel_id=1, source_target_pairs={{0,1},{1,0},{2,3},{3,2},{4,5},{5,4},{6,7},{7,6},{8,9},{9,8},{10,11... | collective-permute-start | bytes 221192 | tf_op jit(solution)/shard_map/ppermute | solution.py:250
  44.2 4.4 %collective-permute-start.1 = (f32[9,8,256]{2,1,0:T(8,128)S(1)}, f32[9,8,256]{2,1,0:T(8,128)S(1)}, u32[]{:S(2)}, u32[]{:S(2)}) collective-permute-start(f32[9,8,256]{2,1,0:T(8,128)S(1)} %add.24), channel_id=1, source_target_pairs={{0,2},{1,3},{2,0},{3,1},{4,6},{5,7},{6,4},{7,5},{8,10},{9,11},{10,... | collective-permute-start | bytes 221192 | tf_op jit(solution)/shard_map/ppermute | solution.py:250
  48.6 5.8 %collective-permute-start.2 = (f32[9,8,256]{2,1,0:T(8,128)S(1)}, f32[9,8,256]{2,1,0:T(8,128)S(1)}, u32[]{:S(2)}, u32[]{:S(2)}) collective-permute-start(f32[9,8,256]{2,1,0:T(8,128)S(1)} %add.25), channel_id=1, source_target_pairs={{0,4},{1,5},{2,6},{3,7},{4,0},{5,1},{6,2},{7,3},{8,12},{9,13},{10,... | collective-permute-start | bytes 221192 | tf_op jit(solution)/shard_map/ppermute | solution.py:250
  54.5 4.4 %collective-permute-start.3 = (f32[9,8,256]{2,1,0:T(8,128)S(1)}, f32[9,8,256]{2,1,0:T(8,128)S(1)}, u32[]{:S(2)}, u32[]{:S(2)}) collective-permute-start(f32[9,8,256]{2,1,0:T(8,128)S(1)} %add.26), channel_id=1, source_target_pairs={{0,8},{8,0},{16,24},{24,16},{1,9},{9,1},{17,25},{25,17},{2,10},{10... | collective-permute-start | bytes 221192 | tf_op jit(solution)/shard_map/ppermute | solution.py:250
  58.9 6.2 %collective-permute-start.4 = (f32[9,8,256]{2,1,0:T(8,128)S(1)}, f32[9,8,256]{2,1,0:T(8,128)S(1)}, u32[]{:S(2)}, u32[]{:S(2)}) collective-permute-start(f32[9,8,256]{2,1,0:T(8,128)S(1)} %add.27), channel_id=1, source_target_pairs={{0,16},{8,24},{16,0},{24,8},{1,17},{9,25},{17,1},{25,9},{2,18},{10... | collective-permute-start | bytes 221192 | tf_op jit(solution)/shard_map/ppermute | solution.py:250
  59.7 3.1 %collective-permute-start.5 = (f32[8,256]{1,0:T(8,128)S(1)}, f32[8,256]{1,0:T(8,128)S(1)}, u32[]{:S(2)}, u32[]{:S(2)}) collective-permute-start(f32[8,256]{1,0:T(8,128)S(1)} %get-tuple-element.13), channel_id=1, source_target_pairs={{1,0},{2,1},{3,2},{4,3},{5,4},{6,5},{7,6},{8,7},{9,8},{10,9},{11,1... | collective-permute-start | bytes 24584 | tf_op jit(solution)/shard_map/ppermute | solution.py:280
  62.7 3.1 %collective-permute-start.6 = (f32[8,256]{1,0:T(8,128)S(1)}, f32[8,256]{1,0:T(8,128)S(1)}, u32[]{:S(2)}, u32[]{:S(2)}) collective-permute-start(f32[8,256]{1,0:T(8,128)S(1)} %add.29.near_image), channel_id=1, source_target_pairs={{0,1},{1,2},{2,3},{3,4},{4,5},{5,6},{6,7},{7,8},{8,9},{9,10},{10,1... | collective-permute-start | bytes 24584 | tf_op jit(solution)/shard_map/ppermute | solution.py:281

commit v2 on v1

v2 whole, which is shorter than its diff:
```python
import functools
import math

import jax
import jax.numpy as jnp
from jax import lax
from jax.experimental import pallas as pl
from jax.experimental.pallas import tpu as pltpu
from jax.sharding import PartitionSpec as P

SCALE_LENGTH = 0.5
NUGGET = 0.5
SQRT_THREE = math.sqrt(3.0)
LANES = 128
HIGHEST = lax.Precision.HIGHEST
F32 = jnp.float32
NN = (((1,), (0,)), ((), ()))
NT = (((1,), (1,)), ((), ()))
AXES = ("grp", "dev")
VMEM_LIMIT = 48 * 1024 * 1024


def split(value):
    high = value.astype(jnp.bfloat16)
    return high, (value - high.astype(F32)).astype(jnp.bfloat16)


def dot(left, right, dims=NN, precision=None):
    return lax.dot_general(left, right, dims, precision=precision, preferred_element_type=F32)


def dot_three(left, right, dims=NN):
    return dot(left[0], right[0], dims) + (dot(left[0], right[1], dims) + dot(left[1], right[0], dims))


def inverse(matrix, beside=()):
    order = matrix.shape[0]
    rows = lax.broadcasted_iota(jnp.int32, (order, order), 0)
    columns = lax.broadcasted_iota(jnp.int32, (order, order), 1)
    identity = (rows == columns).astype(F32)
    start = 2.0 / (2.0 * NUGGET + order)
    least = start * NUGGET
    ahead = start * matrix
    guess = None
    beside = list(beside)
    while True:
        reached = least * (2.0 - least)
        centre = 2.0 / (1.0 + reached)
        least = centre * reached
        ahead_parts = split(ahead)
        if guess is None:
            guess = (centre * start) * (2.0 * identity - ahead)
        else:
            guess = centre * (2.0 * guess - dot_three(split(guess), ahead_parts))
        if beside:
            beside.pop(0)()
        if 1.0 - least < 1e-3:
            break
        ahead = centre * (2.0 * ahead - dot_three(ahead_parts, ahead_parts))
    for work in beside:
        work()
    error = identity - dot(matrix, guess, precision=HIGHEST)
    return guess + dot_three(split(guess), split(error))


def slot_list(slots):
    return [slot for slot in range(slots) if slot != 1]


def mirrored(index, size):
    bits = size.bit_length() - 1
    return sum(((index >> bit) & 1) << (bits - 1 - bit) for bit in range(bits))


def covariance(first, second, alive, same):
    points = second.shape[1]
    rows_at_once = 64
    parts = []
    for start in range(0, points, rows_at_once):
        down = first[start : start + rows_at_once]
        total = None
        for k in range(3):
            offset = down[:, k : k + 1] - second[k : k + 1, :]
            total = offset * offset if total is None else total + offset * offset
        scaled = jnp.sqrt(total)
        value = (1.0 + scaled) * jnp.exp(-scaled) * alive
        if same:
            row = lax.broadcasted_iota(jnp.int32, value.shape, 0) + start
            column = lax.broadcasted_iota(jnp.int32, value.shape, 1)
            value = value + jnp.where(row == column, NUGGET * alive + (1.0 - alive), 0.0)
        parts.append(value)
    return jnp.concatenate(parts, axis=0)


def scaled_places(entry, fields):
    return entry[fields:] * (SQRT_THREE / SCALE_LENGTH)


def live_of(index):
    return (index >= 0).astype(F32)


def pack_kernel(sizes, locations, observed, packed):
    fields = sizes[0]
    packed[...] = jnp.zeros_like(packed)
    packed[:fields] = observed[0]
    packed[fields : fields + 3] = locations[0]


def near_kernel(sizes, nbr, before, mine, middle_out, lower_out, left_out):
    fields = sizes[0]
    alive = live_of(nbr[0, 0])
    places = [scaled_places(before[...], fields), scaled_places(mine[...], fields)]
    turned = [jnp.transpose(place) for place in places]
    side, own = [], []
    first = covariance(turned[0], places[0], alive, True)
    middle = inverse(
        first,
        [
            lambda: side.append(covariance(turned[1], places[0], alive, False)),
            lambda: own.append(covariance(turned[1], places[1], 1.0, True)),
        ],
    )
    lower = dot(side[0], middle, precision=HIGHEST)
    middle_out[...] = middle
    lower_out[...] = lower
    left_out[...] = own[0] - dot_three(split(lower), split(side[0]), NT)


def factor_kernel(
    sizes, nbr, me, before, mine, table, noise, middle_in, lower_in, left_in, part, near_own, near_prev, back_out, last_out, blocks
):
    fields, points, coarse, slots = sizes
    used = slot_list(slots)
    own = len(used)
    ids = [nbr[0, slot] for slot in used] + [me[0]]
    here = lax.rem(me[0], coarse)
    entries = [before[...]]
    entries += [table[mirrored(jnp.maximum(index, 0) ^ here, coarse)] for index in ids[1:own]]
    entries += [mine[...]]
    live = [live_of(index) for index in ids]
    values = [entry[:fields] * alive for entry, alive in zip(entries, live)]
    places = [scaled_places(entry, fields) for entry in entries]
    turned = [jnp.transpose(place) for place in places]

    def build(i, j):
        blocks[i, j] = covariance(turned[i], places[j], live[i] * live[j], i == j)

    halves, lower = {}, {(own, 0): lower_in[...]}

    def parts_of(i, j):
        if (i, j) not in halves:
            halves[i, j] = split(blocks[i, j])
        return halves[i, j]

    def multiply(i, k, middle):
        lower[i, k] = dot(blocks[i, k], middle, precision=HIGHEST)

    def update(i, j, k):
        blocks[i, j] = blocks[i, j] - dot_three(split(lower[i, k]), parts_of(j, k), NT)

    def open_column(i):
        build(i, 0)
        multiply(i, 0, middle_in[...])

    def leave(i, j):
        build(i, j)
        update(i, j, 0)

    blocks[own, own] = left_in[...]
    open_column(1)
    leave(1, 1)
    later = []
    for i in range(2, own):
        later.append(functools.partial(open_column, i))
        later += [functools.partial(leave, i, j) for j in range(1, i + 1)]
    later += [functools.partial(leave, own, j) for j in range(1, own)]
    back = {}

    def go_back(k):
        total = lower[own, k]
        for j in range(k + 1, own):
            total = total - dot_three(split(back[j]), split(lower[j, k]))
        back[k] = total

    for k in range(1, own):
        middle = inverse(blocks[k, k], later)
        for i in range(k + 1, own + 1):
            multiply(i, k, middle)
        update(k + 1, k + 1, k)
        later = [
            functools.partial(update, i, j, k)
            for i in range(k + 1, own + 1)
            for j in range(k + 1, i + 1)
            if (i, j) != (k + 1, k + 1)
        ]
    last = inverse(blocks[own, own], [functools.partial(go_back, k) for k in range(own - 1, -1, -1)])
    for k in range(own):
        back_out[:, k * points : (k + 1) * points] = back[k]
    last_out[...] = last

    middle, spread, slot_parts = apply_block(values, back, last)
    own_part = spread + noise[0] * values[own]
    near_own[...] = own_part
    near_prev[...] = slot_parts[0]
    part[...] = jnp.zeros_like(part)
    product = jnp.sum(middle * spread + noise[0] * values[own] * values[own], axis=1, keepdims=True)
    square = jnp.sum(values[own] * values[own], axis=1, keepdims=True)
    part[coarse] = in_lanes([product, square], (fields, points))
    for index, value in zip(ids, slot_parts + [own_part]):

        @pl.when((index >= 0) & (index < coarse))
        def _(index=index, value=value):
            part[index] = part[index] + value


def in_lanes(columns, shape):
    lane = lax.broadcasted_iota(jnp.int32, shape, 1)
    total = jnp.zeros(shape, F32)
    for at, column in enumerate(columns):
        total = jnp.where(lane == at, column, total)
    return total


def apply_block(values, back, last):
    own = len(values) - 1
    middle = values[own]
    for k in range(own):
        middle = middle - dot_three(split(values[k]), split(back[k]), NT)
    spread = dot_three(split(middle), split(last))
    spread_parts = split(spread)
    slot_parts = [-dot_three(spread_parts, split(back[k])) for k in range(own)]
    return middle, spread, slot_parts


def step_kernel(
    sizes, nbr, me, before, mine, table, noise, summed, near_own, near_prev, own_before, from_after, back, last,
    sends, near_out, own_out, image_out, residual_out, ratio_out,
):
    fields, points, coarse, slots = sizes
    used = slot_list(slots)
    own = len(used)
    ids = [nbr[0, slot] for slot in used] + [me[0]]
    here = lax.rem(me[0], coarse)
    product = summed[coarse][:, 0:1]
    norm_now = summed[coarse][:, 1:2]
    alpha = norm_now / product
    values = []
    for at, index in enumerate(ids):
        image = summed[jnp.clip(index, 0, coarse - 1)]
        if at == 0:
            observed = before[:fields]
            image = jnp.where(index < coarse, image, own_before[...] + near_prev[...])
        elif at == own:
            observed = mine[:fields]
            image = jnp.where(index < coarse, image, near_own[...] + from_after[...])
        else:
            observed = table[mirrored(jnp.maximum(index, 0) ^ here, coarse)][:fields]
        values.append((observed - alpha * image) * live_of(index))
    back_parts = {k: back[:, k * points : (k + 1) * points] for k in range(own)}
    middle, spread, slot_parts = apply_block(values, back_parts, last[...])
    residual = values[own]
    own_part = spread + noise[0] * residual
    inner = jnp.sum(middle * spread + noise[0] * residual * residual, axis=1, keepdims=True)
    cross = jnp.sum(residual * image, axis=1, keepdims=True)
    square = jnp.sum(residual * residual, axis=1, keepdims=True)
    sends[...] = jnp.zeros_like(sends)
    sends[coarse] = in_lanes([inner, cross, square], (fields, points))
    for index, value in zip(ids[1:own], slot_parts[1:]):

        @pl.when(index >= 0)
        def _(index=index, value=value):
            place = mirrored(index ^ here, coarse)
            sends[place] = sends[place] + value

    near_out[...] = slot_parts[0]
    own_out[...] = own_part
    image_out[...] = image
    residual_out[...] = residual
    ratio_out[...] = in_lanes([alpha, norm_now, product], (fields, LANES))


def finish_kernel(
    sizes, me, received, own_part, from_after, image, residual, ratios, observed, solution_out, residual_out
):
    coarse = sizes[2]
    owner = (me[0] < coarse).astype(F32)
    spread = own_part[...] + from_after[...] + owner * received[0]
    scalars = received[1]
    alpha, norm_first, product_first = ratios[:, 0:1], ratios[:, 1:2], ratios[:, 2:3]
    inner, cross, norm_now = scalars[:, 0:1], scalars[:, 1:2], scalars[:, 2:3]
    beta = norm_now / norm_first
    product = inner + beta * (2.0 * cross + beta * product_first)
    step = norm_now / product
    direction = residual[...] + beta * observed[0]
    solution_out[0] = alpha * observed[0] + step * direction
    residual_out[0] = residual[...] - step * (spread + beta * image[...])


def call(kernel, sizes, outs, in_spaces, scratch=()):
    return pl.pallas_call(
        functools.partial(kernel, sizes),
        out_shape=[jax.ShapeDtypeStruct(shape, F32) for shape in outs],
        in_specs=[pl.BlockSpec(memory_space=space) for space in in_spaces],
        out_specs=[pl.BlockSpec(memory_space=pltpu.VMEM)] * len(outs),
        scratch_shapes=list(scratch),
        compiler_params=pltpu.CompilerParams(vmem_limit_bytes=VMEM_LIMIT),
    )


def powers(size):
    assert size & (size - 1) == 0
    return [1 << bit for bit in range(size.bit_length() - 1)]


def swapped(value, axis, reach):
    return lax.ppermute(value, axis, [(at, at ^ reach) for at in range(lax.axis_size(axis))])


def moved(value, distance):
    devices = range(lax.axis_size(AXES))
    return lax.ppermute(value, AXES, [(at, at + distance) for at in devices if at + distance in devices])


def local(locations, neighbours, observations, noise_prec):
    blocks, _, points = locations.shape
    fields = observations.shape[1]
    slots = neighbours.shape[1]
    assert blocks == 1
    coarse, groups = lax.axis_size("dev"), lax.axis_size("grp")
    sizes = (fields, points, coarse, slots)
    depth = len(slot_list(slots)) * points
    me = lax.axis_index(AXES).astype(jnp.int32).reshape(1)
    group = lax.axis_index("grp")
    smem, vmem = pltpu.SMEM, pltpu.VMEM
    square, tile = (points, points), (fields, points)

    (mine,) = call(pack_kernel, sizes, [(2 * fields, points)], [vmem, vmem])(locations, observations)
    before = moved(mine, 1)
    first = mine
    for reach in powers(groups):
        got = lax.ppermute(first, "grp", [(at, at + reach) for at in range(reach)])
        first = jnp.where((group >= reach) & (group < 2 * reach), got, first)
    table = first[None]
    reaches = powers(coarse)[::-1]
    for at, reach in enumerate(reaches):
        if at == 1:
            table, before = lax.optimization_barrier((table, before))
        if at == len(reaches) - 1:
            table, eliminated = lax.optimization_barrier((table, eliminated))
        got = swapped(table, "dev", reach)
        if at == 1:
            eliminated = call(near_kernel, sizes, [square] * 3, [smem, vmem, vmem])(neighbours, before, mine)
        table = jnp.concatenate([table, got], axis=0)
    part, near_own, near_prev, back, last = call(
        factor_kernel,
        sizes,
        [(coarse + 1,) + tile, tile, tile, (points, depth), square],
        [smem, smem] + [vmem] * 7,
        [pltpu.VMEM((slots, slots) + square, F32)],
    )(neighbours, me, before, mine, table, noise_prec, *eliminated)

    own_before, from_after = moved(near_own, 1), moved(near_prev, -1)
    for reach in powers(coarse):
        part = part + swapped(part, "dev", reach)
    part, own_before, from_after = lax.optimization_barrier((part, own_before, from_after))
    for reach in powers(groups):
        part = part + swapped(part, "grp", reach)
    sends, near_part, own_part, image, residual, ratios = call(
        step_kernel,
        sizes,
        [(coarse + 1,) + tile, tile, tile, tile, tile, (fields, LANES)],
        [smem, smem] + [vmem] * 11,
    )(neighbours, me, before, mine, table, noise_prec, part, near_own, near_prev, own_before, from_after, back, last)

    from_after = moved(near_part, -1)
    for reach in powers(coarse):
        kept = (sends.shape[0] - 1) // 2
        got = swapped(sends[kept:], "dev", reach)
        sends = jnp.concatenate([sends[:kept], sends[-1:]], axis=0) + got
    sends, from_after = lax.optimization_barrier((sends, from_after))
    for reach in powers(groups):
        sends = sends + swapped(sends, "grp", reach)
    return tuple(
        call(finish_kernel, sizes, [observations.shape] * 2, [smem] + [vmem] * 7)(
            me, sends, own_part, from_after, image, residual, ratios, observations
        )
    )


def solution(mesh):
    placed = (
        P(AXES, None, None),
        P(AXES, None),
        P(AXES, None, None),
        P(AXES, None, None),
    )
    return jax.shard_map(
        local,
        mesh=mesh,
        in_specs=placed,
        out_specs=(P(AXES, None, None), P(AXES, None, None)),
        check_vma=False,
    )
```

time: 89.5 us -> 93.4 us (1.044)
  starting transfers between devices: 12.8 us -> 37.9 us
  blocking collectives: 20.7 us -> 0 us
  waiting for transfers between devices: 30.9 us -> 27.9 us
  Pallas kernels: 21.9 us -> 23.5 us
    ppermute x7 -> x19, starting transfers between devices: 5.48 us -> 37.9 us  [the longest x13 26.6 us: swapped(): lax.ppermute(value, axis, [(at, at ^ reach) for at in range(lax.axis_size...]
    all_to_all x1 -> x0, blocking collectives: 20.7 us -> none  [local(): received = lax.all_to_all(sends, AXES, 0, 0, tiled=True)]
    all_to_all x1 -> x0, waiting for transfers between devices: 13.5 us -> none  [local(): lax.all_to_all(jnp.broadcast_to(packed, (devices,) + packed.shape), AXES,...]
    ppermute x7 -> x19, waiting for transfers between devices: 17.4 us -> 27.9 us  [the longest x13 24 us: swapped(): lax.ppermute(value, axis, [(at, at ^ reach) for at in range(lax.axis_size...]
    all_to_all x1 -> x0, starting transfers between devices: 7.3 us -> none  [local(): lax.all_to_all(jnp.broadcast_to(packed, (devices,) + packed.shape), AXES,...]
    pallas_call x3 -> x5, Pallas kernels: 21.9 us -> 23.5 us  [the longest x1 15.7 us: local(): call(factor_kernel, sizes, [(coarse + 1,) + tile, tile, tile, (points, de...]
    unnamed x7 -> x10, local copies, waits for them, and re-layouts: 1.39 us -> 2.74 us
  transfers between devices with their start and end apart: 8 -> 19, of which waited for: 7 -> 16; matrix products, arithmetic and copies ran while one was open for 0% -> 0% of each run, Pallas kernels for 0% -> 5%
where the time goes in v2:
time: 93.4 us; the launch traced here: 93 us
  starting transfers between devices  37.9 us (41%)
  waiting for transfers between devices  27.9 us (30%)
  Pallas kernels  23.5 us (25%)
  local copies, waits for them, and re-layouts  2.78 us (3%)
    ppermute x13, starting transfers between devices, swapped(): lax.ppermute(value, axis, [(at, at ^ reach) for at in range(lax.axis_size...  26.6 us
    ppermute x13, waiting for transfers between devices, swapped(): lax.ppermute(value, axis, [(at, at ^ reach) for at in range(lax.axis_size...  24 us
    pallas_call x1, Pallas kernels, local(): call(factor_kernel, sizes, [(coarse + 1,) + tile, tile, tile, (points, de...  15.7 us
    ppermute x2, starting transfers between devices, local(): got = lax.ppermute(first, 'grp', [(at, at + reach) for at in range(reach)])  6.11 us
    ppermute x4, starting transfers between devices, moved(): lax.ppermute(value, AXES, [(at, at + distance) for at in devices if at +...  5.14 us
    pallas_call x1, Pallas kernels, local(): call(near_kernel, sizes, [square] * 3, [smem, vmem, vmem])  5.07 us
    ppermute x2, waiting for transfers between devices, local(): got = lax.ppermute(first, 'grp', [(at, at + reach) for at in range(reach)])  2.83 us
    unnamed x10, local copies, waits for them, and re-layouts  2.74 us
  transfers between devices with their start and end apart: 19, of which 16 were waited for; matrix products, arithmetic and copies ran while one was open for 0% of the time, Pallas kernels for 5%

profile of v2, /device:TPU:0, one launch (start us, length us, event | category | flops | bytes accessed | tf_op | source)
XLA Modules:
  0.0 93.0 jit_solution(12344735639639469315)
XLA Ops:
  0.6 0.7 copy.6.locations
  1.3 0.0 copy-start.1
  1.3 0.7 copy-done.1
  2.0 4.8 %collective-permute-start = (f32[16,256]{1,0:T(8,128)S(1)}, f32[16,256]{1,0:T(8,128)S(1)}, u32[]{:S(2)}, u32[]{:S(2)}) collective-permute-start(f32[16,256]{1,0:T(8,128)S(1)} %shard_map.59.mine), channel_id=1, source_target_pairs={{0,8},{1,9},{2,10},{3,11},{4,12},{5,13},{6,14},{7,15}} | collective-permute-start | bytes 49160 | tf_op jit(solution)/shard_map/ppermute | solution.py:342
  6.9 1.4 %collective-permute-done = f32[16,256]{1,0:T(8,128)S(1)} collective-permute-done((f32[16,256]{1,0:T(8,128)S(1)}, f32[16,256]{1,0:T(8,128)S(1)}, u32[]{:S(2)}, u32[]{:S(2)}) %collective-permute-start) | collective-permute-done | bytes 16416 | tf_op jit(solution)/shard_map/ppermute | solution.py:342
  8.3 1.3 %collective-permute-start.1 = (f32[16,256]{1,0:T(8,128)S(1)}, f32[16,256]{1,0:T(8,128)S(1)}, u32[]{:S(2)}, u32[]{:S(2)}) collective-permute-start(f32[16,256]{1,0:T(8,128)S(1)} %broadcast_select_fusion), channel_id=1, source_target_pairs={{0,16},{8,24},{1,17},{9,25},{2,18},{10,26},{3,19},{11,27},{4,20},{... | collective-permute-start | bytes 49160 | tf_op jit(solution)/shard_map/ppermute | solution.py:342
  9.6 1.4 %collective-permute-done.1 = f32[16,256]{1,0:T(8,128)S(1)} collective-permute-done((f32[16,256]{1,0:T(8,128)S(1)}, f32[16,256]{1,0:T(8,128)S(1)}, u32[]{:S(2)}, u32[]{:S(2)}) %collective-permute-start.1) | collective-permute-done | bytes 16416 | tf_op jit(solution)/shard_map/ppermute | solution.py:342
  11.0 2.6 %collective-permute-start.2 = (f32[1,16,256]{2,1,0:T(8,128)S(1)}, f32[1,16,256]{2,1,0:T(8,128)S(1)}, u32[]{:S(2)}, u32[]{:S(2)}) collective-permute-start(f32[1,16,256]{2,1,0:T(8,128)S(1)} %select_bitcast_fusion), channel_id=1, source_target_pairs={{0,4},{1,5},{2,6},{3,7},{4,0},{5,1},{6,2},{7,3},{8,12},{9,13},{10,... | collective-permute-start | bytes 49160 | tf_op jit(solution)/shard_map/ppermute | solution.py:317
  13.6 1.3 %collective-permute-start.3 = (f32[16,256]{1,0:T(8,128)S(1)}, f32[16,256]{1,0:T(8,128)S(1)}, u32[]{:S(2)}, u32[]{:S(2)}) collective-permute-start(f32[16,256]{1,0:T(8,128)S(1)} %shard_map.59.mine), channel_id=1, source_target_pairs={{0,1},{1,2},{2,3},{3,4},{4,5},{5,6},{6,7},{7,8},{8,9},{9,10},{10,1... | collective-permute-start | bytes 49160 | tf_op jit(solution)/shard_map/ppermute | solution.py:322
  14.9 0.8 collective-permute-done.2
  15.6 0.1 collective-permute-done.3.before
  15.7 4.5 %collective-permute-start.4 = (f32[2,16,256]{2,1,0:T(8,128)S(1)}, f32[2,16,256]{2,1,0:T(8,128)S(1)}, u32[]{:S(2)}, u32[]{:S(2)}) collective-permute-start(f32[2,16,256]{2,1,0:T(8,128)S(1)} %pad_maximum_fusion.1), channel_id=1, source_target_pairs={{0,2},{1,3},{2,0},{3,1},{4,6},{5,7},{6,4},{7,5},{8,10},{9,11},{10,... | collective-permute-start | bytes 98312 | tf_op jit(solution)/shard_map/ppermute | solution.py:317
  20.2 0.0 copy-start.3
  20.2 0.7 copy-done.3
  20.9 5.1 %shard_map.60 = (f32[256,256]{1,0:T(8,128)S(1)}, f32[256,256]{1,0:T(8,128)S(1)}, f32[256,256]{1,0:T(8,128)S(1)}) custom-call(s32[1,4]{1,0:T(1,128)S(1)} %copy-done.3, f32[16,256]{1,0:T(8,128)S(1)} %collective-permute-done.3.before, f32[16,256]{1,0:T(8,128)S(1)} %shard_map.59.mine), custom_call_target="tpu_custom_call" | custom-call | tf_op jit(solution)/shard_map/pallas_call | solution.py:353
  25.9 0.0 collective-permute-done.4
  26.0 0.1 collective-permute-start.5
  26.1 0.0 copy-start
  26.1 1.2 %collective-permute-done.5 = f32[4,16,256]{2,1,0:T(8,128)S(1)} collective-permute-done((f32[4,16,256]{2,1,0:T(8,128)S(1)}, f32[4,16,256]{2,1,0:T(8,128)S(1)}, u32[]{:S(2)}, u32[]{:S(2)}) %collective-permute-start.5) | collective-permute-done | bytes 65568 | tf_op jit(solution)/shard_map/ppermute | solution.py:317
  27.3 0.0 copy-done
  27.3 15.7 %shard_map.61 = (f32[9,8,256]{2,1,0:T(8,128)S(1)}, f32[8,256]{1,0:T(8,128)S(1)}, f32[8,256]{1,0:T(8,128)S(1)}, f32[256,768]{1,0:T(8,128)S(1)}, f32[256,256]{1,0:T(8,128)S(1)}) custom-call(s32[1,4]{1,0:T(1,128)S(1)} %copy-done.3, s32[1]{0:T(128)} %bitcast.me, f32[16,256]{1,0:T(8,128)S(1)} %collective-permute-done.3.before, f32[16,256]{1,0:T(8,128)S(1)} %shard_map.59.mine, ...), custom_call_target="tpu_custom_call" | custom-call | tf_op jit(solution)/shard_map/pallas_call | solution.py:355
  43.0 0.2 collective-permute-start.6
  43.2 1.1 %collective-permute-done.6 = f32[9,8,256]{2,1,0:T(8,128)S(1)} collective-permute-done((f32[9,8,256]{2,1,0:T(8,128)S(1)}, f32[9,8,256]{2,1,0:T(8,128)S(1)}, u32[]{:S(2)}, u32[]{:S(2)}) %collective-permute-start.6) | collective-permute-done | bytes 73760 | tf_op jit(solution)/shard_map/ppermute | solution.py:317
  44.3 0.1 collective-permute-start.7
  44.4 4.3 %collective-permute-done.7 = f32[9,8,256]{2,1,0:T(8,128)S(1)} collective-permute-done((f32[9,8,256]{2,1,0:T(8,128)S(1)}, f32[9,8,256]{2,1,0:T(8,128)S(1)}, u32[]{:S(2)}, u32[]{:S(2)}) %collective-permute-start.7) | collective-permute-done | bytes 73760 | tf_op jit(solution)/shard_map/ppermute | solution.py:317
  48.8 2.0 %collective-permute-start.8 = (f32[9,8,256]{2,1,0:T(8,128)S(1)}, f32[9,8,256]{2,1,0:T(8,128)S(1)}, u32[]{:S(2)}, u32[]{:S(2)}) collective-permute-start(f32[9,8,256]{2,1,0:T(8,128)S(1)} %add.35), channel_id=1, source_target_pairs={{0,4},{1,5},{2,6},{3,7},{4,0},{5,1},{6,2},{7,3},{8,12},{9,13},{10,... | collective-permute-start | bytes 221192 | tf_op jit(solution)/shard_map/ppermute | solution.py:317
  50.7 1.3 %collective-permute-start.9 = (f32[8,256]{1,0:T(8,128)S(1)}, f32[8,256]{1,0:T(8,128)S(1)}, u32[]{:S(2)}, u32[]{:S(2)}) collective-permute-start(f32[8,256]{1,0:T(8,128)S(1)} %get-tuple-element.37.near_own), channel_id=1, source_target_pairs={{0,1},{1,2},{2,3},{3,4},{4,5},{5,6},{6,7},{7,8},{8,9},{9,10},{10,1... | collective-permute-start | bytes 24584 | tf_op jit(solution)/shard_map/ppermute | solution.py:322
  52.0 1.3 %collective-permute-start.10 = (f32[8,256]{1,0:T(8,128)S(1)}, f32[8,256]{1,0:T(8,128)S(1)}, u32[]{:S(2)}, u32[]{:S(2)}) collective-permute-start(f32[8,256]{1,0:T(8,128)S(1)} %get-tuple-element.38.near_prev), channel_id=1, source_target_pairs={{1,0},{2,1},{3,2},{4,3},{5,4},{6,5},{7,6},{8,7},{9,8},{10,9},{11,1... | collective-permute-start | bytes 24584 | tf_op jit(solution)/shard_map/ppermute | solution.py:322
  53.3 1.2 %collective-permute-done.8 = f32[9,8,256]{2,1,0:T(8,128)S(1)} collective-permute-done((f32[9,8,256]{2,1,0:T(8,128)S(1)}, f32[9,8,256]{2,1,0:T(8,128)S(1)}, u32[]{:S(2)}, u32[]{:S(2)}) %collective-permute-start.8) | collective-permute-done | bytes 73760 | tf_op jit(solution)/shard_map/ppermute | solution.py:317
  54.6 0.0 collective-permute-done.9.own_before
  54.6 1.0 %collective-permute-done.10.from_after = f32[8,256]{1,0:T(8,128)S(1)} collective-permute-done((f32[8,256]{1,0:T(8,128)S(1)}, f32[8,256]{1,0:T(8,128)S(1)}, u32[]{:S(2)}, u32[]{:S(2)}) %collective-permute-start.10) | collective-permute-done | bytes 8224 | tf_op jit(solution)/shard_map/ppermute | solution.py:322
  55.6 6.7 %collective-permute-start.11 = (f32[9,8,256]{2,1,0:T(8,128)S(1)}, f32[9,8,256]{2,1,0:T(8,128)S(1)}, u32[]{:S(2)}, u32[]{:S(2)}) collective-permute-start(f32[9,8,256]{2,1,0:T(8,128)S(1)} %add.36), channel_id=1, source_target_pairs={{0,8},{8,0},{16,24},{24,16},{1,9},{9,1},{17,25},{25,17},{2,10},{10... | collective-permute-start | bytes 221192 | tf_op jit(solution)/shard_map/ppermute | solution.py:317
  62.3 2.3 %collective-permute-done.11 = f32[9,8,256]{2,1,0:T(8,128)S(1)} collective-permute-done((f32[9,8,256]{2,1,0:T(8,128)S(1)}, f32[9,8,256]{2,1,0:T(8,128)S(1)}, u32[]{:S(2)}, u32[]{:S(2)}) %collective-permute-start.11) | collective-permute-done | bytes 73760 | tf_op jit(solution)/shard_map/ppermute | solution.py:317
  64.7 3.7 %collective-permute-start.12 = (f32[9,8,256]{2,1,0:T(8,128)S(1)}, f32[9,8,256]{2,1,0:T(8,128)S(1)}, u32[]{:S(2)}, u32[]{:S(2)}) collective-permute-start(f32[9,8,256]{2,1,0:T(8,128)S(1)} %add.37), channel_id=1, source_target_pairs={{0,16},{8,24},{16,0},{24,8},{1,17},{9,25},{17,1},{25,9},{2,18},{10... | collective-permute-start | bytes 221192 | tf_op jit(solution)/shard_map/ppermute | solution.py:317
  68.4 2.3 %collective-permute-done.12 = f32[9,8,256]{2,1,0:T(8,128)S(1)} collective-permute-done((f32[9,8,256]{2,1,0:T(8,128)S(1)}, f32[9,8,256]{2,1,0:T(8,128)S(1)}, u32[]{:S(2)}, u32[]{:S(2)}) %collective-permute-start.12) | collective-permute-done | bytes 73760 | tf_op jit(solution)/shard_map/ppermute | solution.py:317
  70.7 1.7 %shard_map.62 = (f32[9,8,256]{2,1,0:T(8,128)S(1)}, f32[8,256]{1,0:T(8,128)S(1)}, f32[8,256]{1,0:T(8,128)S(1)}, f32[8,256]{1,0:T(8,128)S(1)}, f32[8,256]{1,0:T(8,128)S(1)}, /*index=5*/f32[8,128]{1,0:T(8,128)S(1)}) custom-call(s32[1,4]{1,0:T(1,128)S(1)} %copy-done.3, s32[1]{0:T(128)} %bitcast.me, f32[16,256]{1,0:T(8,128)S(1)} %collective-permute-done.3.before, ...), custom_call_target="tpu_custom_call" | custom-call | tf_op jit(solution)/shard_map/pallas_call | solution.py:369
  72.4 0.0 collective-permute-start.13
  72.5 1.2 %collective-permute-done.13 = f32[5,8,256]{2,1,0:T(8,128)S(1)} collective-permute-done((f32[5,8,256]{2,1,0:T(8,128)S(1)}, f32[5,8,256]{2,1,0:T(8,128)S(1)}, u32[]{:S(2)}, u32[]{:S(2)}) %collective-permute-start.13) | collective-permute-done | bytes 40992 | tf_op jit(solution)/shard_map/ppermute | solution.py:317
  73.7 0.1 collective-permute-start.14
  73.8 1.3 %collective-permute-start.16 = (f32[8,256]{1,0:T(8,128)S(1)}, f32[8,256]{1,0:T(8,128)S(1)}, u32[]{:S(2)}, u32[]{:S(2)}) collective-permute-start(f32[8,256]{1,0:T(8,128)S(1)} %get-tuple-element.45), channel_id=1, source_target_pairs={{1,0},{2,1},{3,2},{4,3},{5,4},{6,5},{7,6},{8,7},{9,8},{10,9},{11,1... | collective-permute-start | bytes 24584 | tf_op jit(solution)/shard_map/ppermute | solution.py:322
  75.1 2.5 %collective-permute-done.14 = f32[3,8,256]{2,1,0:T(8,128)S(1)} collective-permute-done((f32[3,8,256]{2,1,0:T(8,128)S(1)}, f32[3,8,256]{2,1,0:T(8,128)S(1)}, u32[]{:S(2)}, u32[]{:S(2)}) %collective-permute-start.14) | collective-permute-done | bytes 24608 | tf_op jit(solution)/shard_map/ppermute | solution.py:317
  77.6 1.2 %collective-permute-start.15 = (f32[2,8,256]{2,1,0:T(8,128)S(1)}, f32[2,8,256]{2,1,0:T(8,128)S(1)}, u32[]{:S(2)}, u32[]{:S(2)}) collective-permute-start(f32[2,8,256]{2,1,0:T(8,128)S(1)} %slice.41), channel_id=1, source_target_pairs={{0,4},{1,5},{2,6},{3,7},{4,0},{5,1},{6,2},{7,3},{8,12},{9,13},{10,... | collective-permute-start | bytes 49160 | tf_op jit(solution)/shard_map/ppermute | solution.py:317
  78.8 3.5 %collective-permute-done.15 = f32[2,8,256]{2,1,0:T(8,128)S(1)} collective-permute-done((f32[2,8,256]{2,1,0:T(8,128)S(1)}, f32[2,8,256]{2,1,0:T(8,128)S(1)}, u32[]{:S(2)}, u32[]{:S(2)}) %collective-permute-start.15) | collective-permute-done | bytes 16416 | tf_op jit(solution)/shard_map/ppermute | solution.py:317
  82.3 0.0 collective-permute-done.16.from_after
  82.3 2.1 %collective-permute-start.17 = (f32[2,8,256]{2,1,0:T(8,128)S(1)}, f32[2,8,256]{2,1,0:T(8,128)S(1)}, u32[]{:S(2)}, u32[]{:S(2)}) collective-permute-start(f32[2,8,256]{2,1,0:T(8,128)S(1)} %maximum_add_fusion.2), channel_id=1, source_target_pairs={{0,8},{8,0},{16,24},{24,16},{1,9},{9,1},{17,25},{25,17},{2,10},{10... | collective-permute-start | bytes 49160 | tf_op jit(solution)/shard_map/ppermute | solution.py:317
  84.4 1.7 %collective-permute-done.17 = f32[2,8,256]{2,1,0:T(8,128)S(1)} collective-permute-done((f32[2,8,256]{2,1,0:T(8,128)S(1)}, f32[2,8,256]{2,1,0:T(8,128)S(1)}, u32[]{:S(2)}, u32[]{:S(2)}) %collective-permute-start.17) | collective-permute-done | bytes 16416 | tf_op jit(solution)/shard_map/ppermute | solution.py:317
  86.1 3.5 %collective-permute-start.18 = (f32[2,8,256]{2,1,0:T(8,128)S(1)}, f32[2,8,256]{2,1,0:T(8,128)S(1)}, u32[]{:S(2)}, u32[]{:S(2)}) collective-permute-start(f32[2,8,256]{2,1,0:T(8,128)S(1)} %add.42), channel_id=1, source_target_pairs={{0,16},{8,24},{16,0},{24,8},{1,17},{9,25},{17,1},{25,9},{2,18},{10... | collective-permute-start | bytes 49160 | tf_op jit(solution)/shard_map/ppermute | solution.py:317
  89.6 1.7 %collective-permute-done.18 = f32[2,8,256]{2,1,0:T(8,128)S(1)} collective-permute-done((f32[2,8,256]{2,1,0:T(8,128)S(1)}, f32[2,8,256]{2,1,0:T(8,128)S(1)}, u32[]{:S(2)}, u32[]{:S(2)}) %collective-permute-start.18) | collective-permute-done | bytes 16416 | tf_op jit(solution)/shard_map/ppermute | solution.py:317
  91.3 0.0 copy-start.2
  91.3 0.7 copy-done.2
  92.0 1.0 %shard_map.63 = (f32[1,8,256]{2,1,0:T(8,128)}, f32[1,8,256]{2,1,0:T(8,128)}) custom-call(s32[1]{0:T(128)} %bitcast.me, f32[2,8,256]{2,1,0:T(8,128)S(1)} %add.43.received, f32[8,256]{1,0:T(8,128)S(1)} %get-tuple-element.47.own_part, f32[8,256]{1,0:T(8,128)S(1)} %collective-permute-done.16.from_after, f32[8,256]{1,0:T(8,128)S(1)} %get-tuple-element.49.image, ...), custom_call_target="tpu_custom_call" | custom-call | tf_op jit(solution)/shard_map/pallas_call | solution.py:385
  (25 shorter events, 0.1 us)
Async XLA Ops:
  1.3 0.7 copy-start.1
  2.0 6.3 %collective-permute-start = (f32[16,256]{1,0:T(8,128)S(1)}, f32[16,256]{1,0:T(8,128)S(1)}, u32[]{:S(2)}, u32[]{:S(2)}) collective-permute-start(f32[16,256]{1,0:T(8,128)S(1)} %shard_map.59.mine), channel_id=1, source_target_pairs={{0,8},{1,9},{2,10},{3,11},{4,12},{5,13},{6,14},{7,15}} | collective-permute-start | bytes 49160 | tf_op jit(solution)/shard_map/ppermute | solution.py:342
  8.3 2.7 %collective-permute-start.1 = (f32[16,256]{1,0:T(8,128)S(1)}, f32[16,256]{1,0:T(8,128)S(1)}, u32[]{:S(2)}, u32[]{:S(2)}) collective-permute-start(f32[16,256]{1,0:T(8,128)S(1)} %broadcast_select_fusion), channel_id=1, source_target_pairs={{0,16},{8,24},{1,17},{9,25},{2,18},{10,26},{3,19},{11,27},{4,20},{... | collective-permute-start | bytes 49160 | tf_op jit(solution)/shard_map/ppermute | solution.py:342
  11.0 4.6 %collective-permute-start.2 = (f32[1,16,256]{2,1,0:T(8,128)S(1)}, f32[1,16,256]{2,1,0:T(8,128)S(1)}, u32[]{:S(2)}, u32[]{:S(2)}) collective-permute-start(f32[1,16,256]{2,1,0:T(8,128)S(1)} %select_bitcast_fusion), channel_id=1, source_target_pairs={{0,4},{1,5},{2,6},{3,7},{4,0},{5,1},{6,2},{7,3},{8,12},{9,13},{10,... | collective-permute-start | bytes 49160 | tf_op jit(solution)/shard_map/ppermute | solution.py:317
  13.6 2.1 %collective-permute-start.3 = (f32[16,256]{1,0:T(8,128)S(1)}, f32[16,256]{1,0:T(8,128)S(1)}, u32[]{:S(2)}, u32[]{:S(2)}) collective-permute-start(f32[16,256]{1,0:T(8,128)S(1)} %shard_map.59.mine), channel_id=1, source_target_pairs={{0,1},{1,2},{2,3},{3,4},{4,5},{5,6},{6,7},{7,8},{8,9},{9,10},{10,1... | collective-permute-start | bytes 49160 | tf_op jit(solution)/shard_map/ppermute | solution.py:322
  15.7 10.3 %collective-permute-start.4 = (f32[2,16,256]{2,1,0:T(8,128)S(1)}, f32[2,16,256]{2,1,0:T(8,128)S(1)}, u32[]{:S(2)}, u32[]{:S(2)}) collective-permute-start(f32[2,16,256]{2,1,0:T(8,128)S(1)} %pad_maximum_fusion.1), channel_id=1, source_target_pairs={{0,2},{1,3},{2,0},{3,1},{4,6},{5,7},{6,4},{7,5},{8,10},{9,11},{10,... | collective-permute-start | bytes 98312 | tf_op jit(solution)/shard_map/ppermute | solution.py:317
  20.2 0.7 copy-start.3
  26.0 1.3 %collective-permute-start.5 = (f32[4,16,256]{2,1,0:T(8,128)S(1)}, f32[4,16,256]{2,1,0:T(8,128)S(1)}, u32[]{:S(2)}, u32[]{:S(2)}) collective-permute-start(f32[4,16,256]{2,1,0:T(8,128)S(1)} %pad_maximum_fusion), channel_id=1, source_target_pairs={{0,1},{1,0},{2,3},{3,2},{4,5},{5,4},{6,7},{7,6},{8,9},{9,8},{10,11... | collective-permute-start | bytes 196616 | tf_op jit(solution)/shard_map/ppermute | solution.py:317
  26.1 1.2 %copy-start = (f32[1,8,256]{2,1,0:T(8,128)S(1)}, f32[1,8,256]{2,1,0:T(8,128)}, u32[]{:S(2)}) copy-start(f32[1,8,256]{2,1,0:T(8,128)} %noise.3) | copy-start | bytes 24580
  43.0 1.3 %collective-permute-start.6 = (f32[9,8,256]{2,1,0:T(8,128)S(1)}, f32[9,8,256]{2,1,0:T(8,128)S(1)}, u32[]{:S(2)}, u32[]{:S(2)}) collective-permute-start(f32[9,8,256]{2,1,0:T(8,128)S(1)} %get-tuple-element.36), channel_id=1, source_target_pairs={{0,1},{1,0},{2,3},{3,2},{4,5},{5,4},{6,7},{7,6},{8,9},{9,8},{10,11... | collective-permute-start | bytes 221192 | tf_op jit(solution)/shard_map/ppermute | solution.py:317
  44.3 4.4 %collective-permute-start.7 = (f32[9,8,256]{2,1,0:T(8,128)S(1)}, f32[9,8,256]{2,1,0:T(8,128)S(1)}, u32[]{:S(2)}, u32[]{:S(2)}) collective-permute-start(f32[9,8,256]{2,1,0:T(8,128)S(1)} %add.34), channel_id=1, source_target_pairs={{0,2},{1,3},{2,0},{3,1},{4,6},{5,7},{6,4},{7,5},{8,10},{9,11},{10,... | collective-permute-start | bytes 221192 | tf_op jit(solution)/shard_map/ppermute | solution.py:317
  48.8 5.8 %collective-permute-start.8 = (f32[9,8,256]{2,1,0:T(8,128)S(1)}, f32[9,8,256]{2,1,0:T(8,128)S(1)}, u32[]{:S(2)}, u32[]{:S(2)}) collective-permute-start(f32[9,8,256]{2,1,0:T(8,128)S(1)} %add.35), channel_id=1, source_target_pairs={{0,4},{1,5},{2,6},{3,7},{4,0},{5,1},{6,2},{7,3},{8,12},{9,13},{10,... | collective-permute-start | bytes 221192 | tf_op jit(solution)/shard_map/ppermute | solution.py:317
  50.7 3.9 %collective-permute-start.9 = (f32[8,256]{1,0:T(8,128)S(1)}, f32[8,256]{1,0:T(8,128)S(1)}, u32[]{:S(2)}, u32[]{:S(2)}) collective-permute-start(f32[8,256]{1,0:T(8,128)S(1)} %get-tuple-element.37.near_own), channel_id=1, source_target_pairs={{0,1},{1,2},{2,3},{3,4},{4,5},{5,6},{6,7},{7,8},{8,9},{9,10},{10,1... | collective-permute-start | bytes 24584 | tf_op jit(solution)/shard_map/ppermute | solution.py:322
  52.0 3.6 %collective-permute-start.10 = (f32[8,256]{1,0:T(8,128)S(1)}, f32[8,256]{1,0:T(8,128)S(1)}, u32[]{:S(2)}, u32[]{:S(2)}) collective-permute-start(f32[8,256]{1,0:T(8,128)S(1)} %get-tuple-element.38.near_prev), channel_id=1, source_target_pairs={{1,0},{2,1},{3,2},{4,3},{5,4},{6,5},{7,6},{8,7},{9,8},{10,9},{11,1... | collective-permute-start | bytes 24584 | tf_op jit(solution)/shard_map/ppermute | solution.py:322
  55.6 9.0 %collective-permute-start.11 = (f32[9,8,256]{2,1,0:T(8,128)S(1)}, f32[9,8,256]{2,1,0:T(8,128)S(1)}, u32[]{:S(2)}, u32[]{:S(2)}) collective-permute-start(f32[9,8,256]{2,1,0:T(8,128)S(1)} %add.36), channel_id=1, source_target_pairs={{0,8},{8,0},{16,24},{24,16},{1,9},{9,1},{17,25},{25,17},{2,10},{10... | collective-permute-start | bytes 221192 | tf_op jit(solution)/shard_map/ppermute | solution.py:317
  64.7 6.0 %collective-permute-start.12 = (f32[9,8,256]{2,1,0:T(8,128)S(1)}, f32[9,8,256]{2,1,0:T(8,128)S(1)}, u32[]{:S(2)}, u32[]{:S(2)}) collective-permute-start(f32[9,8,256]{2,1,0:T(8,128)S(1)} %add.37), channel_id=1, source_target_pairs={{0,16},{8,24},{16,0},{24,8},{1,17},{9,25},{17,1},{25,9},{2,18},{10... | collective-permute-start | bytes 221192 | tf_op jit(solution)/shard_map/ppermute | solution.py:317
  72.4 1.2 %collective-permute-start.13 = (f32[5,8,256]{2,1,0:T(8,128)S(1)}, f32[5,8,256]{2,1,0:T(8,128)S(1)}, u32[]{:S(2)}, u32[]{:S(2)}) collective-permute-start(f32[5,8,256]{2,1,0:T(8,128)S(1)} %slice.29), channel_id=1, source_target_pairs={{0,1},{1,0},{2,3},{3,2},{4,5},{5,4},{6,7},{7,6},{8,9},{9,8},{10,11... | collective-permute-start | bytes 122888 | tf_op jit(solution)/shard_map/ppermute | solution.py:317
  73.7 3.9 %collective-permute-start.14 = (f32[3,8,256]{2,1,0:T(8,128)S(1)}, f32[3,8,256]{2,1,0:T(8,128)S(1)}, u32[]{:S(2)}, u32[]{:S(2)}) collective-permute-start(f32[3,8,256]{2,1,0:T(8,128)S(1)} %slice.38), channel_id=1, source_target_pairs={{0,2},{1,3},{2,0},{3,1},{4,6},{5,7},{6,4},{7,5},{8,10},{9,11},{10,... | collective-permute-start | bytes 73736 | tf_op jit(solution)/shard_map/ppermute | solution.py:317
  73.8 8.5 %collective-permute-start.16 = (f32[8,256]{1,0:T(8,128)S(1)}, f32[8,256]{1,0:T(8,128)S(1)}, u32[]{:S(2)}, u32[]{:S(2)}) collective-permute-start(f32[8,256]{1,0:T(8,128)S(1)} %get-tuple-element.45), channel_id=1, source_target_pairs={{1,0},{2,1},{3,2},{4,3},{5,4},{6,5},{7,6},{8,7},{9,8},{10,9},{11,1... | collective-permute-start | bytes 24584 | tf_op jit(solution)/shard_map/ppermute | solution.py:322
  77.6 4.7 %collective-permute-start.15 = (f32[2,8,256]{2,1,0:T(8,128)S(1)}, f32[2,8,256]{2,1,0:T(8,128)S(1)}, u32[]{:S(2)}, u32[]{:S(2)}) collective-permute-start(f32[2,8,256]{2,1,0:T(8,128)S(1)} %slice.41), channel_id=1, source_target_pairs={{0,4},{1,5},{2,6},{3,7},{4,0},{5,1},{6,2},{7,3},{8,12},{9,13},{10,... | collective-permute-start | bytes 49160 | tf_op jit(solution)/shard_map/ppermute | solution.py:317
  82.3 3.8 %collective-permute-start.17 = (f32[2,8,256]{2,1,0:T(8,128)S(1)}, f32[2,8,256]{2,1,0:T(8,128)S(1)}, u32[]{:S(2)}, u32[]{:S(2)}) collective-permute-start(f32[2,8,256]{2,1,0:T(8,128)S(1)} %maximum_add_fusion.2), channel_id=1, source_target_pairs={{0,8},{8,0},{16,24},{24,16},{1,9},{9,1},{17,25},{25,17},{2,10},{10... | collective-permute-start | bytes 49160 | tf_op jit(solution)/shard_map/ppermute | solution.py:317
  86.1 5.2 %collective-permute-start.18 = (f32[2,8,256]{2,1,0:T(8,128)S(1)}, f32[2,8,256]{2,1,0:T(8,128)S(1)}, u32[]{:S(2)}, u32[]{:S(2)}) collective-permute-start(f32[2,8,256]{2,1,0:T(8,128)S(1)} %add.42), channel_id=1, source_target_pairs={{0,16},{8,24},{16,0},{24,8},{1,17},{9,25},{17,1},{25,9},{2,18},{10... | collective-permute-start | bytes 49160 | tf_op jit(solution)/shard_map/ppermute | solution.py:317
  91.3 0.7 copy-start.2

commit v3 on v2

v3 whole, which is shorter than its diff:
```python
import functools
import math

import jax
import jax.numpy as jnp
from jax import lax
from jax.experimental import pallas as pl
from jax.experimental.pallas import tpu as pltpu
from jax.sharding import PartitionSpec as P

SCALE_LENGTH = 0.5
NUGGET = 0.5
SQRT_THREE = math.sqrt(3.0)
LANES = 128
HIGHEST = lax.Precision.HIGHEST
F32 = jnp.float32
NN = (((1,), (0,)), ((), ()))
NT = (((1,), (1,)), ((), ()))
AXES = ("grp", "dev")
VMEM_LIMIT = 48 * 1024 * 1024


def split(value):
    high = value.astype(jnp.bfloat16)
    return high, (value - high.astype(F32)).astype(jnp.bfloat16)


def dot(left, right, dims=NN, precision=None):
    return lax.dot_general(left, right, dims, precision=precision, preferred_element_type=F32)


def dot_three(left, right, dims=NN):
    return dot(left[0], right[0], dims) + (dot(left[0], right[1], dims) + dot(left[1], right[0], dims))


def inverse(matrix, beside=()):
    order = matrix.shape[0]
    rows = lax.broadcasted_iota(jnp.int32, (order, order), 0)
    columns = lax.broadcasted_iota(jnp.int32, (order, order), 1)
    identity = (rows == columns).astype(F32)
    start = 2.0 / (2.0 * NUGGET + order)
    least = start * NUGGET
    ahead = start * matrix
    guess = None
    beside = list(beside)
    while True:
        reached = least * (2.0 - least)
        centre = 2.0 / (1.0 + reached)
        least = centre * reached
        ahead_parts = split(ahead)
        if guess is None:
            guess = (centre * start) * (2.0 * identity - ahead)
        else:
            guess = centre * (2.0 * guess - dot_three(split(guess), ahead_parts))
        if beside:
            beside.pop(0)()
        if 1.0 - least < 1e-3:
            break
        ahead = centre * (2.0 * ahead - dot_three(ahead_parts, ahead_parts))
    for work in beside:
        work()
    error = identity - dot(matrix, guess, precision=HIGHEST)
    return guess + dot_three(split(guess), split(error))


def slot_list(slots):
    return [slot for slot in range(slots) if slot != 1]


def mirrored(index, size):
    bits = size.bit_length() - 1
    return sum(((index >> bit) & 1) << (bits - 1 - bit) for bit in range(bits))


def covariance(first, second, alive, same):
    points = second.shape[1]
    rows_at_once = 64
    parts = []
    for start in range(0, points, rows_at_once):
        down = first[start : start + rows_at_once]
        total = None
        for k in range(3):
            offset = down[:, k : k + 1] - second[k : k + 1, :]
            total = offset * offset if total is None else total + offset * offset
        scaled = jnp.sqrt(total)
        value = (1.0 + scaled) * jnp.exp(-scaled) * alive
        if same:
            row = lax.broadcasted_iota(jnp.int32, value.shape, 0) + start
            column = lax.broadcasted_iota(jnp.int32, value.shape, 1)
            value = value + jnp.where(row == column, NUGGET * alive + (1.0 - alive), 0.0)
        parts.append(value)
    return jnp.concatenate(parts, axis=0)


def scaled_places(entry, fields):
    return entry[fields:] * (SQRT_THREE / SCALE_LENGTH)


def live_of(index):
    return (index >= 0).astype(F32)


def pack_kernel(sizes, locations, observed, packed):
    fields = sizes[0]
    packed[...] = jnp.zeros_like(packed)
    packed[:fields] = observed[0]
    packed[fields : fields + 3] = locations[0]


def factor_kernel(sizes, nbr, me, before, table, mine, noise, part, back_out, last_out, blocks):
    fields, points, coarse, slots = sizes
    used = slot_list(slots)
    own = len(used)
    ids = [nbr[0, slot] for slot in used] + [me[0]]
    here = lax.rem(me[0], coarse)
    entries = [before[0]]
    entries += [table[mirrored(jnp.maximum(index, 0) ^ here, coarse)] for index in ids[1:own]]
    entries += [mine[...]]
    live = [live_of(index) for index in ids]
    values = [entry[:fields] * alive for entry, alive in zip(entries, live)]
    places = [scaled_places(entry, fields) for entry in entries]
    turned = [jnp.transpose(place) for place in places]
    halves, lower, back = {}, {}, {}

    def build(i, j):
        blocks[i, j] = covariance(turned[i], places[j], live[i] * live[j], i == j)

    def parts_of(i, j):
        if (i, j) not in halves:
            halves[i, j] = split(blocks[i, j])
        return halves[i, j]

    def multiply(i, k, middle):
        lower[i, k] = dot(blocks[i, k], middle, precision=HIGHEST)

    def update(i, j, k):
        blocks[i, j] = blocks[i, j] - dot_three(split(lower[i, k]), parts_of(j, k), NT)

    def go_back(k):
        total = lower[own, k]
        for j in range(k + 1, own):
            total = total - dot_three(split(back[j]), split(lower[j, k]))
        back[k] = total

    build(0, 0)
    later = [functools.partial(build, i, j) for j in range(own + 1) for i in range(j, own + 1) if i > 0]
    for k in range(own):
        middle = inverse(blocks[k, k], later)
        for i in range(k + 1, own + 1):
            multiply(i, k, middle)
        update(k + 1, k + 1, k)
        later = [
            functools.partial(update, i, j, k)
            for j in range(k + 1, own + 1)
            for i in range(j, own + 1)
            if (i, j) != (k + 1, k + 1)
        ]
    last = inverse(blocks[own, own], [functools.partial(go_back, k) for k in range(own - 1, -1, -1)])
    for k in range(own):
        back_out[:, k * points : (k + 1) * points] = back[k]
    last_out[...] = last

    middle, spread, slot_parts = apply_block(values, back, last)
    own_part = spread + noise[0] * values[own]
    part[...] = jnp.zeros_like(part)
    product = jnp.sum(middle * spread + noise[0] * values[own] * values[own], axis=1, keepdims=True)
    square = jnp.sum(values[own] * values[own], axis=1, keepdims=True)
    part[coarse] = in_lanes([product, square], (fields, points))
    part[coarse + 1] = own_part
    part[coarse + 2] = slot_parts[0]
    for index, value in zip(ids, slot_parts + [own_part]):

        @pl.when((index >= 0) & (index < coarse))
        def _(index=index, value=value):
            part[index] = part[index] + value


def in_lanes(columns, shape):
    lane = lax.broadcasted_iota(jnp.int32, shape, 1)
    total = jnp.zeros(shape, F32)
    for at, column in enumerate(columns):
        total = jnp.where(lane == at, column, total)
    return total


def apply_block(values, back, last):
    own = len(values) - 1
    middle = values[own]
    for k in range(own):
        middle = middle - dot_three(split(values[k]), split(back[k]), NT)
    spread = dot_three(split(middle), split(last))
    spread_parts = split(spread)
    slot_parts = [-dot_three(spread_parts, split(back[k])) for k in range(own)]
    return middle, spread, slot_parts


def step_kernel(
    sizes, nbr, me, before, table, mine, noise, part, summed, shifted, back, last, sends, image_out, residual_out, ratio_out
):
    fields, points, coarse, slots = sizes
    used = slot_list(slots)
    own = len(used)
    ids = [nbr[0, slot] for slot in used] + [me[0]]
    here = lax.rem(me[0], coarse)
    product = summed[coarse][:, 0:1]
    norm_now = summed[coarse][:, 1:2]
    alpha = norm_now / product
    values = []
    for at, index in enumerate(ids):
        image = summed[jnp.clip(index, 0, coarse - 1)]
        if at == 0:
            observed = before[0, :fields]
            image = jnp.where(index < coarse, image, shifted[0] + part[coarse + 2])
        elif at == own:
            observed = mine[:fields]
            image = jnp.where(index < coarse, image, part[coarse + 1] + shifted[1])
        else:
            observed = table[mirrored(jnp.maximum(index, 0) ^ here, coarse)][:fields]
        values.append((observed - alpha * image) * live_of(index))
    back_parts = {k: back[:, k * points : (k + 1) * points] for k in range(own)}
    middle, spread, slot_parts = apply_block(values, back_parts, last[...])
    residual = values[own]
    inner = jnp.sum(middle * spread + noise[0] * residual * residual, axis=1, keepdims=True)
    cross = jnp.sum(residual * image, axis=1, keepdims=True)
    square = jnp.sum(residual * residual, axis=1, keepdims=True)
    sends[...] = jnp.zeros_like(sends)
    sends[coarse] = in_lanes([inner, cross, square], (fields, points))
    sends[coarse + 1] = slot_parts[0]
    for index, value in zip(ids[1:own], slot_parts[1:]):

        @pl.when(index >= 0)
        def _(index=index, value=value):
            place = mirrored(index ^ here, coarse)
            sends[place] = sends[place] + value

    image_out[0] = image
    image_out[1] = spread + noise[0] * residual
    residual_out[...] = residual
    ratio_out[...] = in_lanes([alpha, norm_now, product], (fields, LANES))


def finish_kernel(sizes, me, received, shifted, images, residual, ratios, mine, solution_out, residual_out):
    fields, points, coarse, slots = sizes
    owner = (me[0] < coarse).astype(F32)
    spread = images[1] + shifted[0] + owner * received[0]
    scalars = received[1]
    alpha, norm_first, product_first = ratios[:, 0:1], ratios[:, 1:2], ratios[:, 2:3]
    inner, cross, norm_now = scalars[:, 0:1], scalars[:, 1:2], scalars[:, 2:3]
    beta = norm_now / norm_first
    product = inner + beta * (2.0 * cross + beta * product_first)
    step = norm_now / product
    observed = mine[:fields]
    direction = residual[...] + beta * observed
    solution_out[0] = alpha * observed + step * direction
    residual_out[0] = residual[...] - step * (spread + beta * images[0])


def call(kernel, sizes, outs, in_spaces, scratch=()):
    return pl.pallas_call(
        functools.partial(kernel, sizes),
        out_shape=[jax.ShapeDtypeStruct(shape, F32) for shape in outs],
        in_specs=[pl.BlockSpec(memory_space=space) for space in in_spaces],
        out_specs=[pl.BlockSpec(memory_space=pltpu.VMEM)] * len(outs),
        scratch_shapes=list(scratch),
        compiler_params=pltpu.CompilerParams(vmem_limit_bytes=VMEM_LIMIT),
    )


def powers(size):
    assert size & (size - 1) == 0
    return [1 << bit for bit in range(size.bit_length() - 1)]


def swapped(value, axis, reach):
    return lax.ppermute(value, axis, [(at, at ^ reach) for at in range(lax.axis_size(axis))])


def exchanges():
    steps, bit = [], 0
    for axis in AXES[::-1]:
        for reach in powers(lax.axis_size(axis)):
            steps.append((axis, reach, bit))
            bit += 1
    return steps


def carry(shifted, ends, got, me, bit, kinds):
    low, upper = me & ((1 << bit) - 1), ((me >> bit) & 1) == 1
    new_shifted, new_ends = [], []
    for at, kind in enumerate(kinds):
        if kind == 1:
            takes, keeps = upper & (low == 0), upper
        else:
            takes, keeps = ~upper & (low == (1 << bit) - 1), ~upper
        new_shifted.append(jnp.where(takes, got[at], shifted[at]))
        new_ends.append(jnp.where(keeps, ends[at], got[at]))
    return jnp.stack(new_shifted), jnp.stack(new_ends)


def local(locations, neighbours, observations, noise_prec):
    blocks, _, points = locations.shape
    fields = observations.shape[1]
    slots = neighbours.shape[1]
    assert blocks == 1
    coarse = lax.axis_size("dev")
    sizes = (fields, points, coarse, slots)
    depth = len(slot_list(slots)) * points
    me = lax.axis_index(AXES).astype(jnp.int32)
    group = lax.axis_index("grp")
    smem, vmem = pltpu.SMEM, pltpu.VMEM
    square, tile = (points, points), (fields, points)
    steps = exchanges()

    (mine,) = call(pack_kernel, sizes, [(2 * fields, points)], [vmem, vmem])(locations, observations)
    before, table = mine[None], mine[None]
    for axis, reach, bit in steps[::-1]:
        got = swapped(jnp.concatenate([table, before], axis=0), axis, reach)
        low = (1 << bit) - 1
        before = jnp.where((me & low) == low, got[-1:], before)
        if axis == "grp":
            table = jnp.where((group & reach) != 0, got[:-1], table)
        else:
            table = jnp.concatenate([table, got[:-1]], axis=0)
    at = me.reshape(1)
    part, back, last = call(
        factor_kernel,
        sizes,
        [(coarse + 3,) + tile, (points, depth), square],
        [smem, smem] + [vmem] * 4,
        [pltpu.VMEM((slots, slots) + square, F32)],
    )(neighbours, at, before, table, mine, noise_prec)

    summed, ends, shifted = part[:-2], part[-2:], jnp.zeros_like(part[-2:])
    for axis, reach, bit in steps:
        got = swapped(jnp.concatenate([summed, ends], axis=0), axis, reach)
        summed = summed + got[:-2]
        shifted, ends = carry(shifted, ends, got[-2:], me, bit, (1, -1))
    sends, images, residual, ratios = call(
        step_kernel,
        sizes,
        [(coarse + 2,) + tile, (2,) + tile, tile, (fields, LANES)],
        [smem, smem] + [vmem] * 9,
    )(neighbours, at, before, table, mine, noise_prec, part, summed, shifted, back, last)

    summed, ends, shifted = sends[:-1], sends[-1:], jnp.zeros_like(sends[-1:])
    for axis, reach, bit in steps:
        kept = (summed.shape[0] - 1) // 2 if axis == "dev" else 0
        got = swapped(jnp.concatenate([summed[kept:], ends], axis=0), axis, reach)
        if axis == "dev":
            summed = jnp.concatenate([summed[:kept], summed[-1:]], axis=0)
        summed = summed + got[:-1]
        shifted, ends = carry(shifted, ends, got[-1:], me, bit, (-1,))
    return tuple(
        call(finish_kernel, sizes, [observations.shape] * 2, [smem] + [vmem] * 6)(
            at, summed, shifted, images, residual, ratios, mine
        )
    )


def solution(mesh):
    placed = (
        P(AXES, None, None),
        P(AXES, None),
        P(AXES, None, None),
        P(AXES, None, None),
    )
    return jax.shard_map(
        local,
        mesh=mesh,
        in_specs=placed,
        out_specs=(P(AXES, None, None), P(AXES, None, None)),
        check_vma=False,
    )
```

time: 93.4 us -> 85.4 us (0.914)
  starting transfers between devices: 37.9 us -> 24 us
  waiting for transfers between devices: 27.9 us -> 35.7 us
  Pallas kernels: 23.5 us -> 22.2 us
    ppermute x13 -> x15, waiting for transfers between devices: 24 us -> 35.7 us  [swapped(): lax.ppermute(value, axis, [(at, at ^ reach) for at in range(lax.axis_size...]
    ppermute x6 -> x0, starting transfers between devices: 11.2 us -> none  [the longest x2 6.11 us: local(): got = lax.ppermute(first, 'grp', [(at, at + reach) for at in range(reach)])]
    ppermute x6 -> x0, waiting for transfers between devices: 3.91 us -> none  [the longest x2 2.83 us: local(): got = lax.ppermute(first, 'grp', [(at, at + reach) for at in range(reach)])]
    ppermute x13 -> x15, starting transfers between devices: 26.6 us -> 24 us  [swapped(): lax.ppermute(value, axis, [(at, at ^ reach) for at in range(lax.axis_size...]
    pallas_call x4 -> x3, Pallas kernels: 23.5 us -> 22.2 us  [the longest x1 19.5 us: local(): call(factor_kernel, sizes, [(coarse + 3,) + tile, (points, depth), square...]
    unnamed x10 -> x7, local copies, waits for them, and re-layouts: 2.74 us -> 2.06 us
  transfers between devices with their start and end apart: 19 -> 15, of which waited for: 16 -> 15; matrix products, arithmetic and copies ran while one was open for 0% -> 0% of each run, Pallas kernels for 5% -> 0%
where the time goes in v3:
time: 85.4 us; the launch traced here: 85.1 us
  waiting for transfers between devices  35.7 us (42%)
  starting transfers between devices  24 us (28%)
  Pallas kernels  22.2 us (26%)
  local copies, waits for them, and re-layouts  2.1 us (2%)
  between operations  0.87 us (1%)
    ppermute x15, waiting for transfers between devices, swapped(): lax.ppermute(value, axis, [(at, at ^ reach) for at in range(lax.axis_size...  35.7 us
    ppermute x15, starting transfers between devices, swapped(): lax.ppermute(value, axis, [(at, at ^ reach) for at in range(lax.axis_size...  24 us
    pallas_call x1, Pallas kernels, local(): call(factor_kernel, sizes, [(coarse + 3,) + tile, (points, depth), square...  19.5 us
    unnamed x7, local copies, waits for them, and re-layouts  2.06 us
  transfers between devices with their start and end apart: 15, of which 15 were waited for; matrix products, arithmetic and copies ran while one was open for 0% of the time, Pallas kernels for 0%

profile of v3, /device:TPU:0, one launch (start us, length us, event | category | flops | bytes accessed | tf_op | source)
XLA Modules:
  0.0 85.1 jit_solution(15345347724635183849)
XLA Ops:
  0.6 0.7 copy.6.locations
  1.3 0.0 copy-start.1
  1.3 0.7 copy-done.1
  2.0 3.0 %collective-permute-start = (f32[2,16,256]{2,1,0:T(8,128)S(1)}, f32[2,16,256]{2,1,0:T(8,128)S(1)}, u32[]{:S(2)}, u32[]{:S(2)}) collective-permute-start(f32[2,16,256]{2,1,0:T(8,128)S(1)} %pad_maximum_fusion.7), channel_id=1, source_target_pairs={{0,16},{8,24},{16,0},{24,8},{1,17},{9,25},{17,1},{25,9},{2,18},{10... | collective-permute-start | bytes 98312 | tf_op jit(solution)/shard_map/ppermute | solution.py:275
  5.0 1.9 %collective-permute-done = f32[2,16,256]{2,1,0:T(8,128)S(1)} collective-permute-done((f32[2,16,256]{2,1,0:T(8,128)S(1)}, f32[2,16,256]{2,1,0:T(8,128)S(1)}, u32[]{:S(2)}, u32[]{:S(2)}) %collective-permute-start) | collective-permute-done | bytes 32800 | tf_op jit(solution)/shard_map/ppermute | solution.py:275
  6.9 2.1 %collective-permute-start.1 = (f32[2,16,256]{2,1,0:T(8,128)S(1)}, f32[2,16,256]{2,1,0:T(8,128)S(1)}, u32[]{:S(2)}, u32[]{:S(2)}) collective-permute-start(f32[2,16,256]{2,1,0:T(8,128)S(1)} %pad_maximum_fusion.8), channel_id=1, source_target_pairs={{0,8},{8,0},{16,24},{24,16},{1,9},{9,1},{17,25},{25,17},{2,10},{10... | collective-permute-start | bytes 98312 | tf_op jit(solution)/shard_map/ppermute | solution.py:275
  9.0 1.9 %collective-permute-done.1 = f32[2,16,256]{2,1,0:T(8,128)S(1)} collective-permute-done((f32[2,16,256]{2,1,0:T(8,128)S(1)}, f32[2,16,256]{2,1,0:T(8,128)S(1)}, u32[]{:S(2)}, u32[]{:S(2)}) %collective-permute-start.1) | collective-permute-done | bytes 32800 | tf_op jit(solution)/shard_map/ppermute | solution.py:275
  10.9 3.2 %collective-permute-start.2 = (f32[2,16,256]{2,1,0:T(8,128)S(1)}, f32[2,16,256]{2,1,0:T(8,128)S(1)}, u32[]{:S(2)}, u32[]{:S(2)}) collective-permute-start(f32[2,16,256]{2,1,0:T(8,128)S(1)} %pad_maximum_fusion.9), channel_id=1, source_target_pairs={{0,4},{1,5},{2,6},{3,7},{4,0},{5,1},{6,2},{7,3},{8,12},{9,13},{10,... | collective-permute-start | bytes 98312 | tf_op jit(solution)/shard_map/ppermute | solution.py:275
  14.0 2.0 %collective-permute-done.2 = f32[2,16,256]{2,1,0:T(8,128)S(1)} collective-permute-done((f32[2,16,256]{2,1,0:T(8,128)S(1)}, f32[2,16,256]{2,1,0:T(8,128)S(1)}, u32[]{:S(2)}, u32[]{:S(2)}) %collective-permute-start.2) | collective-permute-done | bytes 32800 | tf_op jit(solution)/shard_map/ppermute | solution.py:275
  16.1 1.9 %collective-permute-start.3 = (f32[3,16,256]{2,1,0:T(8,128)S(1)}, f32[3,16,256]{2,1,0:T(8,128)S(1)}, u32[]{:S(2)}, u32[]{:S(2)}) collective-permute-start(f32[3,16,256]{2,1,0:T(8,128)S(1)} %pad_maximum_fusion.6), channel_id=1, source_target_pairs={{0,2},{1,3},{2,0},{3,1},{4,6},{5,7},{6,4},{7,5},{8,10},{9,11},{10,... | collective-permute-start | bytes 147464 | tf_op jit(solution)/shard_map/ppermute | solution.py:275
  17.9 2.3 %collective-permute-done.3 = f32[3,16,256]{2,1,0:T(8,128)S(1)} collective-permute-done((f32[3,16,256]{2,1,0:T(8,128)S(1)}, f32[3,16,256]{2,1,0:T(8,128)S(1)}, u32[]{:S(2)}, u32[]{:S(2)}) %collective-permute-start.3) | collective-permute-done | bytes 49184 | tf_op jit(solution)/shard_map/ppermute | solution.py:275
  20.2 0.1 collective-permute-start.4
  20.3 1.3 %collective-permute-done.4 = f32[5,16,256]{2,1,0:T(8,128)S(1)} collective-permute-done((f32[5,16,256]{2,1,0:T(8,128)S(1)}, f32[5,16,256]{2,1,0:T(8,128)S(1)}, u32[]{:S(2)}, u32[]{:S(2)}) %collective-permute-start.4) | collective-permute-done | bytes 81952 | tf_op jit(solution)/shard_map/ppermute | solution.py:275
  21.6 0.0 copy-start
  21.6 0.0 copy-start.2
  21.6 0.7 copy-done
  22.3 0.0 copy-done.2
  22.3 19.5 %shard_map.60 = (f32[11,8,256]{2,1,0:T(8,128)S(1)}, f32[256,768]{1,0:T(8,128)S(1)}, f32[256,256]{1,0:T(8,128)S(1)}) custom-call(s32[1,4]{1,0:T(1,128)S(1)} %copy-done.2, s32[1]{0:T(128)} %bitcast.me, f32[1,16,256]{2,1,0:T(8,128)S(1)} %slice.229.before, f32[8,16,256]{2,1,0:T(8,128)S(1)} %pad_maximum_fusion.table, f32[16,256]{1,0:T(8,128)S(1)} %shard_map.59.mine, ...), custom_call_target="tpu_custom_call" | custom-call | tf_op jit(solution)/shard_map/pallas_call | solution.py:325
  41.8 0.2 collective-permute-start.5
  42.0 1.1 %collective-permute-done.5 = f32[11,8,256]{2,1,0:T(8,128)S(1)} collective-permute-done((f32[11,8,256]{2,1,0:T(8,128)S(1)}, f32[11,8,256]{2,1,0:T(8,128)S(1)}, u32[]{:S(2)}, u32[]{:S(2)}) %collective-permute-start.5) | collective-permute-done | bytes 90144 | tf_op jit(solution)/shard_map/ppermute | solution.py:275
  43.1 1.9 %collective-permute-start.6 = (f32[11,8,256]{2,1,0:T(8,128)S(1)}, f32[11,8,256]{2,1,0:T(8,128)S(1)}, u32[]{:S(2)}, u32[]{:S(2)}) collective-permute-start(f32[11,8,256]{2,1,0:T(8,128)S(1)} %pad_maximum_fusion.1), channel_id=1, source_target_pairs={{0,2},{1,3},{2,0},{3,1},{4,6},{5,7},{6,4},{7,5},{8,10},{9,11},{10,... | collective-permute-start | bytes 270344 | tf_op jit(solution)/shard_map/ppermute | solution.py:275
  45.0 2.9 %collective-permute-done.6 = f32[11,8,256]{2,1,0:T(8,128)S(1)} collective-permute-done((f32[11,8,256]{2,1,0:T(8,128)S(1)}, f32[11,8,256]{2,1,0:T(8,128)S(1)}, u32[]{:S(2)}, u32[]{:S(2)}) %collective-permute-start.6) | collective-permute-done | bytes 90144 | tf_op jit(solution)/shard_map/ppermute | solution.py:275
  48.0 2.9 %collective-permute-start.7 = (f32[11,8,256]{2,1,0:T(8,128)S(1)}, f32[11,8,256]{2,1,0:T(8,128)S(1)}, u32[]{:S(2)}, u32[]{:S(2)}) collective-permute-start(f32[11,8,256]{2,1,0:T(8,128)S(1)} %pad_maximum_fusion.2), channel_id=1, source_target_pairs={{0,4},{1,5},{2,6},{3,7},{4,0},{5,1},{6,2},{7,3},{8,12},{9,13},{10,... | collective-permute-start | bytes 270344 | tf_op jit(solution)/shard_map/ppermute | solution.py:275
  50.9 4.3 %collective-permute-done.7 = f32[11,8,256]{2,1,0:T(8,128)S(1)} collective-permute-done((f32[11,8,256]{2,1,0:T(8,128)S(1)}, f32[11,8,256]{2,1,0:T(8,128)S(1)}, u32[]{:S(2)}, u32[]{:S(2)}) %collective-permute-start.7) | collective-permute-done | bytes 90144 | tf_op jit(solution)/shard_map/ppermute | solution.py:275
  55.2 1.6 %collective-permute-start.8 = (f32[11,8,256]{2,1,0:T(8,128)S(1)}, f32[11,8,256]{2,1,0:T(8,128)S(1)}, u32[]{:S(2)}, u32[]{:S(2)}) collective-permute-start(f32[11,8,256]{2,1,0:T(8,128)S(1)} %pad_maximum_fusion.3), channel_id=1, source_target_pairs={{0,8},{8,0},{16,24},{24,16},{1,9},{9,1},{17,25},{25,17},{2,10},{10... | collective-permute-start | bytes 270344 | tf_op jit(solution)/shard_map/ppermute | solution.py:275
  56.7 3.0 %collective-permute-done.8 = f32[11,8,256]{2,1,0:T(8,128)S(1)} collective-permute-done((f32[11,8,256]{2,1,0:T(8,128)S(1)}, f32[11,8,256]{2,1,0:T(8,128)S(1)}, u32[]{:S(2)}, u32[]{:S(2)}) %collective-permute-start.8) | collective-permute-done | bytes 90144 | tf_op jit(solution)/shard_map/ppermute | solution.py:275
  59.8 1.6 %collective-permute-start.9 = (f32[11,8,256]{2,1,0:T(8,128)S(1)}, f32[11,8,256]{2,1,0:T(8,128)S(1)}, u32[]{:S(2)}, u32[]{:S(2)}) collective-permute-start(f32[11,8,256]{2,1,0:T(8,128)S(1)} %pad_maximum_fusion.4), channel_id=1, source_target_pairs={{0,16},{8,24},{16,0},{24,8},{1,17},{9,25},{17,1},{25,9},{2,18},{10... | collective-permute-start | bytes 270344 | tf_op jit(solution)/shard_map/ppermute | solution.py:275
  61.4 3.0 %collective-permute-done.9 = f32[11,8,256]{2,1,0:T(8,128)S(1)} collective-permute-done((f32[11,8,256]{2,1,0:T(8,128)S(1)}, f32[11,8,256]{2,1,0:T(8,128)S(1)}, u32[]{:S(2)}, u32[]{:S(2)}) %collective-permute-start.9) | collective-permute-done | bytes 90144 | tf_op jit(solution)/shard_map/ppermute | solution.py:275
  64.5 1.7 %shard_map.61 = (f32[10,8,256]{2,1,0:T(8,128)S(1)}, f32[2,8,256]{2,1,0:T(8,128)S(1)}, f32[8,256]{1,0:T(8,128)S(1)}, f32[8,128]{1,0:T(8,128)S(1)}) custom-call(s32[1,4]{1,0:T(1,128)S(1)} %copy-done.2, s32[1]{0:T(128)} %bitcast.me, f32[1,16,256]{2,1,0:T(8,128)S(1)} %slice.229.before, f32[8,16,256]{2,1,0:T(8,128)S(1)} %pad_maximum_fusion.table, ...), custom_call_target="tpu_custom_call" | custom-call | tf_op jit(solution)/shard_map/pallas_call | solution.py:338
  66.1 0.0 collective-permute-start.10
  66.2 1.2 %collective-permute-done.10 = f32[6,8,256]{2,1,0:T(8,128)S(1)} collective-permute-done((f32[6,8,256]{2,1,0:T(8,128)S(1)}, f32[6,8,256]{2,1,0:T(8,128)S(1)}, u32[]{:S(2)}, u32[]{:S(2)}) %collective-permute-start.10) | collective-permute-done | bytes 49184 | tf_op jit(solution)/shard_map/ppermute | solution.py:275
  67.5 0.6 collective-permute-start.11
  68.1 3.3 %collective-permute-done.11 = f32[4,8,256]{2,1,0:T(8,128)S(1)} collective-permute-done((f32[4,8,256]{2,1,0:T(8,128)S(1)}, f32[4,8,256]{2,1,0:T(8,128)S(1)}, u32[]{:S(2)}, u32[]{:S(2)}) %collective-permute-start.11) | collective-permute-done | bytes 32800 | tf_op jit(solution)/shard_map/ppermute | solution.py:275
  71.5 2.0 %collective-permute-start.12 = (f32[3,8,256]{2,1,0:T(8,128)S(1)}, f32[3,8,256]{2,1,0:T(8,128)S(1)}, u32[]{:S(2)}, u32[]{:S(2)}) collective-permute-start(f32[3,8,256]{2,1,0:T(8,128)S(1)} %pad_maximum_fusion.11), channel_id=1, source_target_pairs={{0,4},{1,5},{2,6},{3,7},{4,0},{5,1},{6,2},{7,3},{8,12},{9,13},{10,... | collective-permute-start | bytes 73736 | tf_op jit(solution)/shard_map/ppermute | solution.py:275
  73.5 2.8 %collective-permute-done.12 = f32[3,8,256]{2,1,0:T(8,128)S(1)} collective-permute-done((f32[3,8,256]{2,1,0:T(8,128)S(1)}, f32[3,8,256]{2,1,0:T(8,128)S(1)}, u32[]{:S(2)}, u32[]{:S(2)}) %collective-permute-start.12) | collective-permute-done | bytes 24608 | tf_op jit(solution)/shard_map/ppermute | solution.py:275
  76.3 1.6 %collective-permute-start.13 = (f32[3,8,256]{2,1,0:T(8,128)S(1)}, f32[3,8,256]{2,1,0:T(8,128)S(1)}, u32[]{:S(2)}, u32[]{:S(2)}) collective-permute-start(f32[3,8,256]{2,1,0:T(8,128)S(1)} %pad_maximum_fusion.12), channel_id=1, source_target_pairs={{0,8},{8,0},{16,24},{24,16},{1,9},{9,1},{17,25},{25,17},{2,10},{10... | collective-permute-start | bytes 73736 | tf_op jit(solution)/shard_map/ppermute | solution.py:275
  77.8 2.3 %collective-permute-done.13 = f32[3,8,256]{2,1,0:T(8,128)S(1)} collective-permute-done((f32[3,8,256]{2,1,0:T(8,128)S(1)}, f32[3,8,256]{2,1,0:T(8,128)S(1)}, u32[]{:S(2)}, u32[]{:S(2)}) %collective-permute-start.13) | collective-permute-done | bytes 24608 | tf_op jit(solution)/shard_map/ppermute | solution.py:275
  80.2 1.6 %collective-permute-start.14 = (f32[3,8,256]{2,1,0:T(8,128)S(1)}, f32[3,8,256]{2,1,0:T(8,128)S(1)}, u32[]{:S(2)}, u32[]{:S(2)}) collective-permute-start(f32[3,8,256]{2,1,0:T(8,128)S(1)} %pad_maximum_fusion.13), channel_id=1, source_target_pairs={{0,16},{8,24},{16,0},{24,8},{1,17},{9,25},{17,1},{25,9},{2,18},{10... | collective-permute-start | bytes 73736 | tf_op jit(solution)/shard_map/ppermute | solution.py:275
  81.8 2.3 %collective-permute-done.14 = f32[3,8,256]{2,1,0:T(8,128)S(1)} collective-permute-done((f32[3,8,256]{2,1,0:T(8,128)S(1)}, f32[3,8,256]{2,1,0:T(8,128)S(1)}, u32[]{:S(2)}, u32[]{:S(2)}) %collective-permute-start.14) | collective-permute-done | bytes 24608 | tf_op jit(solution)/shard_map/ppermute | solution.py:275
  84.1 1.0 %shard_map.62 = (f32[1,8,256]{2,1,0:T(8,128)}, f32[1,8,256]{2,1,0:T(8,128)}) custom-call(s32[1]{0:T(128)} %bitcast.me, f32[2,8,256]{2,1,0:T(8,128)S(1)} %slice_add_fusion.7.received, f32[1,8,256]{2,1,0:T(8,128)S(1)} %slice_select_fusion.6.shifted, f32[2,8,256]{2,1,0:T(8,128)S(1)} %get-tuple-element.13.images, f32[8,256]{1,0:T(8,128)S(1)} %get-tuple-element.14.residual, ...), custom_call_target="tpu_custom_call" | custom-call | tf_op jit(solution)/shard_map/pallas_call | solution.py:354
  (51 shorter events, 0.3 us)
Async XLA Ops:
  1.3 0.7 copy-start.1
  2.0 4.9 %collective-permute-start = (f32[2,16,256]{2,1,0:T(8,128)S(1)}, f32[2,16,256]{2,1,0:T(8,128)S(1)}, u32[]{:S(2)}, u32[]{:S(2)}) collective-permute-start(f32[2,16,256]{2,1,0:T(8,128)S(1)} %pad_maximum_fusion.7), channel_id=1, source_target_pairs={{0,16},{8,24},{16,0},{24,8},{1,17},{9,25},{17,1},{25,9},{2,18},{10... | collective-permute-start | bytes 98312 | tf_op jit(solution)/shard_map/ppermute | solution.py:275
  6.9 4.0 %collective-permute-start.1 = (f32[2,16,256]{2,1,0:T(8,128)S(1)}, f32[2,16,256]{2,1,0:T(8,128)S(1)}, u32[]{:S(2)}, u32[]{:S(2)}) collective-permute-start(f32[2,16,256]{2,1,0:T(8,128)S(1)} %pad_maximum_fusion.8), channel_id=1, source_target_pairs={{0,8},{8,0},{16,24},{24,16},{1,9},{9,1},{17,25},{25,17},{2,10},{10... | collective-permute-start | bytes 98312 | tf_op jit(solution)/shard_map/ppermute | solution.py:275
  10.9 5.2 %collective-permute-start.2 = (f32[2,16,256]{2,1,0:T(8,128)S(1)}, f32[2,16,256]{2,1,0:T(8,128)S(1)}, u32[]{:S(2)}, u32[]{:S(2)}) collective-permute-start(f32[2,16,256]{2,1,0:T(8,128)S(1)} %pad_maximum_fusion.9), channel_id=1, source_target_pairs={{0,4},{1,5},{2,6},{3,7},{4,0},{5,1},{6,2},{7,3},{8,12},{9,13},{10,... | collective-permute-start | bytes 98312 | tf_op jit(solution)/shard_map/ppermute | solution.py:275
  16.1 4.2 %collective-permute-start.3 = (f32[3,16,256]{2,1,0:T(8,128)S(1)}, f32[3,16,256]{2,1,0:T(8,128)S(1)}, u32[]{:S(2)}, u32[]{:S(2)}) collective-permute-start(f32[3,16,256]{2,1,0:T(8,128)S(1)} %pad_maximum_fusion.6), channel_id=1, source_target_pairs={{0,2},{1,3},{2,0},{3,1},{4,6},{5,7},{6,4},{7,5},{8,10},{9,11},{10,... | collective-permute-start | bytes 147464 | tf_op jit(solution)/shard_map/ppermute | solution.py:275
  20.2 1.3 %collective-permute-start.4 = (f32[5,16,256]{2,1,0:T(8,128)S(1)}, f32[5,16,256]{2,1,0:T(8,128)S(1)}, u32[]{:S(2)}, u32[]{:S(2)}) collective-permute-start(f32[5,16,256]{2,1,0:T(8,128)S(1)} %pad_maximum_fusion.5), channel_id=1, source_target_pairs={{0,1},{1,0},{2,3},{3,2},{4,5},{5,4},{6,7},{7,6},{8,9},{9,8},{10,11... | collective-permute-start | bytes 245768 | tf_op jit(solution)/shard_map/ppermute | solution.py:275
  21.6 0.7 copy-start
  21.6 0.7 copy-start.2
  41.8 1.3 %collective-permute-start.5 = (f32[11,8,256]{2,1,0:T(8,128)S(1)}, f32[11,8,256]{2,1,0:T(8,128)S(1)}, u32[]{:S(2)}, u32[]{:S(2)}) collective-permute-start(f32[11,8,256]{2,1,0:T(8,128)S(1)} %get-tuple-element.9.part), channel_id=1, source_target_pairs={{0,1},{1,0},{2,3},{3,2},{4,5},{5,4},{6,7},{7,6},{8,9},{9,8},{10,11... | collective-permute-start | bytes 270344 | tf_op jit(solution)/shard_map/ppermute | solution.py:275
  43.1 4.8 %collective-permute-start.6 = (f32[11,8,256]{2,1,0:T(8,128)S(1)}, f32[11,8,256]{2,1,0:T(8,128)S(1)}, u32[]{:S(2)}, u32[]{:S(2)}) collective-permute-start(f32[11,8,256]{2,1,0:T(8,128)S(1)} %pad_maximum_fusion.1), channel_id=1, source_target_pairs={{0,2},{1,3},{2,0},{3,1},{4,6},{5,7},{6,4},{7,5},{8,10},{9,11},{10,... | collective-permute-start | bytes 270344 | tf_op jit(solution)/shard_map/ppermute | solution.py:275
  48.0 7.1 %collective-permute-start.7 = (f32[11,8,256]{2,1,0:T(8,128)S(1)}, f32[11,8,256]{2,1,0:T(8,128)S(1)}, u32[]{:S(2)}, u32[]{:S(2)}) collective-permute-start(f32[11,8,256]{2,1,0:T(8,128)S(1)} %pad_maximum_fusion.2), channel_id=1, source_target_pairs={{0,4},{1,5},{2,6},{3,7},{4,0},{5,1},{6,2},{7,3},{8,12},{9,13},{10,... | collective-permute-start | bytes 270344 | tf_op jit(solution)/shard_map/ppermute | solution.py:275
  55.2 4.6 %collective-permute-start.8 = (f32[11,8,256]{2,1,0:T(8,128)S(1)}, f32[11,8,256]{2,1,0:T(8,128)S(1)}, u32[]{:S(2)}, u32[]{:S(2)}) collective-permute-start(f32[11,8,256]{2,1,0:T(8,128)S(1)} %pad_maximum_fusion.3), channel_id=1, source_target_pairs={{0,8},{8,0},{16,24},{24,16},{1,9},{9,1},{17,25},{25,17},{2,10},{10... | collective-permute-start | bytes 270344 | tf_op jit(solution)/shard_map/ppermute | solution.py:275
  59.8 4.6 %collective-permute-start.9 = (f32[11,8,256]{2,1,0:T(8,128)S(1)}, f32[11,8,256]{2,1,0:T(8,128)S(1)}, u32[]{:S(2)}, u32[]{:S(2)}) collective-permute-start(f32[11,8,256]{2,1,0:T(8,128)S(1)} %pad_maximum_fusion.4), channel_id=1, source_target_pairs={{0,16},{8,24},{16,0},{24,8},{1,17},{9,25},{17,1},{25,9},{2,18},{10... | collective-permute-start | bytes 270344 | tf_op jit(solution)/shard_map/ppermute | solution.py:275
  66.1 1.3 %collective-permute-start.10 = (f32[6,8,256]{2,1,0:T(8,128)S(1)}, f32[6,8,256]{2,1,0:T(8,128)S(1)}, u32[]{:S(2)}, u32[]{:S(2)}) collective-permute-start(f32[6,8,256]{2,1,0:T(8,128)S(1)} %concatenate.72), channel_id=1, source_target_pairs={{0,1},{1,0},{2,3},{3,2},{4,5},{5,4},{6,7},{7,6},{8,9},{9,8},{10,11... | collective-permute-start | bytes 147464 | tf_op jit(solution)/shard_map/ppermute | solution.py:275
  67.5 4.0 %collective-permute-start.11 = (f32[4,8,256]{2,1,0:T(8,128)S(1)}, f32[4,8,256]{2,1,0:T(8,128)S(1)}, u32[]{:S(2)}, u32[]{:S(2)}) collective-permute-start(f32[4,8,256]{2,1,0:T(8,128)S(1)} %pad_maximum_fusion.10), channel_id=1, source_target_pairs={{0,2},{1,3},{2,0},{3,1},{4,6},{5,7},{6,4},{7,5},{8,10},{9,11},{10,... | collective-permute-start | bytes 98312 | tf_op jit(solution)/shard_map/ppermute | solution.py:275
  71.5 4.8 %collective-permute-start.12 = (f32[3,8,256]{2,1,0:T(8,128)S(1)}, f32[3,8,256]{2,1,0:T(8,128)S(1)}, u32[]{:S(2)}, u32[]{:S(2)}) collective-permute-start(f32[3,8,256]{2,1,0:T(8,128)S(1)} %pad_maximum_fusion.11), channel_id=1, source_target_pairs={{0,4},{1,5},{2,6},{3,7},{4,0},{5,1},{6,2},{7,3},{8,12},{9,13},{10,... | collective-permute-start | bytes 73736 | tf_op jit(solution)/shard_map/ppermute | solution.py:275
  76.3 3.9 %collective-permute-start.13 = (f32[3,8,256]{2,1,0:T(8,128)S(1)}, f32[3,8,256]{2,1,0:T(8,128)S(1)}, u32[]{:S(2)}, u32[]{:S(2)}) collective-permute-start(f32[3,8,256]{2,1,0:T(8,128)S(1)} %pad_maximum_fusion.12), channel_id=1, source_target_pairs={{0,8},{8,0},{16,24},{24,16},{1,9},{9,1},{17,25},{25,17},{2,10},{10... | collective-permute-start | bytes 73736 | tf_op jit(solution)/shard_map/ppermute | solution.py:275
  80.2 3.9 %collective-permute-start.14 = (f32[3,8,256]{2,1,0:T(8,128)S(1)}, f32[3,8,256]{2,1,0:T(8,128)S(1)}, u32[]{:S(2)}, u32[]{:S(2)}) collective-permute-start(f32[3,8,256]{2,1,0:T(8,128)S(1)} %pad_maximum_fusion.13), channel_id=1, source_target_pairs={{0,16},{8,24},{16,0},{24,8},{1,17},{9,25},{17,1},{25,9},{2,18},{10... | collective-permute-start | bytes 73736 | tf_op jit(solution)/shard_map/ppermute | solution.py:275

commit v4 on v3

--- a/solution.py
+++ b/solution.py
@@ -18,6 +18,8 @@
 NT = (((1,), (1,)), ((), ()))
 AXES = ("grp", "dev")
 VMEM_LIMIT = 48 * 1024 * 1024
+CLOSE = 2e-3
+ALWAYS = 3
 
 
 def split(value):
@@ -33,34 +35,58 @@
     return dot(left[0], right[0], dims) + (dot(left[0], right[1], dims) + dot(left[1], right[0], dims))
 
 
-def inverse(matrix, beside=()):
+def split_fine(value):
+    high = value.astype(jnp.bfloat16)
+    rest = value - high.astype(F32)
+    middle = rest.astype(jnp.bfloat16)
+    return high, middle, (rest - middle.astype(F32)).astype(jnp.bfloat16)
+
+
+def dot_six(left, right, dims=NN):
+    small = dot(left[1], right[1], dims) + (dot(left[0], right[2], dims) + dot(left[2], right[0], dims))
+    return dot(left[0], right[0], dims) + ((dot(left[0], right[1], dims) + dot(left[1], right[0], dims)) + small)
+
+
+def newton_levels(order):
+    least = 1.0 - CLOSE
+    levels = [(1.0, 1.0 / least - NUGGET)]
+    while levels[-1][1] < order + NUGGET:
+        reached = least / (2.0 - least)
+        least = 1.0 - math.sqrt(1.0 - reached)
+        levels.append((2.0 / (1.0 + reached), 1.0 / least - NUGGET))
+    return levels
+
+
+def inverse(matrix, ahead, guess):
     order = matrix.shape[0]
     rows = lax.broadcasted_iota(jnp.int32, (order, order), 0)
     columns = lax.broadcasted_iota(jnp.int32, (order, order), 1)
     identity = (rows == columns).astype(F32)
-    start = 2.0 / (2.0 * NUGGET + order)
-    least = start * NUGGET
-    ahead = start * matrix
-    guess = None
-    beside = list(beside)
-    while True:
-        reached = least * (2.0 - least)
-        centre = 2.0 / (1.0 + reached)
-        least = centre * reached
-        ahead_parts = split(ahead)
-        if guess is None:
-            guess = (centre * start) * (2.0 * identity - ahead)
-        else:
-            guess = centre * (2.0 * guess - dot_three(split(guess), ahead_parts))
-        if beside:
-            beside.pop(0)()
-        if 1.0 - least < 1e-3:
-            break
-        ahead = centre * (2.0 * ahead - dot_three(ahead_parts, ahead_parts))
-    for work in beside:
-        work()
-    error = identity - dot(matrix, guess, precision=HIGHEST)
-    return guess + dot_three(split(guess), split(error))
+    levels = newton_levels(order)
+    always = min(ALWAYS, len(levels) - 1)
+    bound = jnp.minimum(jnp.max(jnp.sum(jnp.abs(matrix), axis=0)), order + NUGGET)
+    start = 2.0 / (NUGGET + levels[always][1])
+    for level in range(always + 1, len(levels)):
+        start = jnp.where(bound > levels[level - 1][1], 2.0 / (NUGGET + levels[level][1]), start)
+    ahead[...] = start * matrix
+    guess[...] = start * identity
+
+    def advance(scale, now, held, only_guess=False):
+        now_parts = split(now)
+        new_held = scale * (2.0 * held - dot_three(split(held), now_parts))
+        return (None if only_guess else scale * (2.0 * now - dot_three(now_parts, now_parts))), new_held
+
+    for level in range(len(levels) - 1, always, -1):
+
+        @pl.when(bound > levels[level - 1][1])
+        def _(scale=levels[level][0]):
+            ahead[...], guess[...] = advance(scale, ahead[...], guess[...])
+
+    now, held = ahead[...], guess[...]
+    for level in range(always, 0, -1):
+        now, held = advance(levels[level][0], now, held, level == 1)
+    error = identity - dot_six(split_fine(matrix), split_fine(held))
+    return held + dot_three(split(held), split(error))
 
 
 def slot_list(slots):
@@ -107,7 +133,7 @@
     packed[fields : fields + 3] = locations[0]
 
 
-def factor_kernel(sizes, nbr, me, before, table, mine, noise, part, back_out, last_out, blocks):
+def factor_kernel(sizes, nbr, me, before, table, mine, noise, part, back_out, last_out, columns, lower, ahead, guess):
     fields, points, coarse, slots = sizes
     used = slot_list(slots)
     own = len(used)
@@ -120,45 +146,33 @@
     values = [entry[:fields] * alive for entry, alive in zip(entries, live)]
     places = [scaled_places(entry, fields) for entry in entries]
     turned = [jnp.transpose(place) for place in places]
-    halves, lower, back = {}, {}, {}
-
-    def build(i, j):
-        blocks[i, j] = covariance(turned[i], places[j], live[i] * live[j], i == j)
-
-    def parts_of(i, j):
-        if (i, j) not in halves:
-            halves[i, j] = split(blocks[i, j])
-        return halves[i, j]
-
-    def multiply(i, k, middle):
-        lower[i, k] = dot(blocks[i, k], middle, precision=HIGHEST)
-
-    def update(i, j, k):
-        blocks[i, j] = blocks[i, j] - dot_three(split(lower[i, k]), parts_of(j, k), NT)
-
-    def go_back(k):
-        total = lower[own, k]
-        for j in range(k + 1, own):
-            total = total - dot_three(split(back[j]), split(lower[j, k]))
-        back[k] = total
-
-    build(0, 0)
-    later = [functools.partial(build, i, j) for j in range(own + 1) for i in range(j, own + 1) if i > 0]
+
+    def at(i, end=None):
+        return pl.ds(i * points, ((i + 1 if end is None else end) - i) * points)
+
+    for j in range(own + 1):
+        for i in range(j, own + 1):
+            columns[j, at(i)] = covariance(turned[i], places[j], live[i] * live[j], i == j)
     for k in range(own):
-        middle = inverse(blocks[k, k], later)
-        for i in range(k + 1, own + 1):
-            multiply(i, k, middle)
-        update(k + 1, k + 1, k)
-        later = [
-            functools.partial(update, i, j, k)
-            for j in range(k + 1, own + 1)
-            for i in range(j, own + 1)
-            if (i, j) != (k + 1, k + 1)
-        ]
-    last = inverse(blocks[own, own], [functools.partial(go_back, k) for k in range(own - 1, -1, -1)])
-    for k in range(own):
-        back_out[:, k * points : (k + 1) * points] = back[k]
+        middle = inverse(columns[k, at(k)], ahead, guess)
+        side = columns[k, at(k + 1, own + 1)]
+        below = dot_six(split_fine(side), split_fine(middle))
+        lower[k, at(k + 1, own + 1)] = below
+        side_parts, below_parts = split(side), split(below)
+        for j in range(k + 1, own + 1):
+            cut = (j - k - 1) * points
+            left = [piece[cut:] for piece in below_parts]
+            right = [piece[cut : cut + points] for piece in side_parts]
+            columns[j, at(j, own + 1)] = columns[j, at(j, own + 1)] - dot_three(left, right, NT)
+    for k in range(own - 1, -1, -1):
+        total = lower[k, at(own)]
+        if k + 1 < own:
+            done = back_out[:, (k + 1) * points :]
+            total = total - dot_three(split(done), split(lower[k, at(k + 1, own)]))
+        back_out[:, k * points : (k + 1) * points] = total
+    last = inverse(columns[own, at(own)], ahead, guess)
     last_out[...] = last
+    back = {k: back_out[:, k * points : (k + 1) * points] for k in range(own)}
 
     middle, spread, slot_parts = apply_block(values, back, last)
     own_part = spread + noise[0] * values[own]
@@ -327,7 +341,7 @@
         sizes,
         [(coarse + 3,) + tile, (points, depth), square],
         [smem, smem] + [vmem] * 4,
-        [pltpu.VMEM((slots, slots) + square, F32)],
+        [pltpu.VMEM((slots, slots * points, points), F32)] * 2 + [pltpu.VMEM(square, F32)] * 2,
     )(neighbours, at, before, table, mine, noise_prec)
 
     summed, ends, shifted = part[:-2], part[-2:], jnp.zeros_like(part[-2:])

time: 85.4 us -> 84.9 us (level)
  Pallas kernels: 22.2 us -> 20.9 us
    pallas_call x1, Pallas kernels: 19.5 us -> 18.2 us  [local(): call(factor_kernel, sizes, [(coarse + 3,) + tile, (points, depth), square...]
where the time goes in v4:
time: 84.9 us; the launch traced here: 84.7 us
  waiting for transfers between devices  36 us (42%)
  starting transfers between devices  24.6 us (29%)
  Pallas kernels  20.9 us (25%)
  local copies, waits for them, and re-layouts  2.1 us (2%)
  between operations  0.87 us (1%)
    ppermute x15, waiting for transfers between devices, swapped(): lax.ppermute(value, axis, [(at, at ^ reach) for at in range(lax.axis_size...  36 us
    ppermute x15, starting transfers between devices, swapped(): lax.ppermute(value, axis, [(at, at ^ reach) for at in range(lax.axis_size...  24.6 us
    pallas_call x1, Pallas kernels, local(): call(factor_kernel, sizes, [(coarse + 3,) + tile, (points, depth), square...  18.2 us
    unnamed x7, local copies, waits for them, and re-layouts  2.06 us
  transfers between devices with their start and end apart: 15, of which 15 were waited for; matrix products, arithmetic and copies ran while one was open for 0% of the time, Pallas kernels for 0%

profile of v4, /device:TPU:0, one launch (start us, length us, event | category | flops | bytes accessed | tf_op | source)
XLA Modules:
  0.0 84.7 jit_solution(8743593501428462338)
XLA Ops:
  0.6 0.7 copy.6.locations
  1.3 0.0 copy-start.1
  1.3 0.7 copy-done.1
  2.0 3.0 %collective-permute-start = (f32[2,16,256]{2,1,0:T(8,128)S(1)}, f32[2,16,256]{2,1,0:T(8,128)S(1)}, u32[]{:S(2)}, u32[]{:S(2)}) collective-permute-start(f32[2,16,256]{2,1,0:T(8,128)S(1)} %pad_maximum_fusion.7), channel_id=1, source_target_pairs={{0,16},{8,24},{16,0},{24,8},{1,17},{9,25},{17,1},{25,9},{2,18},{10... | collective-permute-start | bytes 98312 | tf_op jit(solution)/shard_map/ppermute | solution.py:289
  5.0 1.9 %collective-permute-done = f32[2,16,256]{2,1,0:T(8,128)S(1)} collective-permute-done((f32[2,16,256]{2,1,0:T(8,128)S(1)}, f32[2,16,256]{2,1,0:T(8,128)S(1)}, u32[]{:S(2)}, u32[]{:S(2)}) %collective-permute-start) | collective-permute-done | bytes 32800 | tf_op jit(solution)/shard_map/ppermute | solution.py:289
  6.9 2.1 %collective-permute-start.1 = (f32[2,16,256]{2,1,0:T(8,128)S(1)}, f32[2,16,256]{2,1,0:T(8,128)S(1)}, u32[]{:S(2)}, u32[]{:S(2)}) collective-permute-start(f32[2,16,256]{2,1,0:T(8,128)S(1)} %pad_maximum_fusion.8), channel_id=1, source_target_pairs={{0,8},{8,0},{16,24},{24,16},{1,9},{9,1},{17,25},{25,17},{2,10},{10... | collective-permute-start | bytes 98312 | tf_op jit(solution)/shard_map/ppermute | solution.py:289
  9.0 1.9 %collective-permute-done.1 = f32[2,16,256]{2,1,0:T(8,128)S(1)} collective-permute-done((f32[2,16,256]{2,1,0:T(8,128)S(1)}, f32[2,16,256]{2,1,0:T(8,128)S(1)}, u32[]{:S(2)}, u32[]{:S(2)}) %collective-permute-start.1) | collective-permute-done | bytes 32800 | tf_op jit(solution)/shard_map/ppermute | solution.py:289
  10.9 3.2 %collective-permute-start.2 = (f32[2,16,256]{2,1,0:T(8,128)S(1)}, f32[2,16,256]{2,1,0:T(8,128)S(1)}, u32[]{:S(2)}, u32[]{:S(2)}) collective-permute-start(f32[2,16,256]{2,1,0:T(8,128)S(1)} %pad_maximum_fusion.9), channel_id=1, source_target_pairs={{0,4},{1,5},{2,6},{3,7},{4,0},{5,1},{6,2},{7,3},{8,12},{9,13},{10,... | collective-permute-start | bytes 98312 | tf_op jit(solution)/shard_map/ppermute | solution.py:289
  14.0 2.0 %collective-permute-done.2 = f32[2,16,256]{2,1,0:T(8,128)S(1)} collective-permute-done((f32[2,16,256]{2,1,0:T(8,128)S(1)}, f32[2,16,256]{2,1,0:T(8,128)S(1)}, u32[]{:S(2)}, u32[]{:S(2)}) %collective-permute-start.2) | collective-permute-done | bytes 32800 | tf_op jit(solution)/shard_map/ppermute | solution.py:289
  16.1 1.9 %collective-permute-start.3 = (f32[3,16,256]{2,1,0:T(8,128)S(1)}, f32[3,16,256]{2,1,0:T(8,128)S(1)}, u32[]{:S(2)}, u32[]{:S(2)}) collective-permute-start(f32[3,16,256]{2,1,0:T(8,128)S(1)} %pad_maximum_fusion.6), channel_id=1, source_target_pairs={{0,2},{1,3},{2,0},{3,1},{4,6},{5,7},{6,4},{7,5},{8,10},{9,11},{10,... | collective-permute-start | bytes 147464 | tf_op jit(solution)/shard_map/ppermute | solution.py:289
  17.9 2.3 %collective-permute-done.3 = f32[3,16,256]{2,1,0:T(8,128)S(1)} collective-permute-done((f32[3,16,256]{2,1,0:T(8,128)S(1)}, f32[3,16,256]{2,1,0:T(8,128)S(1)}, u32[]{:S(2)}, u32[]{:S(2)}) %collective-permute-start.3) | collective-permute-done | bytes 49184 | tf_op jit(solution)/shard_map/ppermute | solution.py:289
  20.2 0.1 collective-permute-start.4
  20.3 1.3 %collective-permute-done.4 = f32[5,16,256]{2,1,0:T(8,128)S(1)} collective-permute-done((f32[5,16,256]{2,1,0:T(8,128)S(1)}, f32[5,16,256]{2,1,0:T(8,128)S(1)}, u32[]{:S(2)}, u32[]{:S(2)}) %collective-permute-start.4) | collective-permute-done | bytes 81952 | tf_op jit(solution)/shard_map/ppermute | solution.py:289
  21.6 0.0 copy-start
  21.6 0.0 copy-start.2
  21.6 0.7 copy-done
  22.3 0.0 copy-done.2
  22.3 18.2 %shard_map.60 = (f32[11,8,256]{2,1,0:T(8,128)S(1)}, f32[256,768]{1,0:T(8,128)S(1)}, f32[256,256]{1,0:T(8,128)S(1)}) custom-call(s32[1,4]{1,0:T(1,128)S(1)} %copy-done.2, s32[1]{0:T(128)} %bitcast.me, f32[1,16,256]{2,1,0:T(8,128)S(1)} %slice.229.before, f32[8,16,256]{2,1,0:T(8,128)S(1)} %pad_maximum_fusion.table, f32[16,256]{1,0:T(8,128)S(1)} %shard_map.59.mine, ...), custom_call_target="tpu_custom_call" | custom-call | tf_op jit(solution)/shard_map/pallas_call | solution.py:339
  40.5 0.5 collective-permute-start.5
  41.0 0.9 %collective-permute-done.5 = f32[11,8,256]{2,1,0:T(8,128)S(1)} collective-permute-done((f32[11,8,256]{2,1,0:T(8,128)S(1)}, f32[11,8,256]{2,1,0:T(8,128)S(1)}, u32[]{:S(2)}, u32[]{:S(2)}) %collective-permute-start.5) | collective-permute-done | bytes 90144 | tf_op jit(solution)/shard_map/ppermute | solution.py:289
  42.0 2.1 %collective-permute-start.6 = (f32[11,8,256]{2,1,0:T(8,128)S(1)}, f32[11,8,256]{2,1,0:T(8,128)S(1)}, u32[]{:S(2)}, u32[]{:S(2)}) collective-permute-start(f32[11,8,256]{2,1,0:T(8,128)S(1)} %pad_maximum_fusion.1), channel_id=1, source_target_pairs={{0,2},{1,3},{2,0},{3,1},{4,6},{5,7},{6,4},{7,5},{8,10},{9,11},{10,... | collective-permute-start | bytes 270344 | tf_op jit(solution)/shard_map/ppermute | solution.py:289
  44.1 2.9 %collective-permute-done.6 = f32[11,8,256]{2,1,0:T(8,128)S(1)} collective-permute-done((f32[11,8,256]{2,1,0:T(8,128)S(1)}, f32[11,8,256]{2,1,0:T(8,128)S(1)}, u32[]{:S(2)}, u32[]{:S(2)}) %collective-permute-start.6) | collective-permute-done | bytes 90144 | tf_op jit(solution)/shard_map/ppermute | solution.py:289
  47.1 3.3 %collective-permute-start.7 = (f32[11,8,256]{2,1,0:T(8,128)S(1)}, f32[11,8,256]{2,1,0:T(8,128)S(1)}, u32[]{:S(2)}, u32[]{:S(2)}) collective-permute-start(f32[11,8,256]{2,1,0:T(8,128)S(1)} %pad_maximum_fusion.2), channel_id=1, source_target_pairs={{0,4},{1,5},{2,6},{3,7},{4,0},{5,1},{6,2},{7,3},{8,12},{9,13},{10,... | collective-permute-start | bytes 270344 | tf_op jit(solution)/shard_map/ppermute | solution.py:289
  50.3 4.3 %collective-permute-done.7 = f32[11,8,256]{2,1,0:T(8,128)S(1)} collective-permute-done((f32[11,8,256]{2,1,0:T(8,128)S(1)}, f32[11,8,256]{2,1,0:T(8,128)S(1)}, u32[]{:S(2)}, u32[]{:S(2)}) %collective-permute-start.7) | collective-permute-done | bytes 90144 | tf_op jit(solution)/shard_map/ppermute | solution.py:289
  54.7 1.6 %collective-permute-start.8 = (f32[11,8,256]{2,1,0:T(8,128)S(1)}, f32[11,8,256]{2,1,0:T(8,128)S(1)}, u32[]{:S(2)}, u32[]{:S(2)}) collective-permute-start(f32[11,8,256]{2,1,0:T(8,128)S(1)} %pad_maximum_fusion.3), channel_id=1, source_target_pairs={{0,8},{8,0},{16,24},{24,16},{1,9},{9,1},{17,25},{25,17},{2,10},{10... | collective-permute-start | bytes 270344 | tf_op jit(solution)/shard_map/ppermute | solution.py:289
  56.3 3.0 %collective-permute-done.8 = f32[11,8,256]{2,1,0:T(8,128)S(1)} collective-permute-done((f32[11,8,256]{2,1,0:T(8,128)S(1)}, f32[11,8,256]{2,1,0:T(8,128)S(1)}, u32[]{:S(2)}, u32[]{:S(2)}) %collective-permute-start.8) | collective-permute-done | bytes 90144 | tf_op jit(solution)/shard_map/ppermute | solution.py:289
  59.4 1.2 %collective-permute-start.9 = (f32[11,8,256]{2,1,0:T(8,128)S(1)}, f32[11,8,256]{2,1,0:T(8,128)S(1)}, u32[]{:S(2)}, u32[]{:S(2)}) collective-permute-start(f32[11,8,256]{2,1,0:T(8,128)S(1)} %pad_maximum_fusion.4), channel_id=1, source_target_pairs={{0,16},{8,24},{16,0},{24,8},{1,17},{9,25},{17,1},{25,9},{2,18},{10... | collective-permute-start | bytes 270344 | tf_op jit(solution)/shard_map/ppermute | solution.py:289
  60.6 3.4 %collective-permute-done.9 = f32[11,8,256]{2,1,0:T(8,128)S(1)} collective-permute-done((f32[11,8,256]{2,1,0:T(8,128)S(1)}, f32[11,8,256]{2,1,0:T(8,128)S(1)}, u32[]{:S(2)}, u32[]{:S(2)}) %collective-permute-start.9) | collective-permute-done | bytes 90144 | tf_op jit(solution)/shard_map/ppermute | solution.py:289
  64.0 1.7 %shard_map.61 = (f32[10,8,256]{2,1,0:T(8,128)S(1)}, f32[2,8,256]{2,1,0:T(8,128)S(1)}, f32[8,256]{1,0:T(8,128)S(1)}, f32[8,128]{1,0:T(8,128)S(1)}) custom-call(s32[1,4]{1,0:T(1,128)S(1)} %copy-done.2, s32[1]{0:T(128)} %bitcast.me, f32[1,16,256]{2,1,0:T(8,128)S(1)} %slice.229.before, f32[8,16,256]{2,1,0:T(8,128)S(1)} %pad_maximum_fusion.table, ...), custom_call_target="tpu_custom_call" | custom-call | tf_op jit(solution)/shard_map/pallas_call | solution.py:352
  65.7 0.0 collective-permute-start.10
  65.8 1.2 %collective-permute-done.10 = f32[6,8,256]{2,1,0:T(8,128)S(1)} collective-permute-done((f32[6,8,256]{2,1,0:T(8,128)S(1)}, f32[6,8,256]{2,1,0:T(8,128)S(1)}, u32[]{:S(2)}, u32[]{:S(2)}) %collective-permute-start.10) | collective-permute-done | bytes 49184 | tf_op jit(solution)/shard_map/ppermute | solution.py:289
  67.0 0.8 collective-permute-start.11
  67.8 3.2 %collective-permute-done.11 = f32[4,8,256]{2,1,0:T(8,128)S(1)} collective-permute-done((f32[4,8,256]{2,1,0:T(8,128)S(1)}, f32[4,8,256]{2,1,0:T(8,128)S(1)}, u32[]{:S(2)}, u32[]{:S(2)}) %collective-permute-start.11) | collective-permute-done | bytes 32800 | tf_op jit(solution)/shard_map/ppermute | solution.py:289
  71.0 2.1 %collective-permute-start.12 = (f32[3,8,256]{2,1,0:T(8,128)S(1)}, f32[3,8,256]{2,1,0:T(8,128)S(1)}, u32[]{:S(2)}, u32[]{:S(2)}) collective-permute-start(f32[3,8,256]{2,1,0:T(8,128)S(1)} %pad_maximum_fusion.11), channel_id=1, source_target_pairs={{0,4},{1,5},{2,6},{3,7},{4,0},{5,1},{6,2},{7,3},{8,12},{9,13},{10,... | collective-permute-start | bytes 73736 | tf_op jit(solution)/shard_map/ppermute | solution.py:289
  73.1 2.7 %collective-permute-done.12 = f32[3,8,256]{2,1,0:T(8,128)S(1)} collective-permute-done((f32[3,8,256]{2,1,0:T(8,128)S(1)}, f32[3,8,256]{2,1,0:T(8,128)S(1)}, u32[]{:S(2)}, u32[]{:S(2)}) %collective-permute-start.12) | collective-permute-done | bytes 24608 | tf_op jit(solution)/shard_map/ppermute | solution.py:289
  75.8 1.6 %collective-permute-start.13 = (f32[3,8,256]{2,1,0:T(8,128)S(1)}, f32[3,8,256]{2,1,0:T(8,128)S(1)}, u32[]{:S(2)}, u32[]{:S(2)}) collective-permute-start(f32[3,8,256]{2,1,0:T(8,128)S(1)} %pad_maximum_fusion.12), channel_id=1, source_target_pairs={{0,8},{8,0},{16,24},{24,16},{1,9},{9,1},{17,25},{25,17},{2,10},{10... | collective-permute-start | bytes 73736 | tf_op jit(solution)/shard_map/ppermute | solution.py:289
  77.4 2.3 %collective-permute-done.13 = f32[3,8,256]{2,1,0:T(8,128)S(1)} collective-permute-done((f32[3,8,256]{2,1,0:T(8,128)S(1)}, f32[3,8,256]{2,1,0:T(8,128)S(1)}, u32[]{:S(2)}, u32[]{:S(2)}) %collective-permute-start.13) | collective-permute-done | bytes 24608 | tf_op jit(solution)/shard_map/ppermute | solution.py:289
  79.7 1.2 %collective-permute-start.14 = (f32[3,8,256]{2,1,0:T(8,128)S(1)}, f32[3,8,256]{2,1,0:T(8,128)S(1)}, u32[]{:S(2)}, u32[]{:S(2)}) collective-permute-start(f32[3,8,256]{2,1,0:T(8,128)S(1)} %pad_maximum_fusion.13), channel_id=1, source_target_pairs={{0,16},{8,24},{16,0},{24,8},{1,17},{9,25},{17,1},{25,9},{2,18},{10... | collective-permute-start | bytes 73736 | tf_op jit(solution)/shard_map/ppermute | solution.py:289
  81.0 2.7 %collective-permute-done.14 = f32[3,8,256]{2,1,0:T(8,128)S(1)} collective-permute-done((f32[3,8,256]{2,1,0:T(8,128)S(1)}, f32[3,8,256]{2,1,0:T(8,128)S(1)}, u32[]{:S(2)}, u32[]{:S(2)}) %collective-permute-start.14) | collective-permute-done | bytes 24608 | tf_op jit(solution)/shard_map/ppermute | solution.py:289
  83.7 1.0 %shard_map.62 = (f32[1,8,256]{2,1,0:T(8,128)}, f32[1,8,256]{2,1,0:T(8,128)}) custom-call(s32[1]{0:T(128)} %bitcast.me, f32[2,8,256]{2,1,0:T(8,128)S(1)} %slice_add_fusion.7.received, f32[1,8,256]{2,1,0:T(8,128)S(1)} %slice_select_fusion.6.shifted, f32[2,8,256]{2,1,0:T(8,128)S(1)} %get-tuple-element.13.images, f32[8,256]{1,0:T(8,128)S(1)} %get-tuple-element.14.residual, ...), custom_call_target="tpu_custom_call" | custom-call | tf_op jit(solution)/shard_map/pallas_call | solution.py:368
  (51 shorter events, 0.3 us)
Async XLA Ops:
  1.3 0.7 copy-start.1
  2.0 4.9 %collective-permute-start = (f32[2,16,256]{2,1,0:T(8,128)S(1)}, f32[2,16,256]{2,1,0:T(8,128)S(1)}, u32[]{:S(2)}, u32[]{:S(2)}) collective-permute-start(f32[2,16,256]{2,1,0:T(8,128)S(1)} %pad_maximum_fusion.7), channel_id=1, source_target_pairs={{0,16},{8,24},{16,0},{24,8},{1,17},{9,25},{17,1},{25,9},{2,18},{10... | collective-permute-start | bytes 98312 | tf_op jit(solution)/shard_map/ppermute | solution.py:289
  6.9 4.0 %collective-permute-start.1 = (f32[2,16,256]{2,1,0:T(8,128)S(1)}, f32[2,16,256]{2,1,0:T(8,128)S(1)}, u32[]{:S(2)}, u32[]{:S(2)}) collective-permute-start(f32[2,16,256]{2,1,0:T(8,128)S(1)} %pad_maximum_fusion.8), channel_id=1, source_target_pairs={{0,8},{8,0},{16,24},{24,16},{1,9},{9,1},{17,25},{25,17},{2,10},{10... | collective-permute-start | bytes 98312 | tf_op jit(solution)/shard_map/ppermute | solution.py:289
  10.9 5.2 %collective-permute-start.2 = (f32[2,16,256]{2,1,0:T(8,128)S(1)}, f32[2,16,256]{2,1,0:T(8,128)S(1)}, u32[]{:S(2)}, u32[]{:S(2)}) collective-permute-start(f32[2,16,256]{2,1,0:T(8,128)S(1)} %pad_maximum_fusion.9), channel_id=1, source_target_pairs={{0,4},{1,5},{2,6},{3,7},{4,0},{5,1},{6,2},{7,3},{8,12},{9,13},{10,... | collective-permute-start | bytes 98312 | tf_op jit(solution)/shard_map/ppermute | solution.py:289
  16.1 4.2 %collective-permute-start.3 = (f32[3,16,256]{2,1,0:T(8,128)S(1)}, f32[3,16,256]{2,1,0:T(8,128)S(1)}, u32[]{:S(2)}, u32[]{:S(2)}) collective-permute-start(f32[3,16,256]{2,1,0:T(8,128)S(1)} %pad_maximum_fusion.6), channel_id=1, source_target_pairs={{0,2},{1,3},{2,0},{3,1},{4,6},{5,7},{6,4},{7,5},{8,10},{9,11},{10,... | collective-permute-start | bytes 147464 | tf_op jit(solution)/shard_map/ppermute | solution.py:289
  20.2 1.3 %collective-permute-start.4 = (f32[5,16,256]{2,1,0:T(8,128)S(1)}, f32[5,16,256]{2,1,0:T(8,128)S(1)}, u32[]{:S(2)}, u32[]{:S(2)}) collective-permute-start(f32[5,16,256]{2,1,0:T(8,128)S(1)} %pad_maximum_fusion.5), channel_id=1, source_target_pairs={{0,1},{1,0},{2,3},{3,2},{4,5},{5,4},{6,7},{7,6},{8,9},{9,8},{10,11... | collective-permute-start | bytes 245768 | tf_op jit(solution)/shard_map/ppermute | solution.py:289
  21.6 0.7 copy-start
  21.6 0.7 copy-start.2
  40.5 1.5 %collective-permute-start.5 = (f32[11,8,256]{2,1,0:T(8,128)S(1)}, f32[11,8,256]{2,1,0:T(8,128)S(1)}, u32[]{:S(2)}, u32[]{:S(2)}) collective-permute-start(f32[11,8,256]{2,1,0:T(8,128)S(1)} %get-tuple-element.9.part), channel_id=1, source_target_pairs={{0,1},{1,0},{2,3},{3,2},{4,5},{5,4},{6,7},{7,6},{8,9},{9,8},{10,11... | collective-permute-start | bytes 270344 | tf_op jit(solution)/shard_map/ppermute | solution.py:289
  42.0 5.0 %collective-permute-start.6 = (f32[11,8,256]{2,1,0:T(8,128)S(1)}, f32[11,8,256]{2,1,0:T(8,128)S(1)}, u32[]{:S(2)}, u32[]{:S(2)}) collective-permute-start(f32[11,8,256]{2,1,0:T(8,128)S(1)} %pad_maximum_fusion.1), channel_id=1, source_target_pairs={{0,2},{1,3},{2,0},{3,1},{4,6},{5,7},{6,4},{7,5},{8,10},{9,11},{10,... | collective-permute-start | bytes 270344 | tf_op jit(solution)/shard_map/ppermute | solution.py:289
  47.1 7.6 %collective-permute-start.7 = (f32[11,8,256]{2,1,0:T(8,128)S(1)}, f32[11,8,256]{2,1,0:T(8,128)S(1)}, u32[]{:S(2)}, u32[]{:S(2)}) collective-permute-start(f32[11,8,256]{2,1,0:T(8,128)S(1)} %pad_maximum_fusion.2), channel_id=1, source_target_pairs={{0,4},{1,5},{2,6},{3,7},{4,0},{5,1},{6,2},{7,3},{8,12},{9,13},{10,... | collective-permute-start | bytes 270344 | tf_op jit(solution)/shard_map/ppermute | solution.py:289
  54.7 4.6 %collective-permute-start.8 = (f32[11,8,256]{2,1,0:T(8,128)S(1)}, f32[11,8,256]{2,1,0:T(8,128)S(1)}, u32[]{:S(2)}, u32[]{:S(2)}) collective-permute-start(f32[11,8,256]{2,1,0:T(8,128)S(1)} %pad_maximum_fusion.3), channel_id=1, source_target_pairs={{0,8},{8,0},{16,24},{24,16},{1,9},{9,1},{17,25},{25,17},{2,10},{10... | collective-permute-start | bytes 270344 | tf_op jit(solution)/shard_map/ppermute | solution.py:289
  59.4 4.6 %collective-permute-start.9 = (f32[11,8,256]{2,1,0:T(8,128)S(1)}, f32[11,8,256]{2,1,0:T(8,128)S(1)}, u32[]{:S(2)}, u32[]{:S(2)}) collective-permute-start(f32[11,8,256]{2,1,0:T(8,128)S(1)} %pad_maximum_fusion.4), channel_id=1, source_target_pairs={{0,16},{8,24},{16,0},{24,8},{1,17},{9,25},{17,1},{25,9},{2,18},{10... | collective-permute-start | bytes 270344 | tf_op jit(solution)/shard_map/ppermute | solution.py:289
  65.7 1.3 %collective-permute-start.10 = (f32[6,8,256]{2,1,0:T(8,128)S(1)}, f32[6,8,256]{2,1,0:T(8,128)S(1)}, u32[]{:S(2)}, u32[]{:S(2)}) collective-permute-start(f32[6,8,256]{2,1,0:T(8,128)S(1)} %concatenate.72), channel_id=1, source_target_pairs={{0,1},{1,0},{2,3},{3,2},{4,5},{5,4},{6,7},{7,6},{8,9},{9,8},{10,11... | collective-permute-start | bytes 147464 | tf_op jit(solution)/shard_map/ppermute | solution.py:289
  67.0 4.0 %collective-permute-start.11 = (f32[4,8,256]{2,1,0:T(8,128)S(1)}, f32[4,8,256]{2,1,0:T(8,128)S(1)}, u32[]{:S(2)}, u32[]{:S(2)}) collective-permute-start(f32[4,8,256]{2,1,0:T(8,128)S(1)} %pad_maximum_fusion.10), channel_id=1, source_target_pairs={{0,2},{1,3},{2,0},{3,1},{4,6},{5,7},{6,4},{7,5},{8,10},{9,11},{10,... | collective-permute-start | bytes 98312 | tf_op jit(solution)/shard_map/ppermute | solution.py:289
  71.0 4.8 %collective-permute-start.12 = (f32[3,8,256]{2,1,0:T(8,128)S(1)}, f32[3,8,256]{2,1,0:T(8,128)S(1)}, u32[]{:S(2)}, u32[]{:S(2)}) collective-permute-start(f32[3,8,256]{2,1,0:T(8,128)S(1)} %pad_maximum_fusion.11), channel_id=1, source_target_pairs={{0,4},{1,5},{2,6},{3,7},{4,0},{5,1},{6,2},{7,3},{8,12},{9,13},{10,... | collective-permute-start | bytes 73736 | tf_op jit(solution)/shard_map/ppermute | solution.py:289
  75.8 3.9 %collective-permute-start.13 = (f32[3,8,256]{2,1,0:T(8,128)S(1)}, f32[3,8,256]{2,1,0:T(8,128)S(1)}, u32[]{:S(2)}, u32[]{:S(2)}) collective-permute-start(f32[3,8,256]{2,1,0:T(8,128)S(1)} %pad_maximum_fusion.12), channel_id=1, source_target_pairs={{0,8},{8,0},{16,24},{24,16},{1,9},{9,1},{17,25},{25,17},{2,10},{10... | collective-permute-start | bytes 73736 | tf_op jit(solution)/shard_map/ppermute | solution.py:289
  79.7 3.9 %collective-permute-start.14 = (f32[3,8,256]{2,1,0:T(8,128)S(1)}, f32[3,8,256]{2,1,0:T(8,128)S(1)}, u32[]{:S(2)}, u32[]{:S(2)}) collective-permute-start(f32[3,8,256]{2,1,0:T(8,128)S(1)} %pad_maximum_fusion.13), channel_id=1, source_target_pairs={{0,16},{8,24},{16,0},{24,8},{1,17},{9,25},{17,1},{25,9},{2,18},{10... | collective-permute-start | bytes 73736 | tf_op jit(solution)/shard_map/ppermute | solution.py:289

commit v5 on v4

--- a/solution.py
+++ b/solution.py
@@ -20,6 +20,7 @@
 VMEM_LIMIT = 48 * 1024 * 1024
 CLOSE = 2e-3
 ALWAYS = 3
+ROWS = 128
 
 
 def split(value):
@@ -29,10 +30,6 @@
 
 def dot(left, right, dims=NN, precision=None):
     return lax.dot_general(left, right, dims, precision=precision, preferred_element_type=F32)
-
-
-def dot_three(left, right, dims=NN):
-    return dot(left[0], right[0], dims) + (dot(left[0], right[1], dims) + dot(left[1], right[0], dims))
 
 
 def split_fine(value):
@@ -42,9 +39,21 @@
     return high, middle, (rest - middle.astype(F32)).astype(jnp.bfloat16)
 
 
-def dot_six(left, right, dims=NN):
-    small = dot(left[1], right[1], dims) + (dot(left[0], right[2], dims) + dot(left[2], right[0], dims))
-    return dot(left[0], right[0], dims) + ((dot(left[0], right[1], dims) + dot(left[1], right[0], dims)) + small)
+def taken(base, left, right, dims=NN, rows=None):
+    count = len(left)
+    pieces = []
+    rows = rows or base.shape[0]
+    for first in range(0, base.shape[0], rows):
+        total = base[first : first + rows]
+        cut = [part[first : first + rows] for part in left]
+        for at in range(count):
+            group = None
+            for other in range(count - 1 - at, -1, -1):
+                term = dot(cut[other], right[at], dims)
+                group = term if group is None else group + term
+            total = total - group
+        pieces.append(total)
+    return pieces[0] if len(pieces) == 1 else jnp.concatenate(pieces, axis=0)
 
 
 def newton_levels(order):
@@ -73,8 +82,8 @@
 
     def advance(scale, now, held, only_guess=False):
         now_parts = split(now)
-        new_held = scale * (2.0 * held - dot_three(split(held), now_parts))
-        return (None if only_guess else scale * (2.0 * now - dot_three(now_parts, now_parts))), new_held
+        new_held = scale * taken(2.0 * held, split(held), now_parts, rows=ROWS)
+        return (None if only_guess else scale * taken(2.0 * now, now_parts, now_parts, rows=ROWS)), new_held
 
     for level in range(len(levels) - 1, always, -1):
 
@@ -85,8 +94,8 @@
     now, held = ahead[...], guess[...]
     for level in range(always, 0, -1):
         now, held = advance(levels[level][0], now, held, level == 1)
-    error = identity - dot_six(split_fine(matrix), split_fine(held))
-    return held + dot_three(split(held), split(error))
+    error = taken(identity, split_fine(matrix), split_fine(held), rows=ROWS)
+    return taken(held, split(held), split(-error), rows=ROWS)
 
 
 def slot_list(slots):
@@ -156,19 +165,19 @@
     for k in range(own):
         middle = inverse(columns[k, at(k)], ahead, guess)
         side = columns[k, at(k + 1, own + 1)]
-        below = dot_six(split_fine(side), split_fine(middle))
+        below = -taken(jnp.zeros_like(side), split_fine(side), split_fine(middle))
         lower[k, at(k + 1, own + 1)] = below
         side_parts, below_parts = split(side), split(below)
         for j in range(k + 1, own + 1):
             cut = (j - k - 1) * points
             left = [piece[cut:] for piece in below_parts]
             right = [piece[cut : cut + points] for piece in side_parts]
-            columns[j, at(j, own + 1)] = columns[j, at(j, own + 1)] - dot_three(left, right, NT)
+            columns[j, at(j, own + 1)] = taken(columns[j, at(j, own + 1)], left, right, NT)
     for k in range(own - 1, -1, -1):
         total = lower[k, at(own)]
         if k + 1 < own:
             done = back_out[:, (k + 1) * points :]
-            total = total - dot_three(split(done), split(lower[k, at(k + 1, own)]))
+            total = taken(total, split(done), split(lower[k, at(k + 1, own)]))
         back_out[:, k * points : (k + 1) * points] = total
     last = inverse(columns[own, at(own)], ahead, guess)
     last_out[...] = last
@@ -201,10 +210,10 @@
     own = len(values) - 1
     middle = values[own]
     for k in range(own):
-        middle = middle - dot_three(split(values[k]), split(back[k]), NT)
-    spread = dot_three(split(middle), split(last))
+        middle = taken(middle, split(values[k]), split(back[k]), NT)
+    spread = -taken(jnp.zeros_like(middle), split(middle), split(last))
     spread_parts = split(spread)
-    slot_parts = [-dot_three(spread_parts, split(back[k])) for k in range(own)]
+    slot_parts = [taken(jnp.zeros_like(middle), spread_parts, split(back[k])) for k in range(own)]
     return middle, spread, slot_parts
 
 

time: 84.9 us -> 81.3 us (0.958)
  Pallas kernels: 20.9 us -> 17.2 us
  waiting for transfers between devices: 36 us -> 37 us
    pallas_call x1, Pallas kernels: 18.2 us -> 14.7 us  [local(): call(factor_kernel, sizes, [(coarse + 3,) + tile, (points, depth), square...]
    ppermute x15, waiting for transfers between devices: 36 us -> 37 us  [swapped(): lax.ppermute(value, axis, [(at, at ^ reach) for at in range(lax.axis_size...]
where the time goes in v5:
time: 81.3 us
  waiting for transfers between devices  37 us (46%)
  starting transfers between devices  23.8 us (29%)
  Pallas kernels  17.2 us (21%)
  local copies, waits for them, and re-layouts  2.1 us (3%)
  between operations  0.87 us (1%)
    ppermute x15, waiting for transfers between devices, swapped(): lax.ppermute(value, axis, [(at, at ^ reach) for at in range(lax.axis_size...  37 us
    ppermute x15, starting transfers between devices, swapped(): lax.ppermute(value, axis, [(at, at ^ reach) for at in range(lax.axis_size...  23.8 us
    pallas_call x1, Pallas kernels, local(): call(factor_kernel, sizes, [(coarse + 3,) + tile, (points, depth), square...  14.7 us
    unnamed x7, local copies, waits for them, and re-layouts  2.06 us
  transfers between devices with their start and end apart: 15, of which 15 were waited for; matrix products, arithmetic and copies ran while one was open for 0% of the time, Pallas kernels for 0%

profile of v5, /device:TPU:0, one launch (start us, length us, event | category | flops | bytes accessed | tf_op | source)
XLA Modules:
  0.0 81.3 jit_solution(17038157182484689252)
XLA Ops:
  0.6 0.7 copy.6.locations
  1.3 0.0 copy-start.1
  1.3 0.7 copy-done.1
  2.0 3.0 %collective-permute-start = (f32[2,16,256]{2,1,0:T(8,128)S(1)}, f32[2,16,256]{2,1,0:T(8,128)S(1)}, u32[]{:S(2)}, u32[]{:S(2)}) collective-permute-start(f32[2,16,256]{2,1,0:T(8,128)S(1)} %pad_maximum_fusion.7), channel_id=1, source_target_pairs={{0,16},{8,24},{16,0},{24,8},{1,17},{9,25},{17,1},{25,9},{2,18},{10... | collective-permute-start | bytes 98312 | tf_op jit(solution)/shard_map/ppermute | solution.py:298
  5.0 1.9 %collective-permute-done = f32[2,16,256]{2,1,0:T(8,128)S(1)} collective-permute-done((f32[2,16,256]{2,1,0:T(8,128)S(1)}, f32[2,16,256]{2,1,0:T(8,128)S(1)}, u32[]{:S(2)}, u32[]{:S(2)}) %collective-permute-start) | collective-permute-done | bytes 32800 | tf_op jit(solution)/shard_map/ppermute | solution.py:298
  6.9 2.1 %collective-permute-start.1 = (f32[2,16,256]{2,1,0:T(8,128)S(1)}, f32[2,16,256]{2,1,0:T(8,128)S(1)}, u32[]{:S(2)}, u32[]{:S(2)}) collective-permute-start(f32[2,16,256]{2,1,0:T(8,128)S(1)} %pad_maximum_fusion.8), channel_id=1, source_target_pairs={{0,8},{8,0},{16,24},{24,16},{1,9},{9,1},{17,25},{25,17},{2,10},{10... | collective-permute-start | bytes 98312 | tf_op jit(solution)/shard_map/ppermute | solution.py:298
  9.0 1.9 %collective-permute-done.1 = f32[2,16,256]{2,1,0:T(8,128)S(1)} collective-permute-done((f32[2,16,256]{2,1,0:T(8,128)S(1)}, f32[2,16,256]{2,1,0:T(8,128)S(1)}, u32[]{:S(2)}, u32[]{:S(2)}) %collective-permute-start.1) | collective-permute-done | bytes 32800 | tf_op jit(solution)/shard_map/ppermute | solution.py:298
  10.9 3.2 %collective-permute-start.2 = (f32[2,16,256]{2,1,0:T(8,128)S(1)}, f32[2,16,256]{2,1,0:T(8,128)S(1)}, u32[]{:S(2)}, u32[]{:S(2)}) collective-permute-start(f32[2,16,256]{2,1,0:T(8,128)S(1)} %pad_maximum_fusion.9), channel_id=1, source_target_pairs={{0,4},{1,5},{2,6},{3,7},{4,0},{5,1},{6,2},{7,3},{8,12},{9,13},{10,... | collective-permute-start | bytes 98312 | tf_op jit(solution)/shard_map/ppermute | solution.py:298
  14.0 2.0 %collective-permute-done.2 = f32[2,16,256]{2,1,0:T(8,128)S(1)} collective-permute-done((f32[2,16,256]{2,1,0:T(8,128)S(1)}, f32[2,16,256]{2,1,0:T(8,128)S(1)}, u32[]{:S(2)}, u32[]{:S(2)}) %collective-permute-start.2) | collective-permute-done | bytes 32800 | tf_op jit(solution)/shard_map/ppermute | solution.py:298
  16.1 1.9 %collective-permute-start.3 = (f32[3,16,256]{2,1,0:T(8,128)S(1)}, f32[3,16,256]{2,1,0:T(8,128)S(1)}, u32[]{:S(2)}, u32[]{:S(2)}) collective-permute-start(f32[3,16,256]{2,1,0:T(8,128)S(1)} %pad_maximum_fusion.6), channel_id=1, source_target_pairs={{0,2},{1,3},{2,0},{3,1},{4,6},{5,7},{6,4},{7,5},{8,10},{9,11},{10,... | collective-permute-start | bytes 147464 | tf_op jit(solution)/shard_map/ppermute | solution.py:298
  17.9 2.3 %collective-permute-done.3 = f32[3,16,256]{2,1,0:T(8,128)S(1)} collective-permute-done((f32[3,16,256]{2,1,0:T(8,128)S(1)}, f32[3,16,256]{2,1,0:T(8,128)S(1)}, u32[]{:S(2)}, u32[]{:S(2)}) %collective-permute-start.3) | collective-permute-done | bytes 49184 | tf_op jit(solution)/shard_map/ppermute | solution.py:298
  20.2 0.1 collective-permute-start.4
  20.3 1.3 %collective-permute-done.4 = f32[5,16,256]{2,1,0:T(8,128)S(1)} collective-permute-done((f32[5,16,256]{2,1,0:T(8,128)S(1)}, f32[5,16,256]{2,1,0:T(8,128)S(1)}, u32[]{:S(2)}, u32[]{:S(2)}) %collective-permute-start.4) | collective-permute-done | bytes 81952 | tf_op jit(solution)/shard_map/ppermute | solution.py:298
  21.6 0.0 copy-start
  21.6 0.0 copy-start.2
  21.6 0.7 copy-done
  22.3 0.0 copy-done.2
  22.3 14.7 %shard_map.60 = (f32[11,8,256]{2,1,0:T(8,128)S(1)}, f32[256,768]{1,0:T(8,128)S(1)}, f32[256,256]{1,0:T(8,128)S(1)}) custom-call(s32[1,4]{1,0:T(1,128)S(1)} %copy-done.2, s32[1]{0:T(128)} %bitcast.me, f32[1,16,256]{2,1,0:T(8,128)S(1)} %slice.229.before, f32[8,16,256]{2,1,0:T(8,128)S(1)} %pad_maximum_fusion.table, f32[16,256]{1,0:T(8,128)S(1)} %shard_map.59.mine, ...), custom_call_target="tpu_custom_call" | custom-call | tf_op jit(solution)/shard_map/pallas_call | solution.py:348
  37.0 0.2 collective-permute-start.5
  37.2 1.1 %collective-permute-done.5 = f32[11,8,256]{2,1,0:T(8,128)S(1)} collective-permute-done((f32[11,8,256]{2,1,0:T(8,128)S(1)}, f32[11,8,256]{2,1,0:T(8,128)S(1)}, u32[]{:S(2)}, u32[]{:S(2)}) %collective-permute-start.5) | collective-permute-done | bytes 90144 | tf_op jit(solution)/shard_map/ppermute | solution.py:298
  38.4 2.3 %collective-permute-start.6 = (f32[11,8,256]{2,1,0:T(8,128)S(1)}, f32[11,8,256]{2,1,0:T(8,128)S(1)}, u32[]{:S(2)}, u32[]{:S(2)}) collective-permute-start(f32[11,8,256]{2,1,0:T(8,128)S(1)} %pad_maximum_fusion.1), channel_id=1, source_target_pairs={{0,2},{1,3},{2,0},{3,1},{4,6},{5,7},{6,4},{7,5},{8,10},{9,11},{10,... | collective-permute-start | bytes 270344 | tf_op jit(solution)/shard_map/ppermute | solution.py:298
  40.6 2.9 %collective-permute-done.6 = f32[11,8,256]{2,1,0:T(8,128)S(1)} collective-permute-done((f32[11,8,256]{2,1,0:T(8,128)S(1)}, f32[11,8,256]{2,1,0:T(8,128)S(1)}, u32[]{:S(2)}, u32[]{:S(2)}) %collective-permute-start.6) | collective-permute-done | bytes 90144 | tf_op jit(solution)/shard_map/ppermute | solution.py:298
  43.6 3.3 %collective-permute-start.7 = (f32[11,8,256]{2,1,0:T(8,128)S(1)}, f32[11,8,256]{2,1,0:T(8,128)S(1)}, u32[]{:S(2)}, u32[]{:S(2)}) collective-permute-start(f32[11,8,256]{2,1,0:T(8,128)S(1)} %pad_maximum_fusion.2), channel_id=1, source_target_pairs={{0,4},{1,5},{2,6},{3,7},{4,0},{5,1},{6,2},{7,3},{8,12},{9,13},{10,... | collective-permute-start | bytes 270344 | tf_op jit(solution)/shard_map/ppermute | solution.py:298
  46.9 4.4 %collective-permute-done.7 = f32[11,8,256]{2,1,0:T(8,128)S(1)} collective-permute-done((f32[11,8,256]{2,1,0:T(8,128)S(1)}, f32[11,8,256]{2,1,0:T(8,128)S(1)}, u32[]{:S(2)}, u32[]{:S(2)}) %collective-permute-start.7) | collective-permute-done | bytes 90144 | tf_op jit(solution)/shard_map/ppermute | solution.py:298
  51.4 1.6 %collective-permute-start.8 = (f32[11,8,256]{2,1,0:T(8,128)S(1)}, f32[11,8,256]{2,1,0:T(8,128)S(1)}, u32[]{:S(2)}, u32[]{:S(2)}) collective-permute-start(f32[11,8,256]{2,1,0:T(8,128)S(1)} %pad_maximum_fusion.3), channel_id=1, source_target_pairs={{0,8},{8,0},{16,24},{24,16},{1,9},{9,1},{17,25},{25,17},{2,10},{10... | collective-permute-start | bytes 270344 | tf_op jit(solution)/shard_map/ppermute | solution.py:298
  53.0 3.0 %collective-permute-done.8 = f32[11,8,256]{2,1,0:T(8,128)S(1)} collective-permute-done((f32[11,8,256]{2,1,0:T(8,128)S(1)}, f32[11,8,256]{2,1,0:T(8,128)S(1)}, u32[]{:S(2)}, u32[]{:S(2)}) %collective-permute-start.8) | collective-permute-done | bytes 90144 | tf_op jit(solution)/shard_map/ppermute | solution.py:298
  56.1 1.2 %collective-permute-start.9 = (f32[11,8,256]{2,1,0:T(8,128)S(1)}, f32[11,8,256]{2,1,0:T(8,128)S(1)}, u32[]{:S(2)}, u32[]{:S(2)}) collective-permute-start(f32[11,8,256]{2,1,0:T(8,128)S(1)} %pad_maximum_fusion.4), channel_id=1, source_target_pairs={{0,16},{8,24},{16,0},{24,8},{1,17},{9,25},{17,1},{25,9},{2,18},{10... | collective-permute-start | bytes 270344 | tf_op jit(solution)/shard_map/ppermute | solution.py:298
  57.3 3.4 %collective-permute-done.9 = f32[11,8,256]{2,1,0:T(8,128)S(1)} collective-permute-done((f32[11,8,256]{2,1,0:T(8,128)S(1)}, f32[11,8,256]{2,1,0:T(8,128)S(1)}, u32[]{:S(2)}, u32[]{:S(2)}) %collective-permute-start.9) | collective-permute-done | bytes 90144 | tf_op jit(solution)/shard_map/ppermute | solution.py:298
  60.7 1.5 %shard_map.61 = (f32[10,8,256]{2,1,0:T(8,128)S(1)}, f32[2,8,256]{2,1,0:T(8,128)S(1)}, f32[8,256]{1,0:T(8,128)S(1)}, f32[8,128]{1,0:T(8,128)S(1)}) custom-call(s32[1,4]{1,0:T(1,128)S(1)} %copy-done.2, s32[1]{0:T(128)} %bitcast.me, f32[1,16,256]{2,1,0:T(8,128)S(1)} %slice.229.before, f32[8,16,256]{2,1,0:T(8,128)S(1)} %pad_maximum_fusion.table, ...), custom_call_target="tpu_custom_call" | custom-call | tf_op jit(solution)/shard_map/pallas_call | solution.py:361
  62.2 0.1 collective-permute-start.10
  62.3 1.2 %collective-permute-done.10 = f32[6,8,256]{2,1,0:T(8,128)S(1)} collective-permute-done((f32[6,8,256]{2,1,0:T(8,128)S(1)}, f32[6,8,256]{2,1,0:T(8,128)S(1)}, u32[]{:S(2)}, u32[]{:S(2)}) %collective-permute-start.10) | collective-permute-done | bytes 49184 | tf_op jit(solution)/shard_map/ppermute | solution.py:298
  63.6 0.4 collective-permute-start.11
  64.0 3.5 %collective-permute-done.11 = f32[4,8,256]{2,1,0:T(8,128)S(1)} collective-permute-done((f32[4,8,256]{2,1,0:T(8,128)S(1)}, f32[4,8,256]{2,1,0:T(8,128)S(1)}, u32[]{:S(2)}, u32[]{:S(2)}) %collective-permute-start.11) | collective-permute-done | bytes 32800 | tf_op jit(solution)/shard_map/ppermute | solution.py:298
  67.6 1.8 %collective-permute-start.12 = (f32[3,8,256]{2,1,0:T(8,128)S(1)}, f32[3,8,256]{2,1,0:T(8,128)S(1)}, u32[]{:S(2)}, u32[]{:S(2)}) collective-permute-start(f32[3,8,256]{2,1,0:T(8,128)S(1)} %pad_maximum_fusion.11), channel_id=1, source_target_pairs={{0,4},{1,5},{2,6},{3,7},{4,0},{5,1},{6,2},{7,3},{8,12},{9,13},{10,... | collective-permute-start | bytes 73736 | tf_op jit(solution)/shard_map/ppermute | solution.py:298
  69.4 3.0 %collective-permute-done.12 = f32[3,8,256]{2,1,0:T(8,128)S(1)} collective-permute-done((f32[3,8,256]{2,1,0:T(8,128)S(1)}, f32[3,8,256]{2,1,0:T(8,128)S(1)}, u32[]{:S(2)}, u32[]{:S(2)}) %collective-permute-start.12) | collective-permute-done | bytes 24608 | tf_op jit(solution)/shard_map/ppermute | solution.py:298
  72.4 1.6 %collective-permute-start.13 = (f32[3,8,256]{2,1,0:T(8,128)S(1)}, f32[3,8,256]{2,1,0:T(8,128)S(1)}, u32[]{:S(2)}, u32[]{:S(2)}) collective-permute-start(f32[3,8,256]{2,1,0:T(8,128)S(1)} %pad_maximum_fusion.12), channel_id=1, source_target_pairs={{0,8},{8,0},{16,24},{24,16},{1,9},{9,1},{17,25},{25,17},{2,10},{10... | collective-permute-start | bytes 73736 | tf_op jit(solution)/shard_map/ppermute | solution.py:298
  74.0 2.3 %collective-permute-done.13 = f32[3,8,256]{2,1,0:T(8,128)S(1)} collective-permute-done((f32[3,8,256]{2,1,0:T(8,128)S(1)}, f32[3,8,256]{2,1,0:T(8,128)S(1)}, u32[]{:S(2)}, u32[]{:S(2)}) %collective-permute-start.13) | collective-permute-done | bytes 24608 | tf_op jit(solution)/shard_map/ppermute | solution.py:298
  76.3 1.2 %collective-permute-start.14 = (f32[3,8,256]{2,1,0:T(8,128)S(1)}, f32[3,8,256]{2,1,0:T(8,128)S(1)}, u32[]{:S(2)}, u32[]{:S(2)}) collective-permute-start(f32[3,8,256]{2,1,0:T(8,128)S(1)} %pad_maximum_fusion.13), channel_id=1, source_target_pairs={{0,16},{8,24},{16,0},{24,8},{1,17},{9,25},{17,1},{25,9},{2,18},{10... | collective-permute-start | bytes 73736 | tf_op jit(solution)/shard_map/ppermute | solution.py:298
  77.6 2.7 %collective-permute-done.14 = f32[3,8,256]{2,1,0:T(8,128)S(1)} collective-permute-done((f32[3,8,256]{2,1,0:T(8,128)S(1)}, f32[3,8,256]{2,1,0:T(8,128)S(1)}, u32[]{:S(2)}, u32[]{:S(2)}) %collective-permute-start.14) | collective-permute-done | bytes 24608 | tf_op jit(solution)/shard_map/ppermute | solution.py:298
  80.2 1.0 %shard_map.62 = (f32[1,8,256]{2,1,0:T(8,128)}, f32[1,8,256]{2,1,0:T(8,128)}) custom-call(s32[1]{0:T(128)} %bitcast.me, f32[2,8,256]{2,1,0:T(8,128)S(1)} %slice_add_fusion.7.received, f32[1,8,256]{2,1,0:T(8,128)S(1)} %slice_select_fusion.6.shifted, f32[2,8,256]{2,1,0:T(8,128)S(1)} %get-tuple-element.13.images, f32[8,256]{1,0:T(8,128)S(1)} %get-tuple-element.14.residual, ...), custom_call_target="tpu_custom_call" | custom-call | tf_op jit(solution)/shard_map/pallas_call | solution.py:377
  (51 shorter events, 0.3 us)
Async XLA Ops:
  1.3 0.7 copy-start.1
  2.0 4.9 %collective-permute-start = (f32[2,16,256]{2,1,0:T(8,128)S(1)}, f32[2,16,256]{2,1,0:T(8,128)S(1)}, u32[]{:S(2)}, u32[]{:S(2)}) collective-permute-start(f32[2,16,256]{2,1,0:T(8,128)S(1)} %pad_maximum_fusion.7), channel_id=1, source_target_pairs={{0,16},{8,24},{16,0},{24,8},{1,17},{9,25},{17,1},{25,9},{2,18},{10... | collective-permute-start | bytes 98312 | tf_op jit(solution)/shard_map/ppermute | solution.py:298
  6.9 4.0 %collective-permute-start.1 = (f32[2,16,256]{2,1,0:T(8,128)S(1)}, f32[2,16,256]{2,1,0:T(8,128)S(1)}, u32[]{:S(2)}, u32[]{:S(2)}) collective-permute-start(f32[2,16,256]{2,1,0:T(8,128)S(1)} %pad_maximum_fusion.8), channel_id=1, source_target_pairs={{0,8},{8,0},{16,24},{24,16},{1,9},{9,1},{17,25},{25,17},{2,10},{10... | collective-permute-start | bytes 98312 | tf_op jit(solution)/shard_map/ppermute | solution.py:298
  10.9 5.2 %collective-permute-start.2 = (f32[2,16,256]{2,1,0:T(8,128)S(1)}, f32[2,16,256]{2,1,0:T(8,128)S(1)}, u32[]{:S(2)}, u32[]{:S(2)}) collective-permute-start(f32[2,16,256]{2,1,0:T(8,128)S(1)} %pad_maximum_fusion.9), channel_id=1, source_target_pairs={{0,4},{1,5},{2,6},{3,7},{4,0},{5,1},{6,2},{7,3},{8,12},{9,13},{10,... | collective-permute-start | bytes 98312 | tf_op jit(solution)/shard_map/ppermute | solution.py:298
  16.1 4.2 %collective-permute-start.3 = (f32[3,16,256]{2,1,0:T(8,128)S(1)}, f32[3,16,256]{2,1,0:T(8,128)S(1)}, u32[]{:S(2)}, u32[]{:S(2)}) collective-permute-start(f32[3,16,256]{2,1,0:T(8,128)S(1)} %pad_maximum_fusion.6), channel_id=1, source_target_pairs={{0,2},{1,3},{2,0},{3,1},{4,6},{5,7},{6,4},{7,5},{8,10},{9,11},{10,... | collective-permute-start | bytes 147464 | tf_op jit(solution)/shard_map/ppermute | solution.py:298
  20.2 1.3 %collective-permute-start.4 = (f32[5,16,256]{2,1,0:T(8,128)S(1)}, f32[5,16,256]{2,1,0:T(8,128)S(1)}, u32[]{:S(2)}, u32[]{:S(2)}) collective-permute-start(f32[5,16,256]{2,1,0:T(8,128)S(1)} %pad_maximum_fusion.5), channel_id=1, source_target_pairs={{0,1},{1,0},{2,3},{3,2},{4,5},{5,4},{6,7},{7,6},{8,9},{9,8},{10,11... | collective-permute-start | bytes 245768 | tf_op jit(solution)/shard_map/ppermute | solution.py:298
  21.6 0.7 copy-start
  21.6 0.7 copy-start.2
  37.0 1.3 %collective-permute-start.5 = (f32[11,8,256]{2,1,0:T(8,128)S(1)}, f32[11,8,256]{2,1,0:T(8,128)S(1)}, u32[]{:S(2)}, u32[]{:S(2)}) collective-permute-start(f32[11,8,256]{2,1,0:T(8,128)S(1)} %get-tuple-element.9.part), channel_id=1, source_target_pairs={{0,1},{1,0},{2,3},{3,2},{4,5},{5,4},{6,7},{7,6},{8,9},{9,8},{10,11... | collective-permute-start | bytes 270344 | tf_op jit(solution)/shard_map/ppermute | solution.py:298
  38.4 5.2 %collective-permute-start.6 = (f32[11,8,256]{2,1,0:T(8,128)S(1)}, f32[11,8,256]{2,1,0:T(8,128)S(1)}, u32[]{:S(2)}, u32[]{:S(2)}) collective-permute-start(f32[11,8,256]{2,1,0:T(8,128)S(1)} %pad_maximum_fusion.1), channel_id=1, source_target_pairs={{0,2},{1,3},{2,0},{3,1},{4,6},{5,7},{6,4},{7,5},{8,10},{9,11},{10,... | collective-permute-start | bytes 270344 | tf_op jit(solution)/shard_map/ppermute | solution.py:298
  43.6 7.8 %collective-permute-start.7 = (f32[11,8,256]{2,1,0:T(8,128)S(1)}, f32[11,8,256]{2,1,0:T(8,128)S(1)}, u32[]{:S(2)}, u32[]{:S(2)}) collective-permute-start(f32[11,8,256]{2,1,0:T(8,128)S(1)} %pad_maximum_fusion.2), channel_id=1, source_target_pairs={{0,4},{1,5},{2,6},{3,7},{4,0},{5,1},{6,2},{7,3},{8,12},{9,13},{10,... | collective-permute-start | bytes 270344 | tf_op jit(solution)/shard_map/ppermute | solution.py:298
  51.4 4.6 %collective-permute-start.8 = (f32[11,8,256]{2,1,0:T(8,128)S(1)}, f32[11,8,256]{2,1,0:T(8,128)S(1)}, u32[]{:S(2)}, u32[]{:S(2)}) collective-permute-start(f32[11,8,256]{2,1,0:T(8,128)S(1)} %pad_maximum_fusion.3), channel_id=1, source_target_pairs={{0,8},{8,0},{16,24},{24,16},{1,9},{9,1},{17,25},{25,17},{2,10},{10... | collective-permute-start | bytes 270344 | tf_op jit(solution)/shard_map/ppermute | solution.py:298
  56.1 4.6 %collective-permute-start.9 = (f32[11,8,256]{2,1,0:T(8,128)S(1)}, f32[11,8,256]{2,1,0:T(8,128)S(1)}, u32[]{:S(2)}, u32[]{:S(2)}) collective-permute-start(f32[11,8,256]{2,1,0:T(8,128)S(1)} %pad_maximum_fusion.4), channel_id=1, source_target_pairs={{0,16},{8,24},{16,0},{24,8},{1,17},{9,25},{17,1},{25,9},{2,18},{10... | collective-permute-start | bytes 270344 | tf_op jit(solution)/shard_map/ppermute | solution.py:298
  62.2 1.3 %collective-permute-start.10 = (f32[6,8,256]{2,1,0:T(8,128)S(1)}, f32[6,8,256]{2,1,0:T(8,128)S(1)}, u32[]{:S(2)}, u32[]{:S(2)}) collective-permute-start(f32[6,8,256]{2,1,0:T(8,128)S(1)} %concatenate.72), channel_id=1, source_target_pairs={{0,1},{1,0},{2,3},{3,2},{4,5},{5,4},{6,7},{7,6},{8,9},{9,8},{10,11... | collective-permute-start | bytes 147464 | tf_op jit(solution)/shard_map/ppermute | solution.py:298
  63.6 4.0 %collective-permute-start.11 = (f32[4,8,256]{2,1,0:T(8,128)S(1)}, f32[4,8,256]{2,1,0:T(8,128)S(1)}, u32[]{:S(2)}, u32[]{:S(2)}) collective-permute-start(f32[4,8,256]{2,1,0:T(8,128)S(1)} %pad_maximum_fusion.10), channel_id=1, source_target_pairs={{0,2},{1,3},{2,0},{3,1},{4,6},{5,7},{6,4},{7,5},{8,10},{9,11},{10,... | collective-permute-start | bytes 98312 | tf_op jit(solution)/shard_map/ppermute | solution.py:298
  67.6 4.8 %collective-permute-start.12 = (f32[3,8,256]{2,1,0:T(8,128)S(1)}, f32[3,8,256]{2,1,0:T(8,128)S(1)}, u32[]{:S(2)}, u32[]{:S(2)}) collective-permute-start(f32[3,8,256]{2,1,0:T(8,128)S(1)} %pad_maximum_fusion.11), channel_id=1, source_target_pairs={{0,4},{1,5},{2,6},{3,7},{4,0},{5,1},{6,2},{7,3},{8,12},{9,13},{10,... | collective-permute-start | bytes 73736 | tf_op jit(solution)/shard_map/ppermute | solution.py:298
  72.4 3.9 %collective-permute-start.13 = (f32[3,8,256]{2,1,0:T(8,128)S(1)}, f32[3,8,256]{2,1,0:T(8,128)S(1)}, u32[]{:S(2)}, u32[]{:S(2)}) collective-permute-start(f32[3,8,256]{2,1,0:T(8,128)S(1)} %pad_maximum_fusion.12), channel_id=1, source_target_pairs={{0,8},{8,0},{16,24},{24,16},{1,9},{9,1},{17,25},{25,17},{2,10},{10... | collective-permute-start | bytes 73736 | tf_op jit(solution)/shard_map/ppermute | solution.py:298
  76.3 3.9 %collective-permute-start.14 = (f32[3,8,256]{2,1,0:T(8,128)S(1)}, f32[3,8,256]{2,1,0:T(8,128)S(1)}, u32[]{:S(2)}, u32[]{:S(2)}) collective-permute-start(f32[3,8,256]{2,1,0:T(8,128)S(1)} %pad_maximum_fusion.13), channel_id=1, source_target_pairs={{0,16},{8,24},{16,0},{24,8},{1,17},{9,25},{17,1},{25,9},{2,18},{10... | collective-permute-start | bytes 73736 | tf_op jit(solution)/shard_map/ppermute | solution.py:298

commit v6 on v5

--- a/solution.py
+++ b/solution.py
@@ -127,19 +127,40 @@
     return jnp.concatenate(parts, axis=0)
 
 
-def scaled_places(entry, fields):
-    return entry[fields:] * (SQRT_THREE / SCALE_LENGTH)
+def half_place(index, me, coarse):
+    return index ^ ((me & 1) * (coarse // 2))
 
 
 def live_of(index):
     return (index >= 0).astype(F32)
 
 
-def pack_kernel(sizes, locations, observed, packed):
-    fields = sizes[0]
-    packed[...] = jnp.zeros_like(packed)
-    packed[:fields] = observed[0]
-    packed[fields : fields + 3] = locations[0]
+def pack_kernel(sizes, locations, observed, noise, nbr, packed, noise_out, nbr_out, done):
+    fields, points, coarse, slots = sizes
+    pieces = points // LANES
+    first = fields * pieces
+    packed[first:] = jnp.zeros((4 * pieces, LANES), F32)
+    copies = []
+    for at in range(pieces):
+        lanes = pl.ds(at * LANES, LANES)
+        copies.append((observed.at[0, :, lanes], packed.at[pl.ds(at * fields, fields)]))
+        copies.append((locations.at[0, :, lanes], packed.at[pl.ds(first + 4 * at, 3)]))
+    copies += [(noise, noise_out), (nbr, nbr_out)]
+    copies = [pltpu.make_async_copy(*copy, done.at[at]) for at, copy in enumerate(copies)]
+    for copy in copies:
+        copy.start()
+    for copy in copies:
+        copy.wait()
+
+
+def fields_of(entry, fields, points):
+    return jnp.concatenate([entry[at * fields : (at + 1) * fields] for at in range(points // LANES)], axis=1)
+
+
+def places_of(entry, fields, points):
+    pieces = points // LANES
+    rows = [entry[fields * pieces + 4 * at :][:4] for at in range(pieces)]
+    return jnp.concatenate(rows, axis=1) * (SQRT_THREE / SCALE_LENGTH)
 
 
 def factor_kernel(sizes, nbr, me, before, table, mine, noise, part, back_out, last_out, columns, lower, ahead, guess):
@@ -152,9 +173,9 @@
     entries += [table[mirrored(jnp.maximum(index, 0) ^ here, coarse)] for index in ids[1:own]]
     entries += [mine[...]]
     live = [live_of(index) for index in ids]
-    values = [entry[:fields] * alive for entry, alive in zip(entries, live)]
-    places = [scaled_places(entry, fields) for entry in entries]
-    turned = [jnp.transpose(place) for place in places]
+    values = [fields_of(entry, fields, points) * alive for entry, alive in zip(entries, live)]
+    places = [places_of(entry, fields, points) for entry in entries]
+    turned = [jnp.transpose(jnp.concatenate([place, place], axis=0)) for place in places]
 
     def at(i, end=None):
         return pl.ds(i * points, ((i + 1 if end is None else end) - i) * points)
@@ -181,9 +202,9 @@
         back_out[:, k * points : (k + 1) * points] = total
     last = inverse(columns[own, at(own)], ahead, guess)
     last_out[...] = last
-    back = {k: back_out[:, k * points : (k + 1) * points] for k in range(own)}
-
-    middle, spread, slot_parts = apply_block(values, back, last)
+    back = {k: split(back_out[:, k * points : (k + 1) * points]) for k in range(own)}
+
+    middle, spread, slot_parts = apply_block(values, back, split(last))
     own_part = spread + noise[0] * values[own]
     part[...] = jnp.zeros_like(part)
     product = jnp.sum(middle * spread + noise[0] * values[own] * values[own], axis=1, keepdims=True)
@@ -195,7 +216,8 @@
 
         @pl.when((index >= 0) & (index < coarse))
         def _(index=index, value=value):
-            part[index] = part[index] + value
+            place = half_place(index, me[0], coarse)
+            part[place] = part[place] + value
 
 
 def in_lanes(columns, shape):
@@ -210,38 +232,42 @@
     own = len(values) - 1
     middle = values[own]
     for k in range(own):
-        middle = taken(middle, split(values[k]), split(back[k]), NT)
-    spread = -taken(jnp.zeros_like(middle), split(middle), split(last))
+        middle = taken(middle, split(values[k]), back[k], NT)
+    spread = -taken(jnp.zeros_like(middle), split(middle), last)
     spread_parts = split(spread)
-    slot_parts = [taken(jnp.zeros_like(middle), spread_parts, split(back[k])) for k in range(own)]
+    slot_parts = [taken(jnp.zeros_like(middle), spread_parts, back[k]) for k in range(own)]
     return middle, spread, slot_parts
 
 
 def step_kernel(
-    sizes, nbr, me, before, table, mine, noise, part, summed, shifted, back, last, sends, image_out, residual_out, ratio_out
+    sizes, nbr, me, before, table, mine, noise, part, rows, other_rows, scalars, near, far, back, last,
+    sends, image_out, residual_out, ratio_out,
 ):
     fields, points, coarse, slots = sizes
     used = slot_list(slots)
     own = len(used)
     ids = [nbr[0, slot] for slot in used] + [me[0]]
     here = lax.rem(me[0], coarse)
-    product = summed[coarse][:, 0:1]
-    norm_now = summed[coarse][:, 1:2]
+    product = scalars[0, :, 0:1]
+    norm_now = scalars[0, :, 1:2]
     alpha = norm_now / product
+    half = coarse // 2
+    even = (me[0] & 1) == 0
     values = []
     for at, index in enumerate(ids):
-        image = summed[jnp.clip(index, 0, coarse - 1)]
+        place = half_place(jnp.clip(index, 0, coarse - 1), me[0], coarse)
+        image = jnp.where(place < half, rows[place & (half - 1)], other_rows[place & (half - 1)])
         if at == 0:
-            observed = before[0, :fields]
-            image = jnp.where(index < coarse, image, shifted[0] + part[coarse + 2])
+            entry = before[0]
+            image = jnp.where(index < coarse, image, jnp.where(even, far[0], near[0]) + part[coarse + 2])
         elif at == own:
-            observed = mine[:fields]
-            image = jnp.where(index < coarse, image, part[coarse + 1] + shifted[1])
+            entry = mine[...]
+            image = jnp.where(index < coarse, image, part[coarse + 1] + jnp.where(even, near[0], far[0]))
         else:
-            observed = table[mirrored(jnp.maximum(index, 0) ^ here, coarse)][:fields]
-        values.append((observed - alpha * image) * live_of(index))
-    back_parts = {k: back[:, k * points : (k + 1) * points] for k in range(own)}
-    middle, spread, slot_parts = apply_block(values, back_parts, last[...])
+            entry = table[mirrored(jnp.maximum(index, 0) ^ here, coarse)]
+        values.append((fields_of(entry, fields, points) - alpha * image) * live_of(index))
+    back_parts = {k: split(back[:, k * points : (k + 1) * points]) for k in range(own)}
+    middle, spread, slot_parts = apply_block(values, back_parts, split(last[...]))
     residual = values[own]
     inner = jnp.sum(middle * spread + noise[0] * residual * residual, axis=1, keepdims=True)
     cross = jnp.sum(residual * image, axis=1, keepdims=True)
@@ -272,7 +298,7 @@
     beta = norm_now / norm_first
     product = inner + beta * (2.0 * cross + beta * product_first)
     step = norm_now / product
-    observed = mine[:fields]
+    observed = fields_of(mine[...], fields, points)
     direction = residual[...] + beta * observed
     solution_out[0] = alpha * observed + step * direction
     residual_out[0] = residual[...] - step * (spread + beta * images[0])
@@ -281,7 +307,7 @@
 def call(kernel, sizes, outs, in_spaces, scratch=()):
     return pl.pallas_call(
         functools.partial(kernel, sizes),
-        out_shape=[jax.ShapeDtypeStruct(shape, F32) for shape in outs],
+        out_shape=[out if hasattr(out, "dtype") else jax.ShapeDtypeStruct(out, F32) for out in outs],
         in_specs=[pl.BlockSpec(memory_space=space) for space in in_spaces],
         out_specs=[pl.BlockSpec(memory_space=pltpu.VMEM)] * len(outs),
         scratch_shapes=list(scratch),
@@ -307,17 +333,11 @@
     return steps
 
 
-def carry(shifted, ends, got, me, bit, kinds):
-    low, upper = me & ((1 << bit) - 1), ((me >> bit) & 1) == 1
-    new_shifted, new_ends = [], []
-    for at, kind in enumerate(kinds):
-        if kind == 1:
-            takes, keeps = upper & (low == 0), upper
-        else:
-            takes, keeps = ~upper & (low == (1 << bit) - 1), ~upper
-        new_shifted.append(jnp.where(takes, got[at], shifted[at]))
-        new_ends.append(jnp.where(keeps, ends[at], got[at]))
-    return jnp.stack(new_shifted), jnp.stack(new_ends)
+def carry(shifted, ends, got, number, bit, down):
+    full = (1 << bit) - 1
+    low, upper = number & full, ((number >> bit) & 1) == 1
+    takes = jnp.where(down, ~upper & (low == full), upper & (low == 0))
+    return jnp.where(takes, got, shifted), jnp.where(upper ^ down, ends, got)
 
 
 def local(locations, neighbours, observations, noise_prec):
@@ -328,13 +348,20 @@
     coarse = lax.axis_size("dev")
     sizes = (fields, points, coarse, slots)
     depth = len(slot_list(slots)) * points
+    pieces = points // LANES
     me = lax.axis_index(AXES).astype(jnp.int32)
     group = lax.axis_index("grp")
     smem, vmem = pltpu.SMEM, pltpu.VMEM
     square, tile = (points, points), (fields, points)
     steps = exchanges()
 
-    (mine,) = call(pack_kernel, sizes, [(2 * fields, points)], [vmem, vmem])(locations, observations)
+    mine, noise, nbr = call(
+        pack_kernel,
+        sizes,
+        [((fields + 4) * pieces, LANES), noise_prec, neighbours],
+        [pl.ANY] * 4,
+        [pltpu.SemaphoreType.DMA((2 * pieces + 2,))],
+    )(locations, observations, noise_prec, neighbours)
     before, table = mine[None], mine[None]
     for axis, reach, bit in steps[::-1]:
         got = swapped(jnp.concatenate([table, before], axis=0), axis, reach)
@@ -351,19 +378,24 @@
         [(coarse + 3,) + tile, (points, depth), square],
         [smem, smem] + [vmem] * 4,
         [pltpu.VMEM((slots, slots * points, points), F32)] * 2 + [pltpu.VMEM(square, F32)] * 2,
-    )(neighbours, at, before, table, mine, noise_prec)
-
-    summed, ends, shifted = part[:-2], part[-2:], jnp.zeros_like(part[-2:])
-    for axis, reach, bit in steps:
-        got = swapped(jnp.concatenate([summed, ends], axis=0), axis, reach)
-        summed = summed + got[:-2]
-        shifted, ends = carry(shifted, ends, got[-2:], me, bit, (1, -1))
+    )(nbr, at, before, table, mine, noise)
+
+    half, odd = coarse // 2, (me & 1) == 1
+    got = swapped(part[half:], "dev", 1)
+    rows, scalars = part[:half] + got[:half], part[coarse : coarse + 1] + got[half : half + 1]
+    up, down = got[half + 1 : half + 2], got[half + 2 :]
+    near, ends, far = jnp.where(odd, up, down), jnp.where(odd, down, up), jnp.zeros_like(up)
+    for axis, reach, bit in steps[1:]:
+        got = swapped(jnp.concatenate([rows, scalars, ends], axis=0), axis, reach)
+        rows, scalars = rows + got[:half], scalars + got[half : half + 1]
+        far, ends = carry(far, ends, got[half + 1 :], me >> 1, bit - 1, odd)
+    other_rows = swapped(rows, "dev", 1)
     sends, images, residual, ratios = call(
         step_kernel,
         sizes,
         [(coarse + 2,) + tile, (2,) + tile, tile, (fields, LANES)],
-        [smem, smem] + [vmem] * 9,
-    )(neighbours, at, before, table, mine, noise_prec, part, summed, shifted, back, last)
+        [smem, smem] + [vmem] * 12,
+    )(nbr, at, before, table, mine, noise, part, rows, other_rows, scalars, near, far, back, last)
 
     summed, ends, shifted = sends[:-1], sends[-1:], jnp.zeros_like(sends[-1:])
     for axis, reach, bit in steps:
@@ -372,7 +404,7 @@
         if axis == "dev":
             summed = jnp.concatenate([summed[:kept], summed[-1:]], axis=0)
         summed = summed + got[:-1]
-        shifted, ends = carry(shifted, ends, got[-1:], me, bit, (-1,))
+        shifted, ends = carry(shifted, ends, got[-1:], me, bit, True)
     return tuple(
         call(finish_kernel, sizes, [observations.shape] * 2, [smem] + [vmem] * 6)(
             at, summed, shifted, images, residual, ratios, mine

time: 81.3 us -> 78.5 us (0.966)
  waiting for transfers between devices: 37 us -> 29.9 us
  starting transfers between devices: 23.8 us -> 27.7 us
    ppermute x15 -> x16, waiting for transfers between devices: 37 us -> 29.9 us  [swapped(): lax.ppermute(value, axis, [(at, at ^ reach) for at in range(lax.axis_size...]
    ppermute x15 -> x16, starting transfers between devices: 23.8 us -> 27.7 us  [swapped(): lax.ppermute(value, axis, [(at, at ^ reach) for at in range(lax.axis_size...]
  transfers between devices with their start and end apart: 15 -> 16, of which waited for: 15 -> 16; matrix products, arithmetic and copies ran while one was open for 0% -> 0% of each run, Pallas kernels for 0% -> 0%
where the time goes in v6:
time: 78.5 us; the launch traced here: 78.2 us
  waiting for transfers between devices  29.9 us (38%)
  starting transfers between devices  27.7 us (35%)
  Pallas kernels  17.3 us (22%)
  local copies, waits for them, and re-layouts  2.17 us (3%)
  between operations  0.83 us (1%)
    ppermute x16, waiting for transfers between devices, swapped(): lax.ppermute(value, axis, [(at, at ^ reach) for at in range(lax.axis_size...  29.9 us
    ppermute x16, starting transfers between devices, swapped(): lax.ppermute(value, axis, [(at, at ^ reach) for at in range(lax.axis_size...  27.7 us
    pallas_call x1, Pallas kernels, local(): call(factor_kernel, sizes, [(coarse + 3,) + tile, (points, depth), square...  14.7 us
    unnamed x7, local copies, waits for them, and re-layouts  2.09 us
  transfers between devices with their start and end apart: 16, of which 16 were waited for; matrix products, arithmetic and copies ran while one was open for 0% of the time, Pallas kernels for 0%

profile of v6, /device:TPU:0, one launch (start us, length us, event | category | flops | bytes accessed | tf_op | source)
XLA Modules:
  0.0 78.2 jit_solution(14037614119232783281)
XLA Ops:
  0.6 0.0 copy-start.2
  0.6 0.7 copy.6.locations
  1.3 0.0 copy-done.2
  1.3 0.0 copy-start
  1.3 0.7 copy-done
  2.0 0.0 copy-start.1
  2.0 0.7 copy-done.1
  2.7 0.1 shard_map.59
  2.8 3.0 %collective-permute-start = (f32[2,24,128]{2,1,0:T(8,128)S(1)}, f32[2,24,128]{2,1,0:T(8,128)S(1)}, u32[]{:S(2)}, u32[]{:S(2)}) collective-permute-start(f32[2,24,128]{2,1,0:T(8,128)S(1)} %pad_maximum_fusion.8), channel_id=1, source_target_pairs={{0,16},{8,24},{16,0},{24,8},{1,17},{9,25},{17,1},{25,9},{2,18},{10... | collective-permute-start | bytes 73736 | tf_op jit(solution)/shard_map/ppermute | solution.py:324
  5.9 1.8 %collective-permute-done = f32[2,24,128]{2,1,0:T(8,128)S(1)} collective-permute-done((f32[2,24,128]{2,1,0:T(8,128)S(1)}, f32[2,24,128]{2,1,0:T(8,128)S(1)}, u32[]{:S(2)}, u32[]{:S(2)}) %collective-permute-start) | collective-permute-done | bytes 24608 | tf_op jit(solution)/shard_map/ppermute | solution.py:324
  7.7 2.1 %collective-permute-start.1 = (f32[2,24,128]{2,1,0:T(8,128)S(1)}, f32[2,24,128]{2,1,0:T(8,128)S(1)}, u32[]{:S(2)}, u32[]{:S(2)}) collective-permute-start(f32[2,24,128]{2,1,0:T(8,128)S(1)} %pad_maximum_fusion.9), channel_id=1, source_target_pairs={{0,8},{8,0},{16,24},{24,16},{1,9},{9,1},{17,25},{25,17},{2,10},{10... | collective-permute-start | bytes 73736 | tf_op jit(solution)/shard_map/ppermute | solution.py:324
  9.7 1.8 %collective-permute-done.1 = f32[2,24,128]{2,1,0:T(8,128)S(1)} collective-permute-done((f32[2,24,128]{2,1,0:T(8,128)S(1)}, f32[2,24,128]{2,1,0:T(8,128)S(1)}, u32[]{:S(2)}, u32[]{:S(2)}) %collective-permute-start.1) | collective-permute-done | bytes 24608 | tf_op jit(solution)/shard_map/ppermute | solution.py:324
  11.6 3.2 %collective-permute-start.2 = (f32[2,24,128]{2,1,0:T(8,128)S(1)}, f32[2,24,128]{2,1,0:T(8,128)S(1)}, u32[]{:S(2)}, u32[]{:S(2)}) collective-permute-start(f32[2,24,128]{2,1,0:T(8,128)S(1)} %pad_maximum_fusion.10), channel_id=1, source_target_pairs={{0,4},{1,5},{2,6},{3,7},{4,0},{5,1},{6,2},{7,3},{8,12},{9,13},{10,... | collective-permute-start | bytes 73736 | tf_op jit(solution)/shard_map/ppermute | solution.py:324
  14.7 1.8 %collective-permute-done.2 = f32[2,24,128]{2,1,0:T(8,128)S(1)} collective-permute-done((f32[2,24,128]{2,1,0:T(8,128)S(1)}, f32[2,24,128]{2,1,0:T(8,128)S(1)}, u32[]{:S(2)}, u32[]{:S(2)}) %collective-permute-start.2) | collective-permute-done | bytes 24608 | tf_op jit(solution)/shard_map/ppermute | solution.py:324
  16.6 2.0 %collective-permute-start.3 = (f32[3,24,128]{2,1,0:T(8,128)S(1)}, f32[3,24,128]{2,1,0:T(8,128)S(1)}, u32[]{:S(2)}, u32[]{:S(2)}) collective-permute-start(f32[3,24,128]{2,1,0:T(8,128)S(1)} %pad_maximum_fusion.6), channel_id=1, source_target_pairs={{0,2},{1,3},{2,0},{3,1},{4,6},{5,7},{6,4},{7,5},{8,10},{9,11},{10,... | collective-permute-start | bytes 110600 | tf_op jit(solution)/shard_map/ppermute | solution.py:324
  18.5 2.1 %collective-permute-done.3 = f32[3,24,128]{2,1,0:T(8,128)S(1)} collective-permute-done((f32[3,24,128]{2,1,0:T(8,128)S(1)}, f32[3,24,128]{2,1,0:T(8,128)S(1)}, u32[]{:S(2)}, u32[]{:S(2)}) %collective-permute-start.3) | collective-permute-done | bytes 36896 | tf_op jit(solution)/shard_map/ppermute | solution.py:324
  20.6 0.1 collective-permute-start.4
  20.7 1.2 %collective-permute-done.4 = f32[5,24,128]{2,1,0:T(8,128)S(1)} collective-permute-done((f32[5,24,128]{2,1,0:T(8,128)S(1)}, f32[5,24,128]{2,1,0:T(8,128)S(1)}, u32[]{:S(2)}, u32[]{:S(2)}) %collective-permute-start.4) | collective-permute-done | bytes 61472 | tf_op jit(solution)/shard_map/ppermute | solution.py:324
  21.9 14.7 %shard_map.60 = (f32[11,8,256]{2,1,0:T(8,128)S(1)}, f32[256,768]{1,0:T(8,128)S(1)}, f32[256,256]{1,0:T(8,128)S(1)}) custom-call(s32[1,4]{1,0:T(1,128)S(1)} %get-tuple-element.12.nbr, s32[1]{0:T(128)} %bitcast.me, f32[1,24,128]{2,1,0:T(8,128)S(1)} %slice.206.before, f32[8,24,128]{2,1,0:T(8,128)S(1)} %pad_maximum_fusion.table, ...), custom_call_target="tpu_custom_call" | custom-call | tf_op jit(solution)/shard_map/pallas_call | solution.py:375
  36.7 0.6 collective-permute-start.5
  37.3 0.9 %collective-permute-done.5 = f32[7,8,256]{2,1,0:T(8,128)S(1)} collective-permute-done((f32[7,8,256]{2,1,0:T(8,128)S(1)}, f32[7,8,256]{2,1,0:T(8,128)S(1)}, u32[]{:S(2)}, u32[]{:S(2)}) %collective-permute-start.5) | collective-permute-done | bytes 57376 | tf_op jit(solution)/shard_map/ppermute | solution.py:324
  38.2 2.5 %collective-permute-start.6 = (f32[6,8,256]{2,1,0:T(8,128)S(1)}, f32[6,8,256]{2,1,0:T(8,128)S(1)}, u32[]{:S(2)}, u32[]{:S(2)}) collective-permute-start(f32[6,8,256]{2,1,0:T(8,128)S(1)} %pad_maximum_fusion.2), channel_id=1, source_target_pairs={{0,2},{1,3},{2,0},{3,1},{4,6},{5,7},{6,4},{7,5},{8,10},{9,11},{10,... | collective-permute-start | bytes 147464 | tf_op jit(solution)/shard_map/ppermute | solution.py:324
  40.8 2.1 %collective-permute-done.6 = f32[6,8,256]{2,1,0:T(8,128)S(1)} collective-permute-done((f32[6,8,256]{2,1,0:T(8,128)S(1)}, f32[6,8,256]{2,1,0:T(8,128)S(1)}, u32[]{:S(2)}, u32[]{:S(2)}) %collective-permute-start.6) | collective-permute-done | bytes 49184 | tf_op jit(solution)/shard_map/ppermute | solution.py:324
  42.9 3.1 %collective-permute-start.7 = (f32[6,8,256]{2,1,0:T(8,128)S(1)}, f32[6,8,256]{2,1,0:T(8,128)S(1)}, u32[]{:S(2)}, u32[]{:S(2)}) collective-permute-start(f32[6,8,256]{2,1,0:T(8,128)S(1)} %pad_maximum_fusion.3), channel_id=1, source_target_pairs={{0,4},{1,5},{2,6},{3,7},{4,0},{5,1},{6,2},{7,3},{8,12},{9,13},{10,... | collective-permute-start | bytes 147464 | tf_op jit(solution)/shard_map/ppermute | solution.py:324
  46.0 2.1 %collective-permute-done.7 = f32[6,8,256]{2,1,0:T(8,128)S(1)} collective-permute-done((f32[6,8,256]{2,1,0:T(8,128)S(1)}, f32[6,8,256]{2,1,0:T(8,128)S(1)}, u32[]{:S(2)}, u32[]{:S(2)}) %collective-permute-start.7) | collective-permute-done | bytes 49184 | tf_op jit(solution)/shard_map/ppermute | solution.py:324
  48.1 1.5 %collective-permute-start.8 = (f32[6,8,256]{2,1,0:T(8,128)S(1)}, f32[6,8,256]{2,1,0:T(8,128)S(1)}, u32[]{:S(2)}, u32[]{:S(2)}) collective-permute-start(f32[6,8,256]{2,1,0:T(8,128)S(1)} %pad_maximum_fusion.4), channel_id=1, source_target_pairs={{0,8},{8,0},{16,24},{24,16},{1,9},{9,1},{17,25},{25,17},{2,10},{10... | collective-permute-start | bytes 147464 | tf_op jit(solution)/shard_map/ppermute | solution.py:324
  49.6 2.7 %collective-permute-done.8 = f32[6,8,256]{2,1,0:T(8,128)S(1)} collective-permute-done((f32[6,8,256]{2,1,0:T(8,128)S(1)}, f32[6,8,256]{2,1,0:T(8,128)S(1)}, u32[]{:S(2)}, u32[]{:S(2)}) %collective-permute-start.8) | collective-permute-done | bytes 49184 | tf_op jit(solution)/shard_map/ppermute | solution.py:324
  52.3 1.5 %collective-permute-start.9 = (f32[6,8,256]{2,1,0:T(8,128)S(1)}, f32[6,8,256]{2,1,0:T(8,128)S(1)}, u32[]{:S(2)}, u32[]{:S(2)}) collective-permute-start(f32[6,8,256]{2,1,0:T(8,128)S(1)} %pad_maximum_fusion.5), channel_id=1, source_target_pairs={{0,16},{8,24},{16,0},{24,8},{1,17},{9,25},{17,1},{25,9},{2,18},{10... | collective-permute-start | bytes 147464 | tf_op jit(solution)/shard_map/ppermute | solution.py:324
  53.8 2.6 %collective-permute-done.9 = f32[6,8,256]{2,1,0:T(8,128)S(1)} collective-permute-done((f32[6,8,256]{2,1,0:T(8,128)S(1)}, f32[6,8,256]{2,1,0:T(8,128)S(1)}, u32[]{:S(2)}, u32[]{:S(2)}) %collective-permute-start.9) | collective-permute-done | bytes 49184 | tf_op jit(solution)/shard_map/ppermute | solution.py:324
  56.4 0.0 collective-permute-start.10
  56.4 1.2 %collective-permute-done.10.other_rows = f32[4,8,256]{2,1,0:T(8,128)S(1)} collective-permute-done((f32[4,8,256]{2,1,0:T(8,128)S(1)}, f32[4,8,256]{2,1,0:T(8,128)S(1)}, u32[]{:S(2)}, u32[]{:S(2)}) %collective-permute-start.10) | collective-permute-done | bytes 32800 | tf_op jit(solution)/shard_map/ppermute | solution.py:324
  57.6 1.5 %shard_map.61 = (f32[10,8,256]{2,1,0:T(8,128)S(1)}, f32[2,8,256]{2,1,0:T(8,128)S(1)}, f32[8,256]{1,0:T(8,128)S(1)}, f32[8,128]{1,0:T(8,128)S(1)}) custom-call(s32[1,4]{1,0:T(1,128)S(1)} %get-tuple-element.12.nbr, s32[1]{0:T(128)} %bitcast.me, f32[1,24,128]{2,1,0:T(8,128)S(1)} %slice.206.before, f32[8,24,128]{2,1,0:T(8,128)S(1)} %pad_maximum_fusion.table, ...), custom_call_target="tpu_custom_call" | custom-call | tf_op jit(solution)/shard_map/pallas_call | solution.py:393
  59.1 0.2 collective-permute-start.11
  59.4 1.1 %collective-permute-done.11 = f32[6,8,256]{2,1,0:T(8,128)S(1)} collective-permute-done((f32[6,8,256]{2,1,0:T(8,128)S(1)}, f32[6,8,256]{2,1,0:T(8,128)S(1)}, u32[]{:S(2)}, u32[]{:S(2)}) %collective-permute-start.11) | collective-permute-done | bytes 49184 | tf_op jit(solution)/shard_map/ppermute | solution.py:324
  60.5 2.0 %collective-permute-start.12 = (f32[4,8,256]{2,1,0:T(8,128)S(1)}, f32[4,8,256]{2,1,0:T(8,128)S(1)}, u32[]{:S(2)}, u32[]{:S(2)}) collective-permute-start(f32[4,8,256]{2,1,0:T(8,128)S(1)} %pad_maximum_fusion.7), channel_id=1, source_target_pairs={{0,2},{1,3},{2,0},{3,1},{4,6},{5,7},{6,4},{7,5},{8,10},{9,11},{10,... | collective-permute-start | bytes 98312 | tf_op jit(solution)/shard_map/ppermute | solution.py:324
  62.4 2.0 %collective-permute-done.12 = f32[4,8,256]{2,1,0:T(8,128)S(1)} collective-permute-done((f32[4,8,256]{2,1,0:T(8,128)S(1)}, f32[4,8,256]{2,1,0:T(8,128)S(1)}, u32[]{:S(2)}, u32[]{:S(2)}) %collective-permute-start.12) | collective-permute-done | bytes 32800 | tf_op jit(solution)/shard_map/ppermute | solution.py:324
  64.5 3.0 %collective-permute-start.13 = (f32[3,8,256]{2,1,0:T(8,128)S(1)}, f32[3,8,256]{2,1,0:T(8,128)S(1)}, u32[]{:S(2)}, u32[]{:S(2)}) collective-permute-start(f32[3,8,256]{2,1,0:T(8,128)S(1)} %pad_maximum_fusion.11), channel_id=1, source_target_pairs={{0,4},{1,5},{2,6},{3,7},{4,0},{5,1},{6,2},{7,3},{8,12},{9,13},{10,... | collective-permute-start | bytes 73736 | tf_op jit(solution)/shard_map/ppermute | solution.py:324
  67.5 1.8 %collective-permute-done.13 = f32[3,8,256]{2,1,0:T(8,128)S(1)} collective-permute-done((f32[3,8,256]{2,1,0:T(8,128)S(1)}, f32[3,8,256]{2,1,0:T(8,128)S(1)}, u32[]{:S(2)}, u32[]{:S(2)}) %collective-permute-start.13) | collective-permute-done | bytes 24608 | tf_op jit(solution)/shard_map/ppermute | solution.py:324
  69.3 1.5 %collective-permute-start.14 = (f32[3,8,256]{2,1,0:T(8,128)S(1)}, f32[3,8,256]{2,1,0:T(8,128)S(1)}, u32[]{:S(2)}, u32[]{:S(2)}) collective-permute-start(f32[3,8,256]{2,1,0:T(8,128)S(1)} %pad_maximum_fusion.12), channel_id=1, source_target_pairs={{0,8},{8,0},{16,24},{24,16},{1,9},{9,1},{17,25},{25,17},{2,10},{10... | collective-permute-start | bytes 73736 | tf_op jit(solution)/shard_map/ppermute | solution.py:324
  70.8 2.4 %collective-permute-done.14 = f32[3,8,256]{2,1,0:T(8,128)S(1)} collective-permute-done((f32[3,8,256]{2,1,0:T(8,128)S(1)}, f32[3,8,256]{2,1,0:T(8,128)S(1)}, u32[]{:S(2)}, u32[]{:S(2)}) %collective-permute-start.14) | collective-permute-done | bytes 24608 | tf_op jit(solution)/shard_map/ppermute | solution.py:324
  73.3 1.5 %collective-permute-start.15 = (f32[3,8,256]{2,1,0:T(8,128)S(1)}, f32[3,8,256]{2,1,0:T(8,128)S(1)}, u32[]{:S(2)}, u32[]{:S(2)}) collective-permute-start(f32[3,8,256]{2,1,0:T(8,128)S(1)} %pad_maximum_fusion.13), channel_id=1, source_target_pairs={{0,16},{8,24},{16,0},{24,8},{1,17},{9,25},{17,1},{25,9},{2,18},{10... | collective-permute-start | bytes 73736 | tf_op jit(solution)/shard_map/ppermute | solution.py:324
  74.8 2.4 %collective-permute-done.15 = f32[3,8,256]{2,1,0:T(8,128)S(1)} collective-permute-done((f32[3,8,256]{2,1,0:T(8,128)S(1)}, f32[3,8,256]{2,1,0:T(8,128)S(1)}, u32[]{:S(2)}, u32[]{:S(2)}) %collective-permute-start.15) | collective-permute-done | bytes 24608 | tf_op jit(solution)/shard_map/ppermute | solution.py:324
  77.2 1.0 %shard_map.62 = (f32[1,8,256]{2,1,0:T(8,128)}, f32[1,8,256]{2,1,0:T(8,128)}) custom-call(s32[1]{0:T(128)} %bitcast.me, f32[2,8,256]{2,1,0:T(8,128)S(1)} %slice_add_fusion.7.received, f32[1,8,256]{2,1,0:T(8,128)S(1)} %slice_select_fusion.6.shifted, f32[2,8,256]{2,1,0:T(8,128)S(1)} %get-tuple-element.19.images, f32[8,256]{1,0:T(8,128)S(1)} %get-tuple-element.20.residual, ...), custom_call_target="tpu_custom_call" | custom-call | tf_op jit(solution)/shard_map/pallas_call | solution.py:409
  (49 shorter events, 0.3 us)
Async XLA Ops:
  0.6 0.7 copy-start.2
  1.3 0.7 copy-start
  2.0 0.7 copy-start.1
  2.8 4.8 %collective-permute-start = (f32[2,24,128]{2,1,0:T(8,128)S(1)}, f32[2,24,128]{2,1,0:T(8,128)S(1)}, u32[]{:S(2)}, u32[]{:S(2)}) collective-permute-start(f32[2,24,128]{2,1,0:T(8,128)S(1)} %pad_maximum_fusion.8), channel_id=1, source_target_pairs={{0,16},{8,24},{16,0},{24,8},{1,17},{9,25},{17,1},{25,9},{2,18},{10... | collective-permute-start | bytes 73736 | tf_op jit(solution)/shard_map/ppermute | solution.py:324
  7.7 3.9 %collective-permute-start.1 = (f32[2,24,128]{2,1,0:T(8,128)S(1)}, f32[2,24,128]{2,1,0:T(8,128)S(1)}, u32[]{:S(2)}, u32[]{:S(2)}) collective-permute-start(f32[2,24,128]{2,1,0:T(8,128)S(1)} %pad_maximum_fusion.9), channel_id=1, source_target_pairs={{0,8},{8,0},{16,24},{24,16},{1,9},{9,1},{17,25},{25,17},{2,10},{10... | collective-permute-start | bytes 73736 | tf_op jit(solution)/shard_map/ppermute | solution.py:324
  11.6 5.0 %collective-permute-start.2 = (f32[2,24,128]{2,1,0:T(8,128)S(1)}, f32[2,24,128]{2,1,0:T(8,128)S(1)}, u32[]{:S(2)}, u32[]{:S(2)}) collective-permute-start(f32[2,24,128]{2,1,0:T(8,128)S(1)} %pad_maximum_fusion.10), channel_id=1, source_target_pairs={{0,4},{1,5},{2,6},{3,7},{4,0},{5,1},{6,2},{7,3},{8,12},{9,13},{10,... | collective-permute-start | bytes 73736 | tf_op jit(solution)/shard_map/ppermute | solution.py:324
  16.6 4.0 %collective-permute-start.3 = (f32[3,24,128]{2,1,0:T(8,128)S(1)}, f32[3,24,128]{2,1,0:T(8,128)S(1)}, u32[]{:S(2)}, u32[]{:S(2)}) collective-permute-start(f32[3,24,128]{2,1,0:T(8,128)S(1)} %pad_maximum_fusion.6), channel_id=1, source_target_pairs={{0,2},{1,3},{2,0},{3,1},{4,6},{5,7},{6,4},{7,5},{8,10},{9,11},{10,... | collective-permute-start | bytes 110600 | tf_op jit(solution)/shard_map/ppermute | solution.py:324
  20.6 1.3 %collective-permute-start.4 = (f32[5,24,128]{2,1,0:T(8,128)S(1)}, f32[5,24,128]{2,1,0:T(8,128)S(1)}, u32[]{:S(2)}, u32[]{:S(2)}) collective-permute-start(f32[5,24,128]{2,1,0:T(8,128)S(1)} %pad_maximum_fusion.1), channel_id=1, source_target_pairs={{0,1},{1,0},{2,3},{3,2},{4,5},{5,4},{6,7},{7,6},{8,9},{9,8},{10,11... | collective-permute-start | bytes 184328 | tf_op jit(solution)/shard_map/ppermute | solution.py:324
  36.7 1.5 %collective-permute-start.5 = (f32[7,8,256]{2,1,0:T(8,128)S(1)}, f32[7,8,256]{2,1,0:T(8,128)S(1)}, u32[]{:S(2)}, u32[]{:S(2)}) collective-permute-start(f32[7,8,256]{2,1,0:T(8,128)S(1)} %slice.161), channel_id=1, source_target_pairs={{0,1},{1,0},{2,3},{3,2},{4,5},{5,4},{6,7},{7,6},{8,9},{9,8},{10,11... | collective-permute-start | bytes 172040 | tf_op jit(solution)/shard_map/ppermute | solution.py:324
  38.2 4.6 %collective-permute-start.6 = (f32[6,8,256]{2,1,0:T(8,128)S(1)}, f32[6,8,256]{2,1,0:T(8,128)S(1)}, u32[]{:S(2)}, u32[]{:S(2)}) collective-permute-start(f32[6,8,256]{2,1,0:T(8,128)S(1)} %pad_maximum_fusion.2), channel_id=1, source_target_pairs={{0,2},{1,3},{2,0},{3,1},{4,6},{5,7},{6,4},{7,5},{8,10},{9,11},{10,... | collective-permute-start | bytes 147464 | tf_op jit(solution)/shard_map/ppermute | solution.py:324
  42.9 5.2 %collective-permute-start.7 = (f32[6,8,256]{2,1,0:T(8,128)S(1)}, f32[6,8,256]{2,1,0:T(8,128)S(1)}, u32[]{:S(2)}, u32[]{:S(2)}) collective-permute-start(f32[6,8,256]{2,1,0:T(8,128)S(1)} %pad_maximum_fusion.3), channel_id=1, source_target_pairs={{0,4},{1,5},{2,6},{3,7},{4,0},{5,1},{6,2},{7,3},{8,12},{9,13},{10,... | collective-permute-start | bytes 147464 | tf_op jit(solution)/shard_map/ppermute | solution.py:324
  48.1 4.2 %collective-permute-start.8 = (f32[6,8,256]{2,1,0:T(8,128)S(1)}, f32[6,8,256]{2,1,0:T(8,128)S(1)}, u32[]{:S(2)}, u32[]{:S(2)}) collective-permute-start(f32[6,8,256]{2,1,0:T(8,128)S(1)} %pad_maximum_fusion.4), channel_id=1, source_target_pairs={{0,8},{8,0},{16,24},{24,16},{1,9},{9,1},{17,25},{25,17},{2,10},{10... | collective-permute-start | bytes 147464 | tf_op jit(solution)/shard_map/ppermute | solution.py:324
  52.3 4.2 %collective-permute-start.9 = (f32[6,8,256]{2,1,0:T(8,128)S(1)}, f32[6,8,256]{2,1,0:T(8,128)S(1)}, u32[]{:S(2)}, u32[]{:S(2)}) collective-permute-start(f32[6,8,256]{2,1,0:T(8,128)S(1)} %pad_maximum_fusion.5), channel_id=1, source_target_pairs={{0,16},{8,24},{16,0},{24,8},{1,17},{9,25},{17,1},{25,9},{2,18},{10... | collective-permute-start | bytes 147464 | tf_op jit(solution)/shard_map/ppermute | solution.py:324
  56.4 1.2 %collective-permute-start.10 = (f32[4,8,256]{2,1,0:T(8,128)S(1)}, f32[4,8,256]{2,1,0:T(8,128)S(1)}, u32[]{:S(2)}, u32[]{:S(2)}) collective-permute-start(f32[4,8,256]{2,1,0:T(8,128)S(1)} %slice_add_fusion.1.rows), channel_id=1, source_target_pairs={{0,1},{1,0},{2,3},{3,2},{4,5},{5,4},{6,7},{7,6},{8,9},{9,8},{10,11... | collective-permute-start | bytes 98312 | tf_op jit(solution)/shard_map/ppermute | solution.py:324
  59.1 1.3 %collective-permute-start.11 = (f32[6,8,256]{2,1,0:T(8,128)S(1)}, f32[6,8,256]{2,1,0:T(8,128)S(1)}, u32[]{:S(2)}, u32[]{:S(2)}) collective-permute-start(f32[6,8,256]{2,1,0:T(8,128)S(1)} %concatenate.71), channel_id=1, source_target_pairs={{0,1},{1,0},{2,3},{3,2},{4,5},{5,4},{6,7},{7,6},{8,9},{9,8},{10,11... | collective-permute-start | bytes 147464 | tf_op jit(solution)/shard_map/ppermute | solution.py:324
  60.5 4.0 %collective-permute-start.12 = (f32[4,8,256]{2,1,0:T(8,128)S(1)}, f32[4,8,256]{2,1,0:T(8,128)S(1)}, u32[]{:S(2)}, u32[]{:S(2)}) collective-permute-start(f32[4,8,256]{2,1,0:T(8,128)S(1)} %pad_maximum_fusion.7), channel_id=1, source_target_pairs={{0,2},{1,3},{2,0},{3,1},{4,6},{5,7},{6,4},{7,5},{8,10},{9,11},{10,... | collective-permute-start | bytes 98312 | tf_op jit(solution)/shard_map/ppermute | solution.py:324
  64.5 4.8 %collective-permute-start.13 = (f32[3,8,256]{2,1,0:T(8,128)S(1)}, f32[3,8,256]{2,1,0:T(8,128)S(1)}, u32[]{:S(2)}, u32[]{:S(2)}) collective-permute-start(f32[3,8,256]{2,1,0:T(8,128)S(1)} %pad_maximum_fusion.11), channel_id=1, source_target_pairs={{0,4},{1,5},{2,6},{3,7},{4,0},{5,1},{6,2},{7,3},{8,12},{9,13},{10,... | collective-permute-start | bytes 73736 | tf_op jit(solution)/shard_map/ppermute | solution.py:324
  69.3 3.9 %collective-permute-start.14 = (f32[3,8,256]{2,1,0:T(8,128)S(1)}, f32[3,8,256]{2,1,0:T(8,128)S(1)}, u32[]{:S(2)}, u32[]{:S(2)}) collective-permute-start(f32[3,8,256]{2,1,0:T(8,128)S(1)} %pad_maximum_fusion.12), channel_id=1, source_target_pairs={{0,8},{8,0},{16,24},{24,16},{1,9},{9,1},{17,25},{25,17},{2,10},{10... | collective-permute-start | bytes 73736 | tf_op jit(solution)/shard_map/ppermute | solution.py:324
  73.3 3.9 %collective-permute-start.15 = (f32[3,8,256]{2,1,0:T(8,128)S(1)}, f32[3,8,256]{2,1,0:T(8,128)S(1)}, u32[]{:S(2)}, u32[]{:S(2)}) collective-permute-start(f32[3,8,256]{2,1,0:T(8,128)S(1)} %pad_maximum_fusion.13), channel_id=1, source_target_pairs={{0,16},{8,24},{16,0},{24,8},{1,17},{9,25},{17,1},{25,9},{2,18},{10... | collective-permute-start | bytes 73736 | tf_op jit(solution)/shard_map/ppermute | solution.py:324

commit v7 on v6

--- a/solution.py
+++ b/solution.py
@@ -19,7 +19,6 @@
 AXES = ("grp", "dev")
 VMEM_LIMIT = 48 * 1024 * 1024
 CLOSE = 2e-3
-ALWAYS = 3
 ROWS = 128
 
 
@@ -66,13 +65,13 @@
     return levels
 
 
-def inverse(matrix, ahead, guess):
+def inverse(matrix, ahead, guess, always, beside=()):
     order = matrix.shape[0]
     rows = lax.broadcasted_iota(jnp.int32, (order, order), 0)
     columns = lax.broadcasted_iota(jnp.int32, (order, order), 1)
     identity = (rows == columns).astype(F32)
     levels = newton_levels(order)
-    always = min(ALWAYS, len(levels) - 1)
+    always = min(always, len(levels) - 1)
     bound = jnp.minimum(jnp.max(jnp.sum(jnp.abs(matrix), axis=0)), order + NUGGET)
     start = 2.0 / (NUGGET + levels[always][1])
     for level in range(always + 1, len(levels)):
@@ -82,8 +81,9 @@
 
     def advance(scale, now, held, only_guess=False):
         now_parts = split(now)
+        new_now = None if only_guess else scale * taken(2.0 * now, now_parts, now_parts, rows=ROWS)
         new_held = scale * taken(2.0 * held, split(held), now_parts, rows=ROWS)
-        return (None if only_guess else scale * taken(2.0 * now, now_parts, now_parts, rows=ROWS)), new_held
+        return new_now, new_held
 
     for level in range(len(levels) - 1, always, -1):
 
@@ -91,11 +91,24 @@
         def _(scale=levels[level][0]):
             ahead[...], guess[...] = advance(scale, ahead[...], guess[...])
 
-    now, held = ahead[...], guess[...]
-    for level in range(always, 0, -1):
-        now, held = advance(levels[level][0], now, held, level == 1)
-    error = taken(identity, split_fine(matrix), split_fine(held), rows=ROWS)
-    return taken(held, split(held), split(-error), rows=ROWS)
+    beside = list(beside)
+
+    def also(left):
+        while len(beside) > left:
+            beside.pop(0)()
+
+    count = len(beside)
+    for level in range(always, 1, -1):
+        ahead[...], guess[...] = advance(levels[level][0], ahead[...], guess[...])
+        also(count * level // (always + 1))
+    guess[...] = advance(levels[1][0], ahead[...], guess[...], True)[1]
+    also(count // (always + 1))
+    held = guess[...]
+    ahead[...] = -taken(identity, split_fine(matrix), split_fine(held), rows=ROWS)
+    also(0)
+    held = guess[...]
+    guess[...] = taken(held, split(held), split(ahead[...]), rows=ROWS)
+    return guess[...]
 
 
 def slot_list(slots):
@@ -180,11 +193,13 @@
     def at(i, end=None):
         return pl.ds(i * points, ((i + 1 if end is None else end) - i) * points)
 
-    for j in range(own + 1):
-        for i in range(j, own + 1):
-            columns[j, at(i)] = covariance(turned[i], places[j], live[i] * live[j], i == j)
+    def build(i, j):
+        columns[j, at(i)] = covariance(turned[i], places[j], live[i] * live[j], i == j)
+
+    build(0, 0)
+    later = [functools.partial(build, i, j) for j in range(own + 1) for i in range(max(j, 1), own + 1)]
     for k in range(own):
-        middle = inverse(columns[k, at(k)], ahead, guess)
+        middle = inverse(columns[k, at(k)], ahead, guess, 6 if k == 0 else 3, later if k == 0 else ())
         side = columns[k, at(k + 1, own + 1)]
         below = -taken(jnp.zeros_like(side), split_fine(side), split_fine(middle))
         lower[k, at(k + 1, own + 1)] = below
@@ -194,13 +209,14 @@
             left = [piece[cut:] for piece in below_parts]
             right = [piece[cut : cut + points] for piece in side_parts]
             columns[j, at(j, own + 1)] = taken(columns[j, at(j, own + 1)], left, right, NT)
-    for k in range(own - 1, -1, -1):
+    def go_back(k):
         total = lower[k, at(own)]
         if k + 1 < own:
             done = back_out[:, (k + 1) * points :]
             total = taken(total, split(done), split(lower[k, at(k + 1, own)]))
         back_out[:, k * points : (k + 1) * points] = total
-    last = inverse(columns[own, at(own)], ahead, guess)
+
+    last = inverse(columns[own, at(own)], ahead, guess, 3, [functools.partial(go_back, k) for k in range(own - 1, -1, -1)])
     last_out[...] = last
     back = {k: split(back_out[:, k * points : (k + 1) * points]) for k in range(own)}
 
@@ -359,7 +375,7 @@
         pack_kernel,
         sizes,
         [((fields + 4) * pieces, LANES), noise_prec, neighbours],
-        [pl.ANY] * 4,
+        [pltpu.HBM] * 4,
         [pltpu.SemaphoreType.DMA((2 * pieces + 2,))],
     )(locations, observations, noise_prec, neighbours)
     before, table = mine[None], mine[None]

time: 78.5 us -> 77.1 us (0.982)
  starting transfers between devices: 27.7 us -> 21.6 us
  waiting for transfers between devices: 29.9 us -> 35.2 us
  Pallas kernels: 17.3 us -> 16.3 us
    ppermute x16, starting transfers between devices: 27.7 us -> 21.6 us  [swapped(): lax.ppermute(value, axis, [(at, at ^ reach) for at in range(lax.axis_size...]
    ppermute x16, waiting for transfers between devices: 29.9 us -> 35.2 us  [swapped(): lax.ppermute(value, axis, [(at, at ^ reach) for at in range(lax.axis_size...]
    pallas_call x1, Pallas kernels: 14.7 us -> 13.7 us  [local(): call(factor_kernel, sizes, [(coarse + 3,) + tile, (points, depth), square...]
where the time goes in v7:
time: 77.1 us; the launch traced here: 76.4 us
  waiting for transfers between devices  35.2 us (46%)
  starting transfers between devices  21.6 us (28%)
  Pallas kernels  16.3 us (21%)
  local copies, waits for them, and re-layouts  2.17 us (3%)
  between operations  0.84 us (1%)
    ppermute x16, waiting for transfers between devices, swapped(): lax.ppermute(value, axis, [(at, at ^ reach) for at in range(lax.axis_size...  35.2 us
    ppermute x16, starting transfers between devices, swapped(): lax.ppermute(value, axis, [(at, at ^ reach) for at in range(lax.axis_size...  21.6 us
    pallas_call x1, Pallas kernels, local(): call(factor_kernel, sizes, [(coarse + 3,) + tile, (points, depth), square...  13.7 us
    unnamed x7, local copies, waits for them, and re-layouts  2.09 us
  transfers between devices with their start and end apart: 16, of which 16 were waited for; matrix products, arithmetic and copies ran while one was open for 0% of the time, Pallas kernels for 0%

profile of v7, /device:TPU:0, one launch (start us, length us, event | category | flops | bytes accessed | tf_op | source)
XLA Modules:
  0.0 76.4 jit_solution(10882919658129972689)
XLA Ops:
  0.6 0.0 copy-start.2
  0.6 0.7 copy.6.locations
  1.3 0.0 copy-done.2
  1.3 0.0 copy-start
  1.3 0.7 copy-done
  2.0 0.0 copy-start.1
  2.0 0.7 copy-done.1
  2.7 0.1 shard_map.59
  2.8 3.0 %collective-permute-start = (f32[2,24,128]{2,1,0:T(8,128)S(1)}, f32[2,24,128]{2,1,0:T(8,128)S(1)}, u32[]{:S(2)}, u32[]{:S(2)}) collective-permute-start(f32[2,24,128]{2,1,0:T(8,128)S(1)} %pad_maximum_fusion.8), channel_id=1, source_target_pairs={{0,16},{8,24},{16,0},{24,8},{1,17},{9,25},{17,1},{25,9},{2,18},{10... | collective-permute-start | bytes 73736 | tf_op jit(solution)/shard_map/ppermute | solution.py:340
  5.9 1.8 %collective-permute-done = f32[2,24,128]{2,1,0:T(8,128)S(1)} collective-permute-done((f32[2,24,128]{2,1,0:T(8,128)S(1)}, f32[2,24,128]{2,1,0:T(8,128)S(1)}, u32[]{:S(2)}, u32[]{:S(2)}) %collective-permute-start) | collective-permute-done | bytes 24608 | tf_op jit(solution)/shard_map/ppermute | solution.py:340
  7.7 2.1 %collective-permute-start.1 = (f32[2,24,128]{2,1,0:T(8,128)S(1)}, f32[2,24,128]{2,1,0:T(8,128)S(1)}, u32[]{:S(2)}, u32[]{:S(2)}) collective-permute-start(f32[2,24,128]{2,1,0:T(8,128)S(1)} %pad_maximum_fusion.9), channel_id=1, source_target_pairs={{0,8},{8,0},{16,24},{24,16},{1,9},{9,1},{17,25},{25,17},{2,10},{10... | collective-permute-start | bytes 73736 | tf_op jit(solution)/shard_map/ppermute | solution.py:340
  9.7 1.8 %collective-permute-done.1 = f32[2,24,128]{2,1,0:T(8,128)S(1)} collective-permute-done((f32[2,24,128]{2,1,0:T(8,128)S(1)}, f32[2,24,128]{2,1,0:T(8,128)S(1)}, u32[]{:S(2)}, u32[]{:S(2)}) %collective-permute-start.1) | collective-permute-done | bytes 24608 | tf_op jit(solution)/shard_map/ppermute | solution.py:340
  11.6 3.2 %collective-permute-start.2 = (f32[2,24,128]{2,1,0:T(8,128)S(1)}, f32[2,24,128]{2,1,0:T(8,128)S(1)}, u32[]{:S(2)}, u32[]{:S(2)}) collective-permute-start(f32[2,24,128]{2,1,0:T(8,128)S(1)} %pad_maximum_fusion.10), channel_id=1, source_target_pairs={{0,4},{1,5},{2,6},{3,7},{4,0},{5,1},{6,2},{7,3},{8,12},{9,13},{10,... | collective-permute-start | bytes 73736 | tf_op jit(solution)/shard_map/ppermute | solution.py:340
  14.7 1.8 %collective-permute-done.2 = f32[2,24,128]{2,1,0:T(8,128)S(1)} collective-permute-done((f32[2,24,128]{2,1,0:T(8,128)S(1)}, f32[2,24,128]{2,1,0:T(8,128)S(1)}, u32[]{:S(2)}, u32[]{:S(2)}) %collective-permute-start.2) | collective-permute-done | bytes 24608 | tf_op jit(solution)/shard_map/ppermute | solution.py:340
  16.6 2.0 %collective-permute-start.3 = (f32[3,24,128]{2,1,0:T(8,128)S(1)}, f32[3,24,128]{2,1,0:T(8,128)S(1)}, u32[]{:S(2)}, u32[]{:S(2)}) collective-permute-start(f32[3,24,128]{2,1,0:T(8,128)S(1)} %pad_maximum_fusion.6), channel_id=1, source_target_pairs={{0,2},{1,3},{2,0},{3,1},{4,6},{5,7},{6,4},{7,5},{8,10},{9,11},{10,... | collective-permute-start | bytes 110600 | tf_op jit(solution)/shard_map/ppermute | solution.py:340
  18.5 2.1 %collective-permute-done.3 = f32[3,24,128]{2,1,0:T(8,128)S(1)} collective-permute-done((f32[3,24,128]{2,1,0:T(8,128)S(1)}, f32[3,24,128]{2,1,0:T(8,128)S(1)}, u32[]{:S(2)}, u32[]{:S(2)}) %collective-permute-start.3) | collective-permute-done | bytes 36896 | tf_op jit(solution)/shard_map/ppermute | solution.py:340
  20.6 0.1 collective-permute-start.4
  20.7 1.2 %collective-permute-done.4 = f32[5,24,128]{2,1,0:T(8,128)S(1)} collective-permute-done((f32[5,24,128]{2,1,0:T(8,128)S(1)}, f32[5,24,128]{2,1,0:T(8,128)S(1)}, u32[]{:S(2)}, u32[]{:S(2)}) %collective-permute-start.4) | collective-permute-done | bytes 61472 | tf_op jit(solution)/shard_map/ppermute | solution.py:340
  21.9 13.7 %shard_map.60 = (f32[11,8,256]{2,1,0:T(8,128)S(1)}, f32[256,768]{1,0:T(8,128)S(1)}, f32[256,256]{1,0:T(8,128)S(1)}) custom-call(s32[1,4]{1,0:T(1,128)S(1)} %get-tuple-element.12.nbr, s32[1]{0:T(128)} %bitcast.me, f32[1,24,128]{2,1,0:T(8,128)S(1)} %slice.206.before, f32[8,24,128]{2,1,0:T(8,128)S(1)} %pad_maximum_fusion.table, ...), custom_call_target="tpu_custom_call" | custom-call | tf_op jit(solution)/shard_map/pallas_call | solution.py:391
  35.7 0.1 collective-permute-start.5
  35.8 1.2 %collective-permute-done.5 = f32[7,8,256]{2,1,0:T(8,128)S(1)} collective-permute-done((f32[7,8,256]{2,1,0:T(8,128)S(1)}, f32[7,8,256]{2,1,0:T(8,128)S(1)}, u32[]{:S(2)}, u32[]{:S(2)}) %collective-permute-start.5) | collective-permute-done | bytes 57376 | tf_op jit(solution)/shard_map/ppermute | solution.py:340
  37.0 1.2 %collective-permute-start.6 = (f32[6,8,256]{2,1,0:T(8,128)S(1)}, f32[6,8,256]{2,1,0:T(8,128)S(1)}, u32[]{:S(2)}, u32[]{:S(2)}) collective-permute-start(f32[6,8,256]{2,1,0:T(8,128)S(1)} %pad_maximum_fusion.2), channel_id=1, source_target_pairs={{0,2},{1,3},{2,0},{3,1},{4,6},{5,7},{6,4},{7,5},{8,10},{9,11},{10,... | collective-permute-start | bytes 147464 | tf_op jit(solution)/shard_map/ppermute | solution.py:340
  38.3 2.9 %collective-permute-done.6 = f32[6,8,256]{2,1,0:T(8,128)S(1)} collective-permute-done((f32[6,8,256]{2,1,0:T(8,128)S(1)}, f32[6,8,256]{2,1,0:T(8,128)S(1)}, u32[]{:S(2)}, u32[]{:S(2)}) %collective-permute-start.6) | collective-permute-done | bytes 49184 | tf_op jit(solution)/shard_map/ppermute | solution.py:340
  41.2 1.9 %collective-permute-start.7 = (f32[6,8,256]{2,1,0:T(8,128)S(1)}, f32[6,8,256]{2,1,0:T(8,128)S(1)}, u32[]{:S(2)}, u32[]{:S(2)}) collective-permute-start(f32[6,8,256]{2,1,0:T(8,128)S(1)} %pad_maximum_fusion.3), channel_id=1, source_target_pairs={{0,4},{1,5},{2,6},{3,7},{4,0},{5,1},{6,2},{7,3},{8,12},{9,13},{10,... | collective-permute-start | bytes 147464 | tf_op jit(solution)/shard_map/ppermute | solution.py:340
  43.1 3.2 %collective-permute-done.7 = f32[6,8,256]{2,1,0:T(8,128)S(1)} collective-permute-done((f32[6,8,256]{2,1,0:T(8,128)S(1)}, f32[6,8,256]{2,1,0:T(8,128)S(1)}, u32[]{:S(2)}, u32[]{:S(2)}) %collective-permute-start.7) | collective-permute-done | bytes 49184 | tf_op jit(solution)/shard_map/ppermute | solution.py:340
  46.3 1.1 %collective-permute-start.8 = (f32[6,8,256]{2,1,0:T(8,128)S(1)}, f32[6,8,256]{2,1,0:T(8,128)S(1)}, u32[]{:S(2)}, u32[]{:S(2)}) collective-permute-start(f32[6,8,256]{2,1,0:T(8,128)S(1)} %pad_maximum_fusion.4), channel_id=1, source_target_pairs={{0,8},{8,0},{16,24},{24,16},{1,9},{9,1},{17,25},{25,17},{2,10},{10... | collective-permute-start | bytes 147464 | tf_op jit(solution)/shard_map/ppermute | solution.py:340
  47.4 3.1 %collective-permute-done.8 = f32[6,8,256]{2,1,0:T(8,128)S(1)} collective-permute-done((f32[6,8,256]{2,1,0:T(8,128)S(1)}, f32[6,8,256]{2,1,0:T(8,128)S(1)}, u32[]{:S(2)}, u32[]{:S(2)}) %collective-permute-start.8) | collective-permute-done | bytes 49184 | tf_op jit(solution)/shard_map/ppermute | solution.py:340
  50.5 1.3 %collective-permute-start.9 = (f32[6,8,256]{2,1,0:T(8,128)S(1)}, f32[6,8,256]{2,1,0:T(8,128)S(1)}, u32[]{:S(2)}, u32[]{:S(2)}) collective-permute-start(f32[6,8,256]{2,1,0:T(8,128)S(1)} %pad_maximum_fusion.5), channel_id=1, source_target_pairs={{0,16},{8,24},{16,0},{24,8},{1,17},{9,25},{17,1},{25,9},{2,18},{10... | collective-permute-start | bytes 147464 | tf_op jit(solution)/shard_map/ppermute | solution.py:340
  51.8 2.8 %collective-permute-done.9 = f32[6,8,256]{2,1,0:T(8,128)S(1)} collective-permute-done((f32[6,8,256]{2,1,0:T(8,128)S(1)}, f32[6,8,256]{2,1,0:T(8,128)S(1)}, u32[]{:S(2)}, u32[]{:S(2)}) %collective-permute-start.9) | collective-permute-done | bytes 49184 | tf_op jit(solution)/shard_map/ppermute | solution.py:340
  54.7 0.0 collective-permute-start.10
  54.7 1.2 %collective-permute-done.10.other_rows = f32[4,8,256]{2,1,0:T(8,128)S(1)} collective-permute-done((f32[4,8,256]{2,1,0:T(8,128)S(1)}, f32[4,8,256]{2,1,0:T(8,128)S(1)}, u32[]{:S(2)}, u32[]{:S(2)}) %collective-permute-start.10) | collective-permute-done | bytes 32800 | tf_op jit(solution)/shard_map/ppermute | solution.py:340
  55.9 1.5 %shard_map.61 = (f32[10,8,256]{2,1,0:T(8,128)S(1)}, f32[2,8,256]{2,1,0:T(8,128)S(1)}, f32[8,256]{1,0:T(8,128)S(1)}, f32[8,128]{1,0:T(8,128)S(1)}) custom-call(s32[1,4]{1,0:T(1,128)S(1)} %get-tuple-element.12.nbr, s32[1]{0:T(128)} %bitcast.me, f32[1,24,128]{2,1,0:T(8,128)S(1)} %slice.206.before, f32[8,24,128]{2,1,0:T(8,128)S(1)} %pad_maximum_fusion.table, ...), custom_call_target="tpu_custom_call" | custom-call | tf_op jit(solution)/shard_map/pallas_call | solution.py:409
  57.4 0.2 collective-permute-start.11
  57.6 1.1 %collective-permute-done.11 = f32[6,8,256]{2,1,0:T(8,128)S(1)} collective-permute-done((f32[6,8,256]{2,1,0:T(8,128)S(1)}, f32[6,8,256]{2,1,0:T(8,128)S(1)}, u32[]{:S(2)}, u32[]{:S(2)}) %collective-permute-start.11) | collective-permute-done | bytes 49184 | tf_op jit(solution)/shard_map/ppermute | solution.py:340
  58.7 1.2 %collective-permute-start.12 = (f32[4,8,256]{2,1,0:T(8,128)S(1)}, f32[4,8,256]{2,1,0:T(8,128)S(1)}, u32[]{:S(2)}, u32[]{:S(2)}) collective-permute-start(f32[4,8,256]{2,1,0:T(8,128)S(1)} %pad_maximum_fusion.7), channel_id=1, source_target_pairs={{0,2},{1,3},{2,0},{3,1},{4,6},{5,7},{6,4},{7,5},{8,10},{9,11},{10,... | collective-permute-start | bytes 98312 | tf_op jit(solution)/shard_map/ppermute | solution.py:340
  60.0 2.7 %collective-permute-done.12 = f32[4,8,256]{2,1,0:T(8,128)S(1)} collective-permute-done((f32[4,8,256]{2,1,0:T(8,128)S(1)}, f32[4,8,256]{2,1,0:T(8,128)S(1)}, u32[]{:S(2)}, u32[]{:S(2)}) %collective-permute-start.12) | collective-permute-done | bytes 32800 | tf_op jit(solution)/shard_map/ppermute | solution.py:340
  62.7 1.9 %collective-permute-start.13 = (f32[3,8,256]{2,1,0:T(8,128)S(1)}, f32[3,8,256]{2,1,0:T(8,128)S(1)}, u32[]{:S(2)}, u32[]{:S(2)}) collective-permute-start(f32[3,8,256]{2,1,0:T(8,128)S(1)} %pad_maximum_fusion.11), channel_id=1, source_target_pairs={{0,4},{1,5},{2,6},{3,7},{4,0},{5,1},{6,2},{7,3},{8,12},{9,13},{10,... | collective-permute-start | bytes 73736 | tf_op jit(solution)/shard_map/ppermute | solution.py:340
  64.6 2.9 %collective-permute-done.13 = f32[3,8,256]{2,1,0:T(8,128)S(1)} collective-permute-done((f32[3,8,256]{2,1,0:T(8,128)S(1)}, f32[3,8,256]{2,1,0:T(8,128)S(1)}, u32[]{:S(2)}, u32[]{:S(2)}) %collective-permute-start.13) | collective-permute-done | bytes 24608 | tf_op jit(solution)/shard_map/ppermute | solution.py:340
  67.6 1.1 %collective-permute-start.14 = (f32[3,8,256]{2,1,0:T(8,128)S(1)}, f32[3,8,256]{2,1,0:T(8,128)S(1)}, u32[]{:S(2)}, u32[]{:S(2)}) collective-permute-start(f32[3,8,256]{2,1,0:T(8,128)S(1)} %pad_maximum_fusion.12), channel_id=1, source_target_pairs={{0,8},{8,0},{16,24},{24,16},{1,9},{9,1},{17,25},{25,17},{2,10},{10... | collective-permute-start | bytes 73736 | tf_op jit(solution)/shard_map/ppermute | solution.py:340
  68.6 2.8 %collective-permute-done.14 = f32[3,8,256]{2,1,0:T(8,128)S(1)} collective-permute-done((f32[3,8,256]{2,1,0:T(8,128)S(1)}, f32[3,8,256]{2,1,0:T(8,128)S(1)}, u32[]{:S(2)}, u32[]{:S(2)}) %collective-permute-start.14) | collective-permute-done | bytes 24608 | tf_op jit(solution)/shard_map/ppermute | solution.py:340
  71.5 1.3 %collective-permute-start.15 = (f32[3,8,256]{2,1,0:T(8,128)S(1)}, f32[3,8,256]{2,1,0:T(8,128)S(1)}, u32[]{:S(2)}, u32[]{:S(2)}) collective-permute-start(f32[3,8,256]{2,1,0:T(8,128)S(1)} %pad_maximum_fusion.13), channel_id=1, source_target_pairs={{0,16},{8,24},{16,0},{24,8},{1,17},{9,25},{17,1},{25,9},{2,18},{10... | collective-permute-start | bytes 73736 | tf_op jit(solution)/shard_map/ppermute | solution.py:340
  72.8 2.6 %collective-permute-done.15 = f32[3,8,256]{2,1,0:T(8,128)S(1)} collective-permute-done((f32[3,8,256]{2,1,0:T(8,128)S(1)}, f32[3,8,256]{2,1,0:T(8,128)S(1)}, u32[]{:S(2)}, u32[]{:S(2)}) %collective-permute-start.15) | collective-permute-done | bytes 24608 | tf_op jit(solution)/shard_map/ppermute | solution.py:340
  75.4 1.0 %shard_map.62 = (f32[1,8,256]{2,1,0:T(8,128)}, f32[1,8,256]{2,1,0:T(8,128)}) custom-call(s32[1]{0:T(128)} %bitcast.me, f32[2,8,256]{2,1,0:T(8,128)S(1)} %slice_add_fusion.7.received, f32[1,8,256]{2,1,0:T(8,128)S(1)} %slice_select_fusion.6.shifted, f32[2,8,256]{2,1,0:T(8,128)S(1)} %get-tuple-element.19.images, f32[8,256]{1,0:T(8,128)S(1)} %get-tuple-element.20.residual, ...), custom_call_target="tpu_custom_call" | custom-call | tf_op jit(solution)/shard_map/pallas_call | solution.py:425
  (49 shorter events, 0.3 us)
Async XLA Ops:
  0.6 0.7 copy-start.2
  1.3 0.7 copy-start
  2.0 0.7 copy-start.1
  2.8 4.8 %collective-permute-start = (f32[2,24,128]{2,1,0:T(8,128)S(1)}, f32[2,24,128]{2,1,0:T(8,128)S(1)}, u32[]{:S(2)}, u32[]{:S(2)}) collective-permute-start(f32[2,24,128]{2,1,0:T(8,128)S(1)} %pad_maximum_fusion.8), channel_id=1, source_target_pairs={{0,16},{8,24},{16,0},{24,8},{1,17},{9,25},{17,1},{25,9},{2,18},{10... | collective-permute-start | bytes 73736 | tf_op jit(solution)/shard_map/ppermute | solution.py:340
  7.7 3.9 %collective-permute-start.1 = (f32[2,24,128]{2,1,0:T(8,128)S(1)}, f32[2,24,128]{2,1,0:T(8,128)S(1)}, u32[]{:S(2)}, u32[]{:S(2)}) collective-permute-start(f32[2,24,128]{2,1,0:T(8,128)S(1)} %pad_maximum_fusion.9), channel_id=1, source_target_pairs={{0,8},{8,0},{16,24},{24,16},{1,9},{9,1},{17,25},{25,17},{2,10},{10... | collective-permute-start | bytes 73736 | tf_op jit(solution)/shard_map/ppermute | solution.py:340
  11.6 5.0 %collective-permute-start.2 = (f32[2,24,128]{2,1,0:T(8,128)S(1)}, f32[2,24,128]{2,1,0:T(8,128)S(1)}, u32[]{:S(2)}, u32[]{:S(2)}) collective-permute-start(f32[2,24,128]{2,1,0:T(8,128)S(1)} %pad_maximum_fusion.10), channel_id=1, source_target_pairs={{0,4},{1,5},{2,6},{3,7},{4,0},{5,1},{6,2},{7,3},{8,12},{9,13},{10,... | collective-permute-start | bytes 73736 | tf_op jit(solution)/shard_map/ppermute | solution.py:340
  16.6 4.0 %collective-permute-start.3 = (f32[3,24,128]{2,1,0:T(8,128)S(1)}, f32[3,24,128]{2,1,0:T(8,128)S(1)}, u32[]{:S(2)}, u32[]{:S(2)}) collective-permute-start(f32[3,24,128]{2,1,0:T(8,128)S(1)} %pad_maximum_fusion.6), channel_id=1, source_target_pairs={{0,2},{1,3},{2,0},{3,1},{4,6},{5,7},{6,4},{7,5},{8,10},{9,11},{10,... | collective-permute-start | bytes 110600 | tf_op jit(solution)/shard_map/ppermute | solution.py:340
  20.6 1.3 %collective-permute-start.4 = (f32[5,24,128]{2,1,0:T(8,128)S(1)}, f32[5,24,128]{2,1,0:T(8,128)S(1)}, u32[]{:S(2)}, u32[]{:S(2)}) collective-permute-start(f32[5,24,128]{2,1,0:T(8,128)S(1)} %pad_maximum_fusion.1), channel_id=1, source_target_pairs={{0,1},{1,0},{2,3},{3,2},{4,5},{5,4},{6,7},{7,6},{8,9},{9,8},{10,11... | collective-permute-start | bytes 184328 | tf_op jit(solution)/shard_map/ppermute | solution.py:340
  35.7 1.3 %collective-permute-start.5 = (f32[7,8,256]{2,1,0:T(8,128)S(1)}, f32[7,8,256]{2,1,0:T(8,128)S(1)}, u32[]{:S(2)}, u32[]{:S(2)}) collective-permute-start(f32[7,8,256]{2,1,0:T(8,128)S(1)} %slice.161), channel_id=1, source_target_pairs={{0,1},{1,0},{2,3},{3,2},{4,5},{5,4},{6,7},{7,6},{8,9},{9,8},{10,11... | collective-permute-start | bytes 172040 | tf_op jit(solution)/shard_map/ppermute | solution.py:340
  37.0 4.2 %collective-permute-start.6 = (f32[6,8,256]{2,1,0:T(8,128)S(1)}, f32[6,8,256]{2,1,0:T(8,128)S(1)}, u32[]{:S(2)}, u32[]{:S(2)}) collective-permute-start(f32[6,8,256]{2,1,0:T(8,128)S(1)} %pad_maximum_fusion.2), channel_id=1, source_target_pairs={{0,2},{1,3},{2,0},{3,1},{4,6},{5,7},{6,4},{7,5},{8,10},{9,11},{10,... | collective-permute-start | bytes 147464 | tf_op jit(solution)/shard_map/ppermute | solution.py:340
  41.2 5.1 %collective-permute-start.7 = (f32[6,8,256]{2,1,0:T(8,128)S(1)}, f32[6,8,256]{2,1,0:T(8,128)S(1)}, u32[]{:S(2)}, u32[]{:S(2)}) collective-permute-start(f32[6,8,256]{2,1,0:T(8,128)S(1)} %pad_maximum_fusion.3), channel_id=1, source_target_pairs={{0,4},{1,5},{2,6},{3,7},{4,0},{5,1},{6,2},{7,3},{8,12},{9,13},{10,... | collective-permute-start | bytes 147464 | tf_op jit(solution)/shard_map/ppermute | solution.py:340
  46.3 4.2 %collective-permute-start.8 = (f32[6,8,256]{2,1,0:T(8,128)S(1)}, f32[6,8,256]{2,1,0:T(8,128)S(1)}, u32[]{:S(2)}, u32[]{:S(2)}) collective-permute-start(f32[6,8,256]{2,1,0:T(8,128)S(1)} %pad_maximum_fusion.4), channel_id=1, source_target_pairs={{0,8},{8,0},{16,24},{24,16},{1,9},{9,1},{17,25},{25,17},{2,10},{10... | collective-permute-start | bytes 147464 | tf_op jit(solution)/shard_map/ppermute | solution.py:340
  50.5 4.2 %collective-permute-start.9 = (f32[6,8,256]{2,1,0:T(8,128)S(1)}, f32[6,8,256]{2,1,0:T(8,128)S(1)}, u32[]{:S(2)}, u32[]{:S(2)}) collective-permute-start(f32[6,8,256]{2,1,0:T(8,128)S(1)} %pad_maximum_fusion.5), channel_id=1, source_target_pairs={{0,16},{8,24},{16,0},{24,8},{1,17},{9,25},{17,1},{25,9},{2,18},{10... | collective-permute-start | bytes 147464 | tf_op jit(solution)/shard_map/ppermute | solution.py:340
  54.7 1.2 %collective-permute-start.10 = (f32[4,8,256]{2,1,0:T(8,128)S(1)}, f32[4,8,256]{2,1,0:T(8,128)S(1)}, u32[]{:S(2)}, u32[]{:S(2)}) collective-permute-start(f32[4,8,256]{2,1,0:T(8,128)S(1)} %slice_add_fusion.1.rows), channel_id=1, source_target_pairs={{0,1},{1,0},{2,3},{3,2},{4,5},{5,4},{6,7},{7,6},{8,9},{9,8},{10,11... | collective-permute-start | bytes 98312 | tf_op jit(solution)/shard_map/ppermute | solution.py:340
  57.4 1.3 %collective-permute-start.11 = (f32[6,8,256]{2,1,0:T(8,128)S(1)}, f32[6,8,256]{2,1,0:T(8,128)S(1)}, u32[]{:S(2)}, u32[]{:S(2)}) collective-permute-start(f32[6,8,256]{2,1,0:T(8,128)S(1)} %concatenate.71), channel_id=1, source_target_pairs={{0,1},{1,0},{2,3},{3,2},{4,5},{5,4},{6,7},{7,6},{8,9},{9,8},{10,11... | collective-permute-start | bytes 147464 | tf_op jit(solution)/shard_map/ppermute | solution.py:340
  58.7 4.0 %collective-permute-start.12 = (f32[4,8,256]{2,1,0:T(8,128)S(1)}, f32[4,8,256]{2,1,0:T(8,128)S(1)}, u32[]{:S(2)}, u32[]{:S(2)}) collective-permute-start(f32[4,8,256]{2,1,0:T(8,128)S(1)} %pad_maximum_fusion.7), channel_id=1, source_target_pairs={{0,2},{1,3},{2,0},{3,1},{4,6},{5,7},{6,4},{7,5},{8,10},{9,11},{10,... | collective-permute-start | bytes 98312 | tf_op jit(solution)/shard_map/ppermute | solution.py:340
  62.7 4.8 %collective-permute-start.13 = (f32[3,8,256]{2,1,0:T(8,128)S(1)}, f32[3,8,256]{2,1,0:T(8,128)S(1)}, u32[]{:S(2)}, u32[]{:S(2)}) collective-permute-start(f32[3,8,256]{2,1,0:T(8,128)S(1)} %pad_maximum_fusion.11), channel_id=1, source_target_pairs={{0,4},{1,5},{2,6},{3,7},{4,0},{5,1},{6,2},{7,3},{8,12},{9,13},{10,... | collective-permute-start | bytes 73736 | tf_op jit(solution)/shard_map/ppermute | solution.py:340
  67.6 3.9 %collective-permute-start.14 = (f32[3,8,256]{2,1,0:T(8,128)S(1)}, f32[3,8,256]{2,1,0:T(8,128)S(1)}, u32[]{:S(2)}, u32[]{:S(2)}) collective-permute-start(f32[3,8,256]{2,1,0:T(8,128)S(1)} %pad_maximum_fusion.12), channel_id=1, source_target_pairs={{0,8},{8,0},{16,24},{24,16},{1,9},{9,1},{17,25},{25,17},{2,10},{10... | collective-permute-start | bytes 73736 | tf_op jit(solution)/shard_map/ppermute | solution.py:340
  71.5 3.9 %collective-permute-start.15 = (f32[3,8,256]{2,1,0:T(8,128)S(1)}, f32[3,8,256]{2,1,0:T(8,128)S(1)}, u32[]{:S(2)}, u32[]{:S(2)}) collective-permute-start(f32[3,8,256]{2,1,0:T(8,128)S(1)} %pad_maximum_fusion.13), channel_id=1, source_target_pairs={{0,16},{8,24},{16,0},{24,8},{1,17},{9,25},{17,1},{25,9},{2,18},{10... | collective-permute-start | bytes 73736 | tf_op jit(solution)/shard_map/ppermute | solution.py:340

commit v8 on v7

--- a/solution.py
+++ b/solution.py
@@ -20,6 +20,7 @@
 VMEM_LIMIT = 48 * 1024 * 1024
 CLOSE = 2e-3
 ROWS = 128
+TOPS = (3, 4, 6)
 
 
 def split(value):
@@ -65,17 +66,19 @@
     return levels
 
 
-def inverse(matrix, ahead, guess, always, beside=()):
+def inverse(matrix, ahead, guess, beside=()):
     order = matrix.shape[0]
     rows = lax.broadcasted_iota(jnp.int32, (order, order), 0)
     columns = lax.broadcasted_iota(jnp.int32, (order, order), 1)
     identity = (rows == columns).astype(F32)
     levels = newton_levels(order)
-    always = min(always, len(levels) - 1)
+    last = len(levels) - 1
+    tops = [top for top in TOPS if top < last] + [last]
+    tops += [] if len(tops) > 1 else [last]
     bound = jnp.minimum(jnp.max(jnp.sum(jnp.abs(matrix), axis=0)), order + NUGGET)
-    start = 2.0 / (NUGGET + levels[always][1])
-    for level in range(always + 1, len(levels)):
-        start = jnp.where(bound > levels[level - 1][1], 2.0 / (NUGGET + levels[level][1]), start)
+    start = 2.0 / (NUGGET + levels[tops[0]][1])
+    for below, top in zip(tops, tops[1:]):
+        start = jnp.where(bound > levels[below][1], 2.0 / (NUGGET + levels[top][1]), start)
     ahead[...] = start * matrix
     guess[...] = start * identity
 
@@ -85,12 +88,14 @@
         new_held = scale * taken(2.0 * held, split(held), now_parts, rows=ROWS)
         return new_now, new_held
 
-    for level in range(len(levels) - 1, always, -1):
-
-        @pl.when(bound > levels[level - 1][1])
-        def _(scale=levels[level][0]):
-            ahead[...], guess[...] = advance(scale, ahead[...], guess[...])
-
+    for below, top in list(zip(tops, tops[1:]))[::-1]:
+
+        @pl.when(bound > levels[below][1])
+        def _(below=below, top=top):
+            for level in range(top, below, -1):
+                ahead[...], guess[...] = advance(levels[level][0], ahead[...], guess[...])
+
+    always = tops[0]
     beside = list(beside)
 
     def also(left):
@@ -148,24 +153,6 @@
     return (index >= 0).astype(F32)
 
 
-def pack_kernel(sizes, locations, observed, noise, nbr, packed, noise_out, nbr_out, done):
-    fields, points, coarse, slots = sizes
-    pieces = points // LANES
-    first = fields * pieces
-    packed[first:] = jnp.zeros((4 * pieces, LANES), F32)
-    copies = []
-    for at in range(pieces):
-        lanes = pl.ds(at * LANES, LANES)
-        copies.append((observed.at[0, :, lanes], packed.at[pl.ds(at * fields, fields)]))
-        copies.append((locations.at[0, :, lanes], packed.at[pl.ds(first + 4 * at, 3)]))
-    copies += [(noise, noise_out), (nbr, nbr_out)]
-    copies = [pltpu.make_async_copy(*copy, done.at[at]) for at, copy in enumerate(copies)]
-    for copy in copies:
-        copy.start()
-    for copy in copies:
-        copy.wait()
-
-
 def fields_of(entry, fields, points):
     return jnp.concatenate([entry[at * fields : (at + 1) * fields] for at in range(points // LANES)], axis=1)
 
@@ -199,7 +186,7 @@
     build(0, 0)
     later = [functools.partial(build, i, j) for j in range(own + 1) for i in range(max(j, 1), own + 1)]
     for k in range(own):
-        middle = inverse(columns[k, at(k)], ahead, guess, 6 if k == 0 else 3, later if k == 0 else ())
+        middle = inverse(columns[k, at(k)], ahead, guess, later if k == 0 else ())
         side = columns[k, at(k + 1, own + 1)]
         below = -taken(jnp.zeros_like(side), split_fine(side), split_fine(middle))
         lower[k, at(k + 1, own + 1)] = below
@@ -216,7 +203,7 @@
             total = taken(total, split(done), split(lower[k, at(k + 1, own)]))
         back_out[:, k * points : (k + 1) * points] = total
 
-    last = inverse(columns[own, at(own)], ahead, guess, 3, [functools.partial(go_back, k) for k in range(own - 1, -1, -1)])
+    last = inverse(columns[own, at(own)], ahead, guess, [functools.partial(go_back, k) for k in range(own - 1, -1, -1)])
     last_out[...] = last
     back = {k: split(back_out[:, k * points : (k + 1) * points]) for k in range(own)}
 
@@ -371,13 +358,14 @@
     square, tile = (points, points), (fields, points)
     steps = exchanges()
 
-    mine, noise, nbr = call(
-        pack_kernel,
-        sizes,
-        [((fields + 4) * pieces, LANES), noise_prec, neighbours],
-        [pltpu.HBM] * 4,
-        [pltpu.SemaphoreType.DMA((2 * pieces + 2,))],
-    )(locations, observations, noise_prec, neighbours)
+    lanes = [slice(at * LANES, (at + 1) * LANES) for at in range(pieces)]
+    empty = jnp.zeros((1, LANES), F32)
+    packed = [observations[0, :, cut] for cut in lanes]
+    for cut in lanes:
+        packed += [locations[0, :, cut], empty]
+    mine = jnp.concatenate(packed, axis=0)
+    noise = jnp.where(me < 0, 0.0, noise_prec)
+    nbr = jnp.where(me < 0, -1, neighbours)
     before, table = mine[None], mine[None]
     for axis, reach, bit in steps[::-1]:
         got = swapped(jnp.concatenate([table, before], axis=0), axis, reach)

time: 77.1 us -> 75.7 us (0.982)
  starting transfers between devices: 21.6 us -> 27.3 us
  waiting for transfers between devices: 35.2 us -> 30 us
  Pallas kernels: 16.3 us -> 15.3 us
    ppermute x16, starting transfers between devices: 21.6 us -> 27.3 us  [swapped(): lax.ppermute(value, axis, [(at, at ^ reach) for at in range(lax.axis_size...]
    ppermute x16, waiting for transfers between devices: 35.2 us -> 30 us  [swapped(): lax.ppermute(value, axis, [(at, at ^ reach) for at in range(lax.axis_size...]
    unnamed x7 -> x4, local copies, waits for them, and re-layouts: 2.09 us -> 0.56 us
    pallas_call x1, Pallas kernels: 13.7 us -> 12.8 us  [local(): call(factor_kernel, sizes, [(coarse + 3,) + tile, (points, depth), square...]
where the time goes in v8:
time: 75.7 us; the launch traced here: 75.8 us
  waiting for transfers between devices  30 us (40%)
  starting transfers between devices  27.3 us (36%)
  Pallas kernels  15.3 us (20%)
  local copies, waits for them, and re-layouts  2.07 us (3%)
  between operations  0.82 us (1%)
    ppermute x16, waiting for transfers between devices, swapped(): lax.ppermute(value, axis, [(at, at ^ reach) for at in range(lax.axis_size...  30 us
    ppermute x16, starting transfers between devices, swapped(): lax.ppermute(value, axis, [(at, at ^ reach) for at in range(lax.axis_size...  27.3 us
    pallas_call x1, Pallas kernels, local(): call(factor_kernel, sizes, [(coarse + 3,) + tile, (points, depth), square...  12.8 us
  transfers between devices with their start and end apart: 16, of which 16 were waited for; matrix products, arithmetic and copies ran while one was open for 0% of the time, Pallas kernels for 0%

profile of v8, /device:TPU:0, one launch (start us, length us, event | category | flops | bytes accessed | tf_op | source)
XLA Modules:
  0.0 75.8 jit_solution(1611664589085051551)
XLA Ops:
  0.6 0.7 fusion.3
  1.3 0.7 slice_bitcast_fusion
  2.1 3.0 %collective-permute-start = (f32[2,24,128]{2,1,0:T(8,128)S(1)}, f32[2,24,128]{2,1,0:T(8,128)S(1)}, u32[]{:S(2)}, u32[]{:S(2)}) collective-permute-start(f32[2,24,128]{2,1,0:T(8,128)S(1)} %pad_maximum_fusion.8), channel_id=1, source_target_pairs={{0,16},{8,24},{16,0},{24,8},{1,17},{9,25},{17,1},{25,9},{2,18},{10... | collective-permute-start | bytes 73736 | tf_op jit(solution)/shard_map/ppermute | solution.py:327
  5.1 1.8 %collective-permute-done = f32[2,24,128]{2,1,0:T(8,128)S(1)} collective-permute-done((f32[2,24,128]{2,1,0:T(8,128)S(1)}, f32[2,24,128]{2,1,0:T(8,128)S(1)}, u32[]{:S(2)}, u32[]{:S(2)}) %collective-permute-start) | collective-permute-done | bytes 24608 | tf_op jit(solution)/shard_map/ppermute | solution.py:327
  6.9 2.1 %collective-permute-start.1 = (f32[2,24,128]{2,1,0:T(8,128)S(1)}, f32[2,24,128]{2,1,0:T(8,128)S(1)}, u32[]{:S(2)}, u32[]{:S(2)}) collective-permute-start(f32[2,24,128]{2,1,0:T(8,128)S(1)} %pad_maximum_fusion.9), channel_id=1, source_target_pairs={{0,8},{8,0},{16,24},{24,16},{1,9},{9,1},{17,25},{25,17},{2,10},{10... | collective-permute-start | bytes 73736 | tf_op jit(solution)/shard_map/ppermute | solution.py:327
  9.0 1.8 %collective-permute-done.1 = f32[2,24,128]{2,1,0:T(8,128)S(1)} collective-permute-done((f32[2,24,128]{2,1,0:T(8,128)S(1)}, f32[2,24,128]{2,1,0:T(8,128)S(1)}, u32[]{:S(2)}, u32[]{:S(2)}) %collective-permute-start.1) | collective-permute-done | bytes 24608 | tf_op jit(solution)/shard_map/ppermute | solution.py:327
  10.8 3.2 %collective-permute-start.2 = (f32[2,24,128]{2,1,0:T(8,128)S(1)}, f32[2,24,128]{2,1,0:T(8,128)S(1)}, u32[]{:S(2)}, u32[]{:S(2)}) collective-permute-start(f32[2,24,128]{2,1,0:T(8,128)S(1)} %pad_maximum_fusion.10), channel_id=1, source_target_pairs={{0,4},{1,5},{2,6},{3,7},{4,0},{5,1},{6,2},{7,3},{8,12},{9,13},{10,... | collective-permute-start | bytes 73736 | tf_op jit(solution)/shard_map/ppermute | solution.py:327
  14.0 1.8 %collective-permute-done.2 = f32[2,24,128]{2,1,0:T(8,128)S(1)} collective-permute-done((f32[2,24,128]{2,1,0:T(8,128)S(1)}, f32[2,24,128]{2,1,0:T(8,128)S(1)}, u32[]{:S(2)}, u32[]{:S(2)}) %collective-permute-start.2) | collective-permute-done | bytes 24608 | tf_op jit(solution)/shard_map/ppermute | solution.py:327
  15.8 0.0 copy-start
  15.8 2.0 %collective-permute-start.3 = (f32[3,24,128]{2,1,0:T(8,128)S(1)}, f32[3,24,128]{2,1,0:T(8,128)S(1)}, u32[]{:S(2)}, u32[]{:S(2)}) collective-permute-start(f32[3,24,128]{2,1,0:T(8,128)S(1)} %pad_maximum_fusion.6), channel_id=1, source_target_pairs={{0,2},{1,3},{2,0},{3,1},{4,6},{5,7},{6,4},{7,5},{8,10},{9,11},{10,... | collective-permute-start | bytes 110600 | tf_op jit(solution)/shard_map/ppermute | solution.py:327
  17.8 0.0 copy-done
  17.8 2.0 %collective-permute-done.3 = f32[3,24,128]{2,1,0:T(8,128)S(1)} collective-permute-done((f32[3,24,128]{2,1,0:T(8,128)S(1)}, f32[3,24,128]{2,1,0:T(8,128)S(1)}, u32[]{:S(2)}, u32[]{:S(2)}) %collective-permute-start.3) | collective-permute-done | bytes 36896 | tf_op jit(solution)/shard_map/ppermute | solution.py:327
  19.8 0.0 copy-start.1
  19.9 0.1 collective-permute-start.4
  19.9 0.6 copy-done.1
  20.5 0.7 collective-permute-done.4
  21.2 12.8 %shard_map.59 = (f32[11,8,256]{2,1,0:T(8,128)S(1)}, f32[256,768]{1,0:T(8,128)S(1)}, f32[256,256]{1,0:T(8,128)S(1)}) custom-call(s32[1,4]{1,0:T(1,128)S(1)} %broadcast_select_fusion.1.nbr, s32[1]{0:T(128)} %bitcast.me, f32[1,24,128]{2,1,0:T(8,128)S(1)} %slice.222.before, f32[8,24,128]{2,1,0:T(8,128)S(1)} %pad_maximum_fusion.table, ...), custom_call_target="tpu_custom_call" | custom-call | tf_op jit(solution)/shard_map/pallas_call | solution.py:379
  34.0 1.3 %collective-permute-start.5 = (f32[7,8,256]{2,1,0:T(8,128)S(1)}, f32[7,8,256]{2,1,0:T(8,128)S(1)}, u32[]{:S(2)}, u32[]{:S(2)}) collective-permute-start(f32[7,8,256]{2,1,0:T(8,128)S(1)} %slice.177), channel_id=1, source_target_pairs={{0,1},{1,0},{2,3},{3,2},{4,5},{5,4},{6,7},{7,6},{8,9},{9,8},{10,11... | collective-permute-start | bytes 172040 | tf_op jit(solution)/shard_map/ppermute | solution.py:327
  35.3 0.9 %collective-permute-done.5 = f32[7,8,256]{2,1,0:T(8,128)S(1)} collective-permute-done((f32[7,8,256]{2,1,0:T(8,128)S(1)}, f32[7,8,256]{2,1,0:T(8,128)S(1)}, u32[]{:S(2)}, u32[]{:S(2)}) %collective-permute-start.5) | collective-permute-done | bytes 57376 | tf_op jit(solution)/shard_map/ppermute | solution.py:327
  36.2 1.5 %collective-permute-start.6 = (f32[6,8,256]{2,1,0:T(8,128)S(1)}, f32[6,8,256]{2,1,0:T(8,128)S(1)}, u32[]{:S(2)}, u32[]{:S(2)}) collective-permute-start(f32[6,8,256]{2,1,0:T(8,128)S(1)} %pad_maximum_fusion.2), channel_id=1, source_target_pairs={{0,2},{1,3},{2,0},{3,1},{4,6},{5,7},{6,4},{7,5},{8,10},{9,11},{10,... | collective-permute-start | bytes 147464 | tf_op jit(solution)/shard_map/ppermute | solution.py:327
  37.7 2.6 %collective-permute-done.6 = f32[6,8,256]{2,1,0:T(8,128)S(1)} collective-permute-done((f32[6,8,256]{2,1,0:T(8,128)S(1)}, f32[6,8,256]{2,1,0:T(8,128)S(1)}, u32[]{:S(2)}, u32[]{:S(2)}) %collective-permute-start.6) | collective-permute-done | bytes 49184 | tf_op jit(solution)/shard_map/ppermute | solution.py:327
  40.4 2.9 %collective-permute-start.7 = (f32[6,8,256]{2,1,0:T(8,128)S(1)}, f32[6,8,256]{2,1,0:T(8,128)S(1)}, u32[]{:S(2)}, u32[]{:S(2)}) collective-permute-start(f32[6,8,256]{2,1,0:T(8,128)S(1)} %pad_maximum_fusion.3), channel_id=1, source_target_pairs={{0,4},{1,5},{2,6},{3,7},{4,0},{5,1},{6,2},{7,3},{8,12},{9,13},{10,... | collective-permute-start | bytes 147464 | tf_op jit(solution)/shard_map/ppermute | solution.py:327
  43.3 2.4 %collective-permute-done.7 = f32[6,8,256]{2,1,0:T(8,128)S(1)} collective-permute-done((f32[6,8,256]{2,1,0:T(8,128)S(1)}, f32[6,8,256]{2,1,0:T(8,128)S(1)}, u32[]{:S(2)}, u32[]{:S(2)}) %collective-permute-start.7) | collective-permute-done | bytes 49184 | tf_op jit(solution)/shard_map/ppermute | solution.py:327
  45.7 1.9 %collective-permute-start.8 = (f32[6,8,256]{2,1,0:T(8,128)S(1)}, f32[6,8,256]{2,1,0:T(8,128)S(1)}, u32[]{:S(2)}, u32[]{:S(2)}) collective-permute-start(f32[6,8,256]{2,1,0:T(8,128)S(1)} %pad_maximum_fusion.4), channel_id=1, source_target_pairs={{0,8},{8,0},{16,24},{24,16},{1,9},{9,1},{17,25},{25,17},{2,10},{10... | collective-permute-start | bytes 147464 | tf_op jit(solution)/shard_map/ppermute | solution.py:327
  47.6 2.2 %collective-permute-done.8 = f32[6,8,256]{2,1,0:T(8,128)S(1)} collective-permute-done((f32[6,8,256]{2,1,0:T(8,128)S(1)}, f32[6,8,256]{2,1,0:T(8,128)S(1)}, u32[]{:S(2)}, u32[]{:S(2)}) %collective-permute-start.8) | collective-permute-done | bytes 49184 | tf_op jit(solution)/shard_map/ppermute | solution.py:327
  49.9 1.4 %collective-permute-start.9 = (f32[6,8,256]{2,1,0:T(8,128)S(1)}, f32[6,8,256]{2,1,0:T(8,128)S(1)}, u32[]{:S(2)}, u32[]{:S(2)}) collective-permute-start(f32[6,8,256]{2,1,0:T(8,128)S(1)} %pad_maximum_fusion.5), channel_id=1, source_target_pairs={{0,16},{8,24},{16,0},{24,8},{1,17},{9,25},{17,1},{25,9},{2,18},{10... | collective-permute-start | bytes 147464 | tf_op jit(solution)/shard_map/ppermute | solution.py:327
  51.3 2.7 %collective-permute-done.9 = f32[6,8,256]{2,1,0:T(8,128)S(1)} collective-permute-done((f32[6,8,256]{2,1,0:T(8,128)S(1)}, f32[6,8,256]{2,1,0:T(8,128)S(1)}, u32[]{:S(2)}, u32[]{:S(2)}) %collective-permute-start.9) | collective-permute-done | bytes 49184 | tf_op jit(solution)/shard_map/ppermute | solution.py:327
  54.0 0.0 collective-permute-start.10
  54.0 1.2 %collective-permute-done.10.other_rows = f32[4,8,256]{2,1,0:T(8,128)S(1)} collective-permute-done((f32[4,8,256]{2,1,0:T(8,128)S(1)}, f32[4,8,256]{2,1,0:T(8,128)S(1)}, u32[]{:S(2)}, u32[]{:S(2)}) %collective-permute-start.10) | collective-permute-done | bytes 32800 | tf_op jit(solution)/shard_map/ppermute | solution.py:327
  55.2 1.5 %shard_map.60 = (f32[10,8,256]{2,1,0:T(8,128)S(1)}, f32[2,8,256]{2,1,0:T(8,128)S(1)}, f32[8,256]{1,0:T(8,128)S(1)}, f32[8,128]{1,0:T(8,128)S(1)}) custom-call(s32[1,4]{1,0:T(1,128)S(1)} %broadcast_select_fusion.1.nbr, s32[1]{0:T(128)} %bitcast.me, f32[1,24,128]{2,1,0:T(8,128)S(1)} %slice.222.before, f32[8,24,128]{2,1,0:T(8,128)S(1)} %pad_maximum_fusion.table, ...), custom_call_target="tpu_custom_call" | custom-call | tf_op jit(solution)/shard_map/pallas_call | solution.py:397
  56.7 0.2 collective-permute-start.11
  57.0 1.1 %collective-permute-done.11 = f32[6,8,256]{2,1,0:T(8,128)S(1)} collective-permute-done((f32[6,8,256]{2,1,0:T(8,128)S(1)}, f32[6,8,256]{2,1,0:T(8,128)S(1)}, u32[]{:S(2)}, u32[]{:S(2)}) %collective-permute-start.11) | collective-permute-done | bytes 49184 | tf_op jit(solution)/shard_map/ppermute | solution.py:327
  58.1 1.6 %collective-permute-start.12 = (f32[4,8,256]{2,1,0:T(8,128)S(1)}, f32[4,8,256]{2,1,0:T(8,128)S(1)}, u32[]{:S(2)}, u32[]{:S(2)}) collective-permute-start(f32[4,8,256]{2,1,0:T(8,128)S(1)} %pad_maximum_fusion.7), channel_id=1, source_target_pairs={{0,2},{1,3},{2,0},{3,1},{4,6},{5,7},{6,4},{7,5},{8,10},{9,11},{10,... | collective-permute-start | bytes 98312 | tf_op jit(solution)/shard_map/ppermute | solution.py:327
  59.7 2.3 %collective-permute-done.12 = f32[4,8,256]{2,1,0:T(8,128)S(1)} collective-permute-done((f32[4,8,256]{2,1,0:T(8,128)S(1)}, f32[4,8,256]{2,1,0:T(8,128)S(1)}, u32[]{:S(2)}, u32[]{:S(2)}) %collective-permute-start.12) | collective-permute-done | bytes 32800 | tf_op jit(solution)/shard_map/ppermute | solution.py:327
  62.1 2.7 %collective-permute-start.13 = (f32[3,8,256]{2,1,0:T(8,128)S(1)}, f32[3,8,256]{2,1,0:T(8,128)S(1)}, u32[]{:S(2)}, u32[]{:S(2)}) collective-permute-start(f32[3,8,256]{2,1,0:T(8,128)S(1)} %pad_maximum_fusion.11), channel_id=1, source_target_pairs={{0,4},{1,5},{2,6},{3,7},{4,0},{5,1},{6,2},{7,3},{8,12},{9,13},{10,... | collective-permute-start | bytes 73736 | tf_op jit(solution)/shard_map/ppermute | solution.py:327
  64.8 2.1 %collective-permute-done.13 = f32[3,8,256]{2,1,0:T(8,128)S(1)} collective-permute-done((f32[3,8,256]{2,1,0:T(8,128)S(1)}, f32[3,8,256]{2,1,0:T(8,128)S(1)}, u32[]{:S(2)}, u32[]{:S(2)}) %collective-permute-start.13) | collective-permute-done | bytes 24608 | tf_op jit(solution)/shard_map/ppermute | solution.py:327
  66.9 1.9 %collective-permute-start.14 = (f32[3,8,256]{2,1,0:T(8,128)S(1)}, f32[3,8,256]{2,1,0:T(8,128)S(1)}, u32[]{:S(2)}, u32[]{:S(2)}) collective-permute-start(f32[3,8,256]{2,1,0:T(8,128)S(1)} %pad_maximum_fusion.12), channel_id=1, source_target_pairs={{0,8},{8,0},{16,24},{24,16},{1,9},{9,1},{17,25},{25,17},{2,10},{10... | collective-permute-start | bytes 73736 | tf_op jit(solution)/shard_map/ppermute | solution.py:327
  68.8 2.0 %collective-permute-done.14 = f32[3,8,256]{2,1,0:T(8,128)S(1)} collective-permute-done((f32[3,8,256]{2,1,0:T(8,128)S(1)}, f32[3,8,256]{2,1,0:T(8,128)S(1)}, u32[]{:S(2)}, u32[]{:S(2)}) %collective-permute-start.14) | collective-permute-done | bytes 24608 | tf_op jit(solution)/shard_map/ppermute | solution.py:327
  70.8 1.5 %collective-permute-start.15 = (f32[3,8,256]{2,1,0:T(8,128)S(1)}, f32[3,8,256]{2,1,0:T(8,128)S(1)}, u32[]{:S(2)}, u32[]{:S(2)}) collective-permute-start(f32[3,8,256]{2,1,0:T(8,128)S(1)} %pad_maximum_fusion.13), channel_id=1, source_target_pairs={{0,16},{8,24},{16,0},{24,8},{1,17},{9,25},{17,1},{25,9},{2,18},{10... | collective-permute-start | bytes 73736 | tf_op jit(solution)/shard_map/ppermute | solution.py:327
  72.3 2.4 %collective-permute-done.15 = f32[3,8,256]{2,1,0:T(8,128)S(1)} collective-permute-done((f32[3,8,256]{2,1,0:T(8,128)S(1)}, f32[3,8,256]{2,1,0:T(8,128)S(1)}, u32[]{:S(2)}, u32[]{:S(2)}) %collective-permute-start.15) | collective-permute-done | bytes 24608 | tf_op jit(solution)/shard_map/ppermute | solution.py:327
  74.7 1.0 %shard_map.61 = (f32[1,8,256]{2,1,0:T(8,128)}, f32[1,8,256]{2,1,0:T(8,128)}) custom-call(s32[1]{0:T(128)} %bitcast.me, f32[2,8,256]{2,1,0:T(8,128)S(1)} %slice_add_fusion.7.received, f32[1,8,256]{2,1,0:T(8,128)S(1)} %slice_select_fusion.6.shifted, f32[2,8,256]{2,1,0:T(8,128)S(1)} %get-tuple-element.13.images, f32[8,256]{1,0:T(8,128)S(1)} %get-tuple-element.14.residual, ...), custom_call_target="tpu_custom_call" | custom-call | tf_op jit(solution)/shard_map/pallas_call | solution.py:413
  (54 shorter events, 0.3 us)
Async XLA Ops:
  2.1 4.8 %collective-permute-start = (f32[2,24,128]{2,1,0:T(8,128)S(1)}, f32[2,24,128]{2,1,0:T(8,128)S(1)}, u32[]{:S(2)}, u32[]{:S(2)}) collective-permute-start(f32[2,24,128]{2,1,0:T(8,128)S(1)} %pad_maximum_fusion.8), channel_id=1, source_target_pairs={{0,16},{8,24},{16,0},{24,8},{1,17},{9,25},{17,1},{25,9},{2,18},{10... | collective-permute-start | bytes 73736 | tf_op jit(solution)/shard_map/ppermute | solution.py:327
  6.9 3.9 %collective-permute-start.1 = (f32[2,24,128]{2,1,0:T(8,128)S(1)}, f32[2,24,128]{2,1,0:T(8,128)S(1)}, u32[]{:S(2)}, u32[]{:S(2)}) collective-permute-start(f32[2,24,128]{2,1,0:T(8,128)S(1)} %pad_maximum_fusion.9), channel_id=1, source_target_pairs={{0,8},{8,0},{16,24},{24,16},{1,9},{9,1},{17,25},{25,17},{2,10},{10... | collective-permute-start | bytes 73736 | tf_op jit(solution)/shard_map/ppermute | solution.py:327
  10.8 5.0 %collective-permute-start.2 = (f32[2,24,128]{2,1,0:T(8,128)S(1)}, f32[2,24,128]{2,1,0:T(8,128)S(1)}, u32[]{:S(2)}, u32[]{:S(2)}) collective-permute-start(f32[2,24,128]{2,1,0:T(8,128)S(1)} %pad_maximum_fusion.10), channel_id=1, source_target_pairs={{0,4},{1,5},{2,6},{3,7},{4,0},{5,1},{6,2},{7,3},{8,12},{9,13},{10,... | collective-permute-start | bytes 73736 | tf_op jit(solution)/shard_map/ppermute | solution.py:327
  15.8 2.0 %copy-start = (f32[1,8,256]{2,1,0:T(8,128)S(1)}, f32[1,8,256]{2,1,0:T(8,128)}, u32[]{:S(2)}) copy-start(f32[1,8,256]{2,1,0:T(8,128)} %param.7) | copy-start | bytes 24580
  15.8 4.0 %collective-permute-start.3 = (f32[3,24,128]{2,1,0:T(8,128)S(1)}, f32[3,24,128]{2,1,0:T(8,128)S(1)}, u32[]{:S(2)}, u32[]{:S(2)}) collective-permute-start(f32[3,24,128]{2,1,0:T(8,128)S(1)} %pad_maximum_fusion.6), channel_id=1, source_target_pairs={{0,2},{1,3},{2,0},{3,1},{4,6},{5,7},{6,4},{7,5},{8,10},{9,11},{10,... | collective-permute-start | bytes 110600 | tf_op jit(solution)/shard_map/ppermute | solution.py:327
  19.8 0.7 copy-start.1
  19.9 1.3 %collective-permute-start.4 = (f32[5,24,128]{2,1,0:T(8,128)S(1)}, f32[5,24,128]{2,1,0:T(8,128)S(1)}, u32[]{:S(2)}, u32[]{:S(2)}) collective-permute-start(f32[5,24,128]{2,1,0:T(8,128)S(1)} %pad_maximum_fusion.1), channel_id=1, source_target_pairs={{0,1},{1,0},{2,3},{3,2},{4,5},{5,4},{6,7},{7,6},{8,9},{9,8},{10,11... | collective-permute-start | bytes 184328 | tf_op jit(solution)/shard_map/ppermute | solution.py:327
  34.0 2.1 %collective-permute-start.5 = (f32[7,8,256]{2,1,0:T(8,128)S(1)}, f32[7,8,256]{2,1,0:T(8,128)S(1)}, u32[]{:S(2)}, u32[]{:S(2)}) collective-permute-start(f32[7,8,256]{2,1,0:T(8,128)S(1)} %slice.177), channel_id=1, source_target_pairs={{0,1},{1,0},{2,3},{3,2},{4,5},{5,4},{6,7},{7,6},{8,9},{9,8},{10,11... | collective-permute-start | bytes 172040 | tf_op jit(solution)/shard_map/ppermute | solution.py:327
  36.2 4.2 %collective-permute-start.6 = (f32[6,8,256]{2,1,0:T(8,128)S(1)}, f32[6,8,256]{2,1,0:T(8,128)S(1)}, u32[]{:S(2)}, u32[]{:S(2)}) collective-permute-start(f32[6,8,256]{2,1,0:T(8,128)S(1)} %pad_maximum_fusion.2), channel_id=1, source_target_pairs={{0,2},{1,3},{2,0},{3,1},{4,6},{5,7},{6,4},{7,5},{8,10},{9,11},{10,... | collective-permute-start | bytes 147464 | tf_op jit(solution)/shard_map/ppermute | solution.py:327
  40.4 5.3 %collective-permute-start.7 = (f32[6,8,256]{2,1,0:T(8,128)S(1)}, f32[6,8,256]{2,1,0:T(8,128)S(1)}, u32[]{:S(2)}, u32[]{:S(2)}) collective-permute-start(f32[6,8,256]{2,1,0:T(8,128)S(1)} %pad_maximum_fusion.3), channel_id=1, source_target_pairs={{0,4},{1,5},{2,6},{3,7},{4,0},{5,1},{6,2},{7,3},{8,12},{9,13},{10,... | collective-permute-start | bytes 147464 | tf_op jit(solution)/shard_map/ppermute | solution.py:327
  45.7 4.2 %collective-permute-start.8 = (f32[6,8,256]{2,1,0:T(8,128)S(1)}, f32[6,8,256]{2,1,0:T(8,128)S(1)}, u32[]{:S(2)}, u32[]{:S(2)}) collective-permute-start(f32[6,8,256]{2,1,0:T(8,128)S(1)} %pad_maximum_fusion.4), channel_id=1, source_target_pairs={{0,8},{8,0},{16,24},{24,16},{1,9},{9,1},{17,25},{25,17},{2,10},{10... | collective-permute-start | bytes 147464 | tf_op jit(solution)/shard_map/ppermute | solution.py:327
  49.9 4.2 %collective-permute-start.9 = (f32[6,8,256]{2,1,0:T(8,128)S(1)}, f32[6,8,256]{2,1,0:T(8,128)S(1)}, u32[]{:S(2)}, u32[]{:S(2)}) collective-permute-start(f32[6,8,256]{2,1,0:T(8,128)S(1)} %pad_maximum_fusion.5), channel_id=1, source_target_pairs={{0,16},{8,24},{16,0},{24,8},{1,17},{9,25},{17,1},{25,9},{2,18},{10... | collective-permute-start | bytes 147464 | tf_op jit(solution)/shard_map/ppermute | solution.py:327
  54.0 1.2 %collective-permute-start.10 = (f32[4,8,256]{2,1,0:T(8,128)S(1)}, f32[4,8,256]{2,1,0:T(8,128)S(1)}, u32[]{:S(2)}, u32[]{:S(2)}) collective-permute-start(f32[4,8,256]{2,1,0:T(8,128)S(1)} %slice_add_fusion.1.rows), channel_id=1, source_target_pairs={{0,1},{1,0},{2,3},{3,2},{4,5},{5,4},{6,7},{7,6},{8,9},{9,8},{10,11... | collective-permute-start | bytes 98312 | tf_op jit(solution)/shard_map/ppermute | solution.py:327
  56.7 1.3 %collective-permute-start.11 = (f32[6,8,256]{2,1,0:T(8,128)S(1)}, f32[6,8,256]{2,1,0:T(8,128)S(1)}, u32[]{:S(2)}, u32[]{:S(2)}) collective-permute-start(f32[6,8,256]{2,1,0:T(8,128)S(1)} %concatenate.75), channel_id=1, source_target_pairs={{0,1},{1,0},{2,3},{3,2},{4,5},{5,4},{6,7},{7,6},{8,9},{9,8},{10,11... | collective-permute-start | bytes 147464 | tf_op jit(solution)/shard_map/ppermute | solution.py:327
  58.1 4.0 %collective-permute-start.12 = (f32[4,8,256]{2,1,0:T(8,128)S(1)}, f32[4,8,256]{2,1,0:T(8,128)S(1)}, u32[]{:S(2)}, u32[]{:S(2)}) collective-permute-start(f32[4,8,256]{2,1,0:T(8,128)S(1)} %pad_maximum_fusion.7), channel_id=1, source_target_pairs={{0,2},{1,3},{2,0},{3,1},{4,6},{5,7},{6,4},{7,5},{8,10},{9,11},{10,... | collective-permute-start | bytes 98312 | tf_op jit(solution)/shard_map/ppermute | solution.py:327
  62.1 4.8 %collective-permute-start.13 = (f32[3,8,256]{2,1,0:T(8,128)S(1)}, f32[3,8,256]{2,1,0:T(8,128)S(1)}, u32[]{:S(2)}, u32[]{:S(2)}) collective-permute-start(f32[3,8,256]{2,1,0:T(8,128)S(1)} %pad_maximum_fusion.11), channel_id=1, source_target_pairs={{0,4},{1,5},{2,6},{3,7},{4,0},{5,1},{6,2},{7,3},{8,12},{9,13},{10,... | collective-permute-start | bytes 73736 | tf_op jit(solution)/shard_map/ppermute | solution.py:327
  66.9 3.9 %collective-permute-start.14 = (f32[3,8,256]{2,1,0:T(8,128)S(1)}, f32[3,8,256]{2,1,0:T(8,128)S(1)}, u32[]{:S(2)}, u32[]{:S(2)}) collective-permute-start(f32[3,8,256]{2,1,0:T(8,128)S(1)} %pad_maximum_fusion.12), channel_id=1, source_target_pairs={{0,8},{8,0},{16,24},{24,16},{1,9},{9,1},{17,25},{25,17},{2,10},{10... | collective-permute-start | bytes 73736 | tf_op jit(solution)/shard_map/ppermute | solution.py:327
  70.8 3.9 %collective-permute-start.15 = (f32[3,8,256]{2,1,0:T(8,128)S(1)}, f32[3,8,256]{2,1,0:T(8,128)S(1)}, u32[]{:S(2)}, u32[]{:S(2)}) collective-permute-start(f32[3,8,256]{2,1,0:T(8,128)S(1)} %pad_maximum_fusion.13), channel_id=1, source_target_pairs={{0,16},{8,24},{16,0},{24,8},{1,17},{9,25},{17,1},{25,9},{2,18},{10... | collective-permute-start | bytes 73736 | tf_op jit(solution)/shard_map/ppermute | solution.py:327

commit v9 on v8

--- a/solution.py
+++ b/solution.py
@@ -163,7 +163,10 @@
     return jnp.concatenate(rows, axis=1) * (SQRT_THREE / SCALE_LENGTH)
 
 
-def factor_kernel(sizes, nbr, me, before, table, mine, noise, part, back_out, last_out, columns, lower, ahead, guess):
+def factor_kernel(
+    sizes, nbr, me, before, table, mine, noise, part, back_high, back_low, last_high, last_low,
+    columns, lower, ahead, guess,
+):
     fields, points, coarse, slots = sizes
     used = slot_list(slots)
     own = len(used)
@@ -196,18 +199,22 @@
             left = [piece[cut:] for piece in below_parts]
             right = [piece[cut : cut + points] for piece in side_parts]
             columns[j, at(j, own + 1)] = taken(columns[j, at(j, own + 1)], left, right, NT)
+    back = {}
+
     def go_back(k):
         total = lower[k, at(own)]
-        if k + 1 < own:
-            done = back_out[:, (k + 1) * points :]
-            total = taken(total, split(done), split(lower[k, at(k + 1, own)]))
-        back_out[:, k * points : (k + 1) * points] = total
-
-    last = inverse(columns[own, at(own)], ahead, guess, [functools.partial(go_back, k) for k in range(own - 1, -1, -1)])
-    last_out[...] = last
-    back = {k: split(back_out[:, k * points : (k + 1) * points]) for k in range(own)}
-
-    middle, spread, slot_parts = apply_block(values, back, split(last))
+        for j in range(own - 1, k, -1):
+            total = taken(total, back[j], split(lower[k, at(j)]))
+        back[k] = split(total)
+        place = slice(k * points, (k + 1) * points)
+        back_high[:, place], back_low[:, place] = back[k]
+
+    last = split(
+        inverse(columns[own, at(own)], ahead, guess, [functools.partial(go_back, k) for k in range(own - 1, -1, -1)])
+    )
+    last_high[...], last_low[...] = last
+
+    middle, spread, slot_parts = apply_block(values, back, last)
     own_part = spread + noise[0] * values[own]
     part[...] = jnp.zeros_like(part)
     product = jnp.sum(middle * spread + noise[0] * values[own] * values[own], axis=1, keepdims=True)
@@ -243,7 +250,8 @@
 
 
 def step_kernel(
-    sizes, nbr, me, before, table, mine, noise, part, rows, other_rows, scalars, near, far, back, last,
+    sizes, nbr, me, before, table, mine, noise, part, rows, other_rows, scalars, near, far,
+    back_high, back_low, last_high, last_low,
     sends, image_out, residual_out, ratio_out,
 ):
     fields, points, coarse, slots = sizes
@@ -269,8 +277,9 @@
         else:
             entry = table[mirrored(jnp.maximum(index, 0) ^ here, coarse)]
         values.append((fields_of(entry, fields, points) - alpha * image) * live_of(index))
-    back_parts = {k: split(back[:, k * points : (k + 1) * points]) for k in range(own)}
-    middle, spread, slot_parts = apply_block(values, back_parts, split(last[...]))
+    places = [slice(k * points, (k + 1) * points) for k in range(own)]
+    back = {k: (back_high[:, place], back_low[:, place]) for k, place in enumerate(places)}
+    middle, spread, slot_parts = apply_block(values, back, (last_high[...], last_low[...]))
     residual = values[own]
     inner = jnp.sum(middle * spread + noise[0] * residual * residual, axis=1, keepdims=True)
     cross = jnp.sum(residual * image, axis=1, keepdims=True)
@@ -376,10 +385,10 @@
         else:
             table = jnp.concatenate([table, got[:-1]], axis=0)
     at = me.reshape(1)
-    part, back, last = call(
+    part, *inverses = call(
         factor_kernel,
         sizes,
-        [(coarse + 3,) + tile, (points, depth), square],
+        [(coarse + 3,) + tile] + [jax.ShapeDtypeStruct(shape, jnp.bfloat16) for shape in ((points, depth),) * 2 + (square,) * 2],
         [smem, smem] + [vmem] * 4,
         [pltpu.VMEM((slots, slots * points, points), F32)] * 2 + [pltpu.VMEM(square, F32)] * 2,
     )(nbr, at, before, table, mine, noise)
@@ -398,8 +407,8 @@
         step_kernel,
         sizes,
         [(coarse + 2,) + tile, (2,) + tile, tile, (fields, LANES)],
-        [smem, smem] + [vmem] * 12,
-    )(nbr, at, before, table, mine, noise, part, rows, other_rows, scalars, near, far, back, last)
+        [smem, smem] + [vmem] * 14,
+    )(nbr, at, before, table, mine, noise, part, rows, other_rows, scalars, near, far, *inverses)
 
     summed, ends, shifted = sends[:-1], sends[-1:], jnp.zeros_like(sends[-1:])
     for axis, reach, bit in steps:

time: 75.7 us -> 75.9 us (level)
  waiting for transfers between devices: 30 us -> 28.1 us
  starting transfers between devices: 27.3 us -> 28.8 us
    ppermute x16, waiting for transfers between devices: 30 us -> 28.1 us  [swapped(): lax.ppermute(value, axis, [(at, at ^ reach) for at in range(lax.axis_size...]
    ppermute x16, starting transfers between devices: 27.3 us -> 28.8 us  [swapped(): lax.ppermute(value, axis, [(at, at ^ reach) for at in range(lax.axis_size...]
where the time goes in v9:
time: 75.9 us; the launch traced here: 75.4 us
  starting transfers between devices  28.8 us (38%)
  waiting for transfers between devices  28.1 us (37%)
  Pallas kernels  15.4 us (20%)
  local copies, waits for them, and re-layouts  2.07 us (3%)
  between operations  0.82 us (1%)
    ppermute x16, starting transfers between devices, swapped(): lax.ppermute(value, axis, [(at, at ^ reach) for at in range(lax.axis_size...  28.8 us
    ppermute x16, waiting for transfers between devices, swapped(): lax.ppermute(value, axis, [(at, at ^ reach) for at in range(lax.axis_size...  28.1 us
    pallas_call x1, Pallas kernels, local(): call(factor_kernel, sizes, [(coarse + 3,) + tile] + [jax.ShapeDtypeStruct...  12.9 us
  transfers between devices with their start and end apart: 16, of which 16 were waited for; matrix products, arithmetic and copies ran while one was open for 0% of the time, Pallas kernels for 0%

profile of v9, /device:TPU:0, one launch (start us, length us, event | category | flops | bytes accessed | tf_op | source)
XLA Modules:
  0.0 75.4 jit_solution(7247578578986919776)
XLA Ops:
  0.6 0.7 fusion.3
  1.3 0.7 slice_bitcast_fusion
  2.1 3.0 %collective-permute-start = (f32[2,24,128]{2,1,0:T(8,128)S(1)}, f32[2,24,128]{2,1,0:T(8,128)S(1)}, u32[]{:S(2)}, u32[]{:S(2)}) collective-permute-start(f32[2,24,128]{2,1,0:T(8,128)S(1)} %pad_maximum_fusion.8), channel_id=1, source_target_pairs={{0,16},{8,24},{16,0},{24,8},{1,17},{9,25},{17,1},{25,9},{2,18},{10... | collective-permute-start | bytes 73736 | tf_op jit(solution)/shard_map/ppermute | solution.py:336
  5.1 1.8 %collective-permute-done = f32[2,24,128]{2,1,0:T(8,128)S(1)} collective-permute-done((f32[2,24,128]{2,1,0:T(8,128)S(1)}, f32[2,24,128]{2,1,0:T(8,128)S(1)}, u32[]{:S(2)}, u32[]{:S(2)}) %collective-permute-start) | collective-permute-done | bytes 24608 | tf_op jit(solution)/shard_map/ppermute | solution.py:336
  6.9 2.1 %collective-permute-start.1 = (f32[2,24,128]{2,1,0:T(8,128)S(1)}, f32[2,24,128]{2,1,0:T(8,128)S(1)}, u32[]{:S(2)}, u32[]{:S(2)}) collective-permute-start(f32[2,24,128]{2,1,0:T(8,128)S(1)} %pad_maximum_fusion.9), channel_id=1, source_target_pairs={{0,8},{8,0},{16,24},{24,16},{1,9},{9,1},{17,25},{25,17},{2,10},{10... | collective-permute-start | bytes 73736 | tf_op jit(solution)/shard_map/ppermute | solution.py:336
  9.0 1.8 %collective-permute-done.1 = f32[2,24,128]{2,1,0:T(8,128)S(1)} collective-permute-done((f32[2,24,128]{2,1,0:T(8,128)S(1)}, f32[2,24,128]{2,1,0:T(8,128)S(1)}, u32[]{:S(2)}, u32[]{:S(2)}) %collective-permute-start.1) | collective-permute-done | bytes 24608 | tf_op jit(solution)/shard_map/ppermute | solution.py:336
  10.8 3.2 %collective-permute-start.2 = (f32[2,24,128]{2,1,0:T(8,128)S(1)}, f32[2,24,128]{2,1,0:T(8,128)S(1)}, u32[]{:S(2)}, u32[]{:S(2)}) collective-permute-start(f32[2,24,128]{2,1,0:T(8,128)S(1)} %pad_maximum_fusion.10), channel_id=1, source_target_pairs={{0,4},{1,5},{2,6},{3,7},{4,0},{5,1},{6,2},{7,3},{8,12},{9,13},{10,... | collective-permute-start | bytes 73736 | tf_op jit(solution)/shard_map/ppermute | solution.py:336
  14.0 1.8 %collective-permute-done.2 = f32[2,24,128]{2,1,0:T(8,128)S(1)} collective-permute-done((f32[2,24,128]{2,1,0:T(8,128)S(1)}, f32[2,24,128]{2,1,0:T(8,128)S(1)}, u32[]{:S(2)}, u32[]{:S(2)}) %collective-permute-start.2) | collective-permute-done | bytes 24608 | tf_op jit(solution)/shard_map/ppermute | solution.py:336
  15.8 0.0 copy-start
  15.8 2.0 %collective-permute-start.3 = (f32[3,24,128]{2,1,0:T(8,128)S(1)}, f32[3,24,128]{2,1,0:T(8,128)S(1)}, u32[]{:S(2)}, u32[]{:S(2)}) collective-permute-start(f32[3,24,128]{2,1,0:T(8,128)S(1)} %pad_maximum_fusion.6), channel_id=1, source_target_pairs={{0,2},{1,3},{2,0},{3,1},{4,6},{5,7},{6,4},{7,5},{8,10},{9,11},{10,... | collective-permute-start | bytes 110600 | tf_op jit(solution)/shard_map/ppermute | solution.py:336
  17.8 0.0 copy-done
  17.8 2.0 %collective-permute-done.3 = f32[3,24,128]{2,1,0:T(8,128)S(1)} collective-permute-done((f32[3,24,128]{2,1,0:T(8,128)S(1)}, f32[3,24,128]{2,1,0:T(8,128)S(1)}, u32[]{:S(2)}, u32[]{:S(2)}) %collective-permute-start.3) | collective-permute-done | bytes 36896 | tf_op jit(solution)/shard_map/ppermute | solution.py:336
  19.8 0.0 copy-start.1
  19.9 0.1 collective-permute-start.4
  19.9 0.6 copy-done.1
  20.5 0.7 collective-permute-done.4
  21.2 12.9 %shard_map.59 = (f32[11,8,256]{2,1,0:T(8,128)S(1)}, bf16[256,768]{1,0:T(8,128)(2,1)S(1)}, bf16[256,768]{1,0:T(8,128)(2,1)S(1)}, bf16[256,256]{1,0:T(8,128)(2,1)S(1)}, bf16[256,256]{1,0:T(8,128)(2,1)S(1)}) custom-call(s32[1,4]{1,0:T(1,128)S(1)} %broadcast_select_fusion.1.nbr, s32[1]{0:T(128)} %bitcast.me, f32[1,24,128]{2,1,0:T(8,128)S(1)} %slice.222.before, ...), custom_call_target="tpu_custom_call" | custom-call | tf_op jit(solution)/shard_map/pallas_call | solution.py:388
  34.1 0.2 collective-permute-start.5
  34.4 1.1 %collective-permute-done.5 = f32[7,8,256]{2,1,0:T(8,128)S(1)} collective-permute-done((f32[7,8,256]{2,1,0:T(8,128)S(1)}, f32[7,8,256]{2,1,0:T(8,128)S(1)}, u32[]{:S(2)}, u32[]{:S(2)}) %collective-permute-start.5) | collective-permute-done | bytes 57376 | tf_op jit(solution)/shard_map/ppermute | solution.py:336
  35.5 2.0 %collective-permute-start.6 = (f32[6,8,256]{2,1,0:T(8,128)S(1)}, f32[6,8,256]{2,1,0:T(8,128)S(1)}, u32[]{:S(2)}, u32[]{:S(2)}) collective-permute-start(f32[6,8,256]{2,1,0:T(8,128)S(1)} %pad_maximum_fusion.2), channel_id=1, source_target_pairs={{0,2},{1,3},{2,0},{3,1},{4,6},{5,7},{6,4},{7,5},{8,10},{9,11},{10,... | collective-permute-start | bytes 147464 | tf_op jit(solution)/shard_map/ppermute | solution.py:336
  37.4 2.2 %collective-permute-done.6 = f32[6,8,256]{2,1,0:T(8,128)S(1)} collective-permute-done((f32[6,8,256]{2,1,0:T(8,128)S(1)}, f32[6,8,256]{2,1,0:T(8,128)S(1)}, u32[]{:S(2)}, u32[]{:S(2)}) %collective-permute-start.6) | collective-permute-done | bytes 49184 | tf_op jit(solution)/shard_map/ppermute | solution.py:336
  39.6 3.2 %collective-permute-start.7 = (f32[6,8,256]{2,1,0:T(8,128)S(1)}, f32[6,8,256]{2,1,0:T(8,128)S(1)}, u32[]{:S(2)}, u32[]{:S(2)}) collective-permute-start(f32[6,8,256]{2,1,0:T(8,128)S(1)} %pad_maximum_fusion.3), channel_id=1, source_target_pairs={{0,4},{1,5},{2,6},{3,7},{4,0},{5,1},{6,2},{7,3},{8,12},{9,13},{10,... | collective-permute-start | bytes 147464 | tf_op jit(solution)/shard_map/ppermute | solution.py:336
  42.8 2.3 %collective-permute-done.7 = f32[6,8,256]{2,1,0:T(8,128)S(1)} collective-permute-done((f32[6,8,256]{2,1,0:T(8,128)S(1)}, f32[6,8,256]{2,1,0:T(8,128)S(1)}, u32[]{:S(2)}, u32[]{:S(2)}) %collective-permute-start.7) | collective-permute-done | bytes 49184 | tf_op jit(solution)/shard_map/ppermute | solution.py:336
  45.1 2.2 %collective-permute-start.8 = (f32[6,8,256]{2,1,0:T(8,128)S(1)}, f32[6,8,256]{2,1,0:T(8,128)S(1)}, u32[]{:S(2)}, u32[]{:S(2)}) collective-permute-start(f32[6,8,256]{2,1,0:T(8,128)S(1)} %pad_maximum_fusion.4), channel_id=1, source_target_pairs={{0,8},{8,0},{16,24},{24,16},{1,9},{9,1},{17,25},{25,17},{2,10},{10... | collective-permute-start | bytes 147464 | tf_op jit(solution)/shard_map/ppermute | solution.py:336
  47.4 2.1 %collective-permute-done.8 = f32[6,8,256]{2,1,0:T(8,128)S(1)} collective-permute-done((f32[6,8,256]{2,1,0:T(8,128)S(1)}, f32[6,8,256]{2,1,0:T(8,128)S(1)}, u32[]{:S(2)}, u32[]{:S(2)}) %collective-permute-start.8) | collective-permute-done | bytes 49184 | tf_op jit(solution)/shard_map/ppermute | solution.py:336
  49.5 2.1 %collective-permute-start.9 = (f32[6,8,256]{2,1,0:T(8,128)S(1)}, f32[6,8,256]{2,1,0:T(8,128)S(1)}, u32[]{:S(2)}, u32[]{:S(2)}) collective-permute-start(f32[6,8,256]{2,1,0:T(8,128)S(1)} %pad_maximum_fusion.5), channel_id=1, source_target_pairs={{0,16},{8,24},{16,0},{24,8},{1,17},{9,25},{17,1},{25,9},{2,18},{10... | collective-permute-start | bytes 147464 | tf_op jit(solution)/shard_map/ppermute | solution.py:336
  51.6 2.1 %collective-permute-done.9 = f32[6,8,256]{2,1,0:T(8,128)S(1)} collective-permute-done((f32[6,8,256]{2,1,0:T(8,128)S(1)}, f32[6,8,256]{2,1,0:T(8,128)S(1)}, u32[]{:S(2)}, u32[]{:S(2)}) %collective-permute-start.9) | collective-permute-done | bytes 49184 | tf_op jit(solution)/shard_map/ppermute | solution.py:336
  53.7 0.0 collective-permute-start.10
  53.7 1.2 %collective-permute-done.10.other_rows = f32[4,8,256]{2,1,0:T(8,128)S(1)} collective-permute-done((f32[4,8,256]{2,1,0:T(8,128)S(1)}, f32[4,8,256]{2,1,0:T(8,128)S(1)}, u32[]{:S(2)}, u32[]{:S(2)}) %collective-permute-start.10) | collective-permute-done | bytes 32800 | tf_op jit(solution)/shard_map/ppermute | solution.py:336
  54.9 1.5 %shard_map.60 = (f32[10,8,256]{2,1,0:T(8,128)S(1)}, f32[2,8,256]{2,1,0:T(8,128)S(1)}, f32[8,256]{1,0:T(8,128)S(1)}, f32[8,128]{1,0:T(8,128)S(1)}) custom-call(s32[1,4]{1,0:T(1,128)S(1)} %broadcast_select_fusion.1.nbr, s32[1]{0:T(128)} %bitcast.me, f32[1,24,128]{2,1,0:T(8,128)S(1)} %slice.222.before, f32[8,24,128]{2,1,0:T(8,128)S(1)} %pad_maximum_fusion.table, ...), custom_call_target="tpu_custom_call" | custom-call | tf_op jit(solution)/shard_map/pallas_call | solution.py:406
  56.4 0.2 collective-permute-start.11
  56.6 1.1 %collective-permute-done.11 = f32[6,8,256]{2,1,0:T(8,128)S(1)} collective-permute-done((f32[6,8,256]{2,1,0:T(8,128)S(1)}, f32[6,8,256]{2,1,0:T(8,128)S(1)}, u32[]{:S(2)}, u32[]{:S(2)}) %collective-permute-start.11) | collective-permute-done | bytes 49184 | tf_op jit(solution)/shard_map/ppermute | solution.py:336
  57.7 1.6 %collective-permute-start.12 = (f32[4,8,256]{2,1,0:T(8,128)S(1)}, f32[4,8,256]{2,1,0:T(8,128)S(1)}, u32[]{:S(2)}, u32[]{:S(2)}) collective-permute-start(f32[4,8,256]{2,1,0:T(8,128)S(1)} %pad_maximum_fusion.7), channel_id=1, source_target_pairs={{0,2},{1,3},{2,0},{3,1},{4,6},{5,7},{6,4},{7,5},{8,10},{9,11},{10,... | collective-permute-start | bytes 98312 | tf_op jit(solution)/shard_map/ppermute | solution.py:336
  59.4 2.4 %collective-permute-done.12 = f32[4,8,256]{2,1,0:T(8,128)S(1)} collective-permute-done((f32[4,8,256]{2,1,0:T(8,128)S(1)}, f32[4,8,256]{2,1,0:T(8,128)S(1)}, u32[]{:S(2)}, u32[]{:S(2)}) %collective-permute-start.12) | collective-permute-done | bytes 32800 | tf_op jit(solution)/shard_map/ppermute | solution.py:336
  61.8 2.7 %collective-permute-start.13 = (f32[3,8,256]{2,1,0:T(8,128)S(1)}, f32[3,8,256]{2,1,0:T(8,128)S(1)}, u32[]{:S(2)}, u32[]{:S(2)}) collective-permute-start(f32[3,8,256]{2,1,0:T(8,128)S(1)} %pad_maximum_fusion.11), channel_id=1, source_target_pairs={{0,4},{1,5},{2,6},{3,7},{4,0},{5,1},{6,2},{7,3},{8,12},{9,13},{10,... | collective-permute-start | bytes 73736 | tf_op jit(solution)/shard_map/ppermute | solution.py:336
  64.5 2.1 %collective-permute-done.13 = f32[3,8,256]{2,1,0:T(8,128)S(1)} collective-permute-done((f32[3,8,256]{2,1,0:T(8,128)S(1)}, f32[3,8,256]{2,1,0:T(8,128)S(1)}, u32[]{:S(2)}, u32[]{:S(2)}) %collective-permute-start.13) | collective-permute-done | bytes 24608 | tf_op jit(solution)/shard_map/ppermute | solution.py:336
  66.6 2.1 %collective-permute-start.14 = (f32[3,8,256]{2,1,0:T(8,128)S(1)}, f32[3,8,256]{2,1,0:T(8,128)S(1)}, u32[]{:S(2)}, u32[]{:S(2)}) collective-permute-start(f32[3,8,256]{2,1,0:T(8,128)S(1)} %pad_maximum_fusion.12), channel_id=1, source_target_pairs={{0,8},{8,0},{16,24},{24,16},{1,9},{9,1},{17,25},{25,17},{2,10},{10... | collective-permute-start | bytes 73736 | tf_op jit(solution)/shard_map/ppermute | solution.py:336
  68.6 1.8 %collective-permute-done.14 = f32[3,8,256]{2,1,0:T(8,128)S(1)} collective-permute-done((f32[3,8,256]{2,1,0:T(8,128)S(1)}, f32[3,8,256]{2,1,0:T(8,128)S(1)}, u32[]{:S(2)}, u32[]{:S(2)}) %collective-permute-start.14) | collective-permute-done | bytes 24608 | tf_op jit(solution)/shard_map/ppermute | solution.py:336
  70.5 2.1 %collective-permute-start.15 = (f32[3,8,256]{2,1,0:T(8,128)S(1)}, f32[3,8,256]{2,1,0:T(8,128)S(1)}, u32[]{:S(2)}, u32[]{:S(2)}) collective-permute-start(f32[3,8,256]{2,1,0:T(8,128)S(1)} %pad_maximum_fusion.13), channel_id=1, source_target_pairs={{0,16},{8,24},{16,0},{24,8},{1,17},{9,25},{17,1},{25,9},{2,18},{10... | collective-permute-start | bytes 73736 | tf_op jit(solution)/shard_map/ppermute | solution.py:336
  72.6 1.8 %collective-permute-done.15 = f32[3,8,256]{2,1,0:T(8,128)S(1)} collective-permute-done((f32[3,8,256]{2,1,0:T(8,128)S(1)}, f32[3,8,256]{2,1,0:T(8,128)S(1)}, u32[]{:S(2)}, u32[]{:S(2)}) %collective-permute-start.15) | collective-permute-done | bytes 24608 | tf_op jit(solution)/shard_map/ppermute | solution.py:336
  74.4 1.0 %shard_map.61 = (f32[1,8,256]{2,1,0:T(8,128)}, f32[1,8,256]{2,1,0:T(8,128)}) custom-call(s32[1]{0:T(128)} %bitcast.me, f32[2,8,256]{2,1,0:T(8,128)S(1)} %slice_add_fusion.7.received, f32[1,8,256]{2,1,0:T(8,128)S(1)} %slice_select_fusion.6.shifted, f32[2,8,256]{2,1,0:T(8,128)S(1)} %get-tuple-element.17.images, f32[8,256]{1,0:T(8,128)S(1)} %get-tuple-element.18.residual, ...), custom_call_target="tpu_custom_call" | custom-call | tf_op jit(solution)/shard_map/pallas_call | solution.py:422
  (54 shorter events, 0.3 us)
Async XLA Ops:
  2.1 4.8 %collective-permute-start = (f32[2,24,128]{2,1,0:T(8,128)S(1)}, f32[2,24,128]{2,1,0:T(8,128)S(1)}, u32[]{:S(2)}, u32[]{:S(2)}) collective-permute-start(f32[2,24,128]{2,1,0:T(8,128)S(1)} %pad_maximum_fusion.8), channel_id=1, source_target_pairs={{0,16},{8,24},{16,0},{24,8},{1,17},{9,25},{17,1},{25,9},{2,18},{10... | collective-permute-start | bytes 73736 | tf_op jit(solution)/shard_map/ppermute | solution.py:336
  6.9 3.9 %collective-permute-start.1 = (f32[2,24,128]{2,1,0:T(8,128)S(1)}, f32[2,24,128]{2,1,0:T(8,128)S(1)}, u32[]{:S(2)}, u32[]{:S(2)}) collective-permute-start(f32[2,24,128]{2,1,0:T(8,128)S(1)} %pad_maximum_fusion.9), channel_id=1, source_target_pairs={{0,8},{8,0},{16,24},{24,16},{1,9},{9,1},{17,25},{25,17},{2,10},{10... | collective-permute-start | bytes 73736 | tf_op jit(solution)/shard_map/ppermute | solution.py:336
  10.8 5.0 %collective-permute-start.2 = (f32[2,24,128]{2,1,0:T(8,128)S(1)}, f32[2,24,128]{2,1,0:T(8,128)S(1)}, u32[]{:S(2)}, u32[]{:S(2)}) collective-permute-start(f32[2,24,128]{2,1,0:T(8,128)S(1)} %pad_maximum_fusion.10), channel_id=1, source_target_pairs={{0,4},{1,5},{2,6},{3,7},{4,0},{5,1},{6,2},{7,3},{8,12},{9,13},{10,... | collective-permute-start | bytes 73736 | tf_op jit(solution)/shard_map/ppermute | solution.py:336
  15.8 2.0 %copy-start = (f32[1,8,256]{2,1,0:T(8,128)S(1)}, f32[1,8,256]{2,1,0:T(8,128)}, u32[]{:S(2)}) copy-start(f32[1,8,256]{2,1,0:T(8,128)} %param.7) | copy-start | bytes 24580
  15.8 4.0 %collective-permute-start.3 = (f32[3,24,128]{2,1,0:T(8,128)S(1)}, f32[3,24,128]{2,1,0:T(8,128)S(1)}, u32[]{:S(2)}, u32[]{:S(2)}) collective-permute-start(f32[3,24,128]{2,1,0:T(8,128)S(1)} %pad_maximum_fusion.6), channel_id=1, source_target_pairs={{0,2},{1,3},{2,0},{3,1},{4,6},{5,7},{6,4},{7,5},{8,10},{9,11},{10,... | collective-permute-start | bytes 110600 | tf_op jit(solution)/shard_map/ppermute | solution.py:336
  19.8 0.7 copy-start.1
  19.9 1.3 %collective-permute-start.4 = (f32[5,24,128]{2,1,0:T(8,128)S(1)}, f32[5,24,128]{2,1,0:T(8,128)S(1)}, u32[]{:S(2)}, u32[]{:S(2)}) collective-permute-start(f32[5,24,128]{2,1,0:T(8,128)S(1)} %pad_maximum_fusion.1), channel_id=1, source_target_pairs={{0,1},{1,0},{2,3},{3,2},{4,5},{5,4},{6,7},{7,6},{8,9},{9,8},{10,11... | collective-permute-start | bytes 184328 | tf_op jit(solution)/shard_map/ppermute | solution.py:336
  34.1 1.3 %collective-permute-start.5 = (f32[7,8,256]{2,1,0:T(8,128)S(1)}, f32[7,8,256]{2,1,0:T(8,128)S(1)}, u32[]{:S(2)}, u32[]{:S(2)}) collective-permute-start(f32[7,8,256]{2,1,0:T(8,128)S(1)} %slice.177), channel_id=1, source_target_pairs={{0,1},{1,0},{2,3},{3,2},{4,5},{5,4},{6,7},{7,6},{8,9},{9,8},{10,11... | collective-permute-start | bytes 172040 | tf_op jit(solution)/shard_map/ppermute | solution.py:336
  35.5 4.2 %collective-permute-start.6 = (f32[6,8,256]{2,1,0:T(8,128)S(1)}, f32[6,8,256]{2,1,0:T(8,128)S(1)}, u32[]{:S(2)}, u32[]{:S(2)}) collective-permute-start(f32[6,8,256]{2,1,0:T(8,128)S(1)} %pad_maximum_fusion.2), channel_id=1, source_target_pairs={{0,2},{1,3},{2,0},{3,1},{4,6},{5,7},{6,4},{7,5},{8,10},{9,11},{10,... | collective-permute-start | bytes 147464 | tf_op jit(solution)/shard_map/ppermute | solution.py:336
  39.6 5.5 %collective-permute-start.7 = (f32[6,8,256]{2,1,0:T(8,128)S(1)}, f32[6,8,256]{2,1,0:T(8,128)S(1)}, u32[]{:S(2)}, u32[]{:S(2)}) collective-permute-start(f32[6,8,256]{2,1,0:T(8,128)S(1)} %pad_maximum_fusion.3), channel_id=1, source_target_pairs={{0,4},{1,5},{2,6},{3,7},{4,0},{5,1},{6,2},{7,3},{8,12},{9,13},{10,... | collective-permute-start | bytes 147464 | tf_op jit(solution)/shard_map/ppermute | solution.py:336
  45.1 4.3 %collective-permute-start.8 = (f32[6,8,256]{2,1,0:T(8,128)S(1)}, f32[6,8,256]{2,1,0:T(8,128)S(1)}, u32[]{:S(2)}, u32[]{:S(2)}) collective-permute-start(f32[6,8,256]{2,1,0:T(8,128)S(1)} %pad_maximum_fusion.4), channel_id=1, source_target_pairs={{0,8},{8,0},{16,24},{24,16},{1,9},{9,1},{17,25},{25,17},{2,10},{10... | collective-permute-start | bytes 147464 | tf_op jit(solution)/shard_map/ppermute | solution.py:336
  49.5 4.2 %collective-permute-start.9 = (f32[6,8,256]{2,1,0:T(8,128)S(1)}, f32[6,8,256]{2,1,0:T(8,128)S(1)}, u32[]{:S(2)}, u32[]{:S(2)}) collective-permute-start(f32[6,8,256]{2,1,0:T(8,128)S(1)} %pad_maximum_fusion.5), channel_id=1, source_target_pairs={{0,16},{8,24},{16,0},{24,8},{1,17},{9,25},{17,1},{25,9},{2,18},{10... | collective-permute-start | bytes 147464 | tf_op jit(solution)/shard_map/ppermute | solution.py:336
  53.7 1.2 %collective-permute-start.10 = (f32[4,8,256]{2,1,0:T(8,128)S(1)}, f32[4,8,256]{2,1,0:T(8,128)S(1)}, u32[]{:S(2)}, u32[]{:S(2)}) collective-permute-start(f32[4,8,256]{2,1,0:T(8,128)S(1)} %slice_add_fusion.1.rows), channel_id=1, source_target_pairs={{0,1},{1,0},{2,3},{3,2},{4,5},{5,4},{6,7},{7,6},{8,9},{9,8},{10,11... | collective-permute-start | bytes 98312 | tf_op jit(solution)/shard_map/ppermute | solution.py:336
  56.4 1.3 %collective-permute-start.11 = (f32[6,8,256]{2,1,0:T(8,128)S(1)}, f32[6,8,256]{2,1,0:T(8,128)S(1)}, u32[]{:S(2)}, u32[]{:S(2)}) collective-permute-start(f32[6,8,256]{2,1,0:T(8,128)S(1)} %concatenate.75), channel_id=1, source_target_pairs={{0,1},{1,0},{2,3},{3,2},{4,5},{5,4},{6,7},{7,6},{8,9},{9,8},{10,11... | collective-permute-start | bytes 147464 | tf_op jit(solution)/shard_map/ppermute | solution.py:336
  57.7 4.0 %collective-permute-start.12 = (f32[4,8,256]{2,1,0:T(8,128)S(1)}, f32[4,8,256]{2,1,0:T(8,128)S(1)}, u32[]{:S(2)}, u32[]{:S(2)}) collective-permute-start(f32[4,8,256]{2,1,0:T(8,128)S(1)} %pad_maximum_fusion.7), channel_id=1, source_target_pairs={{0,2},{1,3},{2,0},{3,1},{4,6},{5,7},{6,4},{7,5},{8,10},{9,11},{10,... | collective-permute-start | bytes 98312 | tf_op jit(solution)/shard_map/ppermute | solution.py:336
  61.8 4.8 %collective-permute-start.13 = (f32[3,8,256]{2,1,0:T(8,128)S(1)}, f32[3,8,256]{2,1,0:T(8,128)S(1)}, u32[]{:S(2)}, u32[]{:S(2)}) collective-permute-start(f32[3,8,256]{2,1,0:T(8,128)S(1)} %pad_maximum_fusion.11), channel_id=1, source_target_pairs={{0,4},{1,5},{2,6},{3,7},{4,0},{5,1},{6,2},{7,3},{8,12},{9,13},{10,... | collective-permute-start | bytes 73736 | tf_op jit(solution)/shard_map/ppermute | solution.py:336
  66.6 3.9 %collective-permute-start.14 = (f32[3,8,256]{2,1,0:T(8,128)S(1)}, f32[3,8,256]{2,1,0:T(8,128)S(1)}, u32[]{:S(2)}, u32[]{:S(2)}) collective-permute-start(f32[3,8,256]{2,1,0:T(8,128)S(1)} %pad_maximum_fusion.12), channel_id=1, source_target_pairs={{0,8},{8,0},{16,24},{24,16},{1,9},{9,1},{17,25},{25,17},{2,10},{10... | collective-permute-start | bytes 73736 | tf_op jit(solution)/shard_map/ppermute | solution.py:336
  70.5 3.9 %collective-permute-start.15 = (f32[3,8,256]{2,1,0:T(8,128)S(1)}, f32[3,8,256]{2,1,0:T(8,128)S(1)}, u32[]{:S(2)}, u32[]{:S(2)}) collective-permute-start(f32[3,8,256]{2,1,0:T(8,128)S(1)} %pad_maximum_fusion.13), channel_id=1, source_target_pairs={{0,16},{8,24},{16,0},{24,8},{1,17},{9,25},{17,1},{25,9},{2,18},{10... | collective-permute-start | bytes 73736 | tf_op jit(solution)/shard_map/ppermute | solution.py:336

commit v10 on v9

--- a/solution.py
+++ b/solution.py
@@ -66,7 +66,7 @@
     return levels
 
 
-def inverse(matrix, ahead, guess, beside=()):
+def inverse(matrix, ahead, guess, beside=(), refine=True):
     order = matrix.shape[0]
     rows = lax.broadcasted_iota(jnp.int32, (order, order), 0)
     columns = lax.broadcasted_iota(jnp.int32, (order, order), 1)
@@ -108,6 +108,9 @@
         also(count * level // (always + 1))
     guess[...] = advance(levels[1][0], ahead[...], guess[...], True)[1]
     also(count // (always + 1))
+    if not refine:
+        also(0)
+        return guess[...]
     held = guess[...]
     ahead[...] = -taken(identity, split_fine(matrix), split_fine(held), rows=ROWS)
     also(0)
@@ -189,11 +192,14 @@
     build(0, 0)
     later = [functools.partial(build, i, j) for j in range(own + 1) for i in range(max(j, 1), own + 1)]
     for k in range(own):
-        middle = inverse(columns[k, at(k)], ahead, guess, later if k == 0 else ())
+        middle = split(inverse(columns[k, at(k)], ahead, guess, later if k == 0 else (), refine=False))
         side = columns[k, at(k + 1, own + 1)]
-        below = -taken(jnp.zeros_like(side), split_fine(side), split_fine(middle))
+        side_parts = split(side)
+        rough = -taken(jnp.zeros_like(side), side_parts, middle)
+        rest = taken(side, split_fine(rough), split_fine(columns[k, at(k)]))
+        below = taken(rough, split(-rest), middle)
         lower[k, at(k + 1, own + 1)] = below
-        side_parts, below_parts = split(side), split(below)
+        below_parts = split(below)
         for j in range(k + 1, own + 1):
             cut = (j - k - 1) * points
             left = [piece[cut:] for piece in below_parts]

time: 75.9 us -> 76.1 us (level)
  waiting for transfers between devices: 28.1 us -> 30.7 us
  starting transfers between devices: 28.8 us -> 27 us
    ppermute x16, waiting for transfers between devices: 28.1 us -> 30.7 us  [swapped(): lax.ppermute(value, axis, [(at, at ^ reach) for at in range(lax.axis_size...]
    ppermute x16, starting transfers between devices: 28.8 us -> 27 us  [swapped(): lax.ppermute(value, axis, [(at, at ^ reach) for at in range(lax.axis_size...]
where the time goes in v10:
time: 76.1 us
  waiting for transfers between devices  30.7 us (40%)
  starting transfers between devices  27 us (35%)
  Pallas kernels  15.3 us (20%)
  local copies, waits for them, and re-layouts  2.07 us (3%)
  between operations  0.82 us (1%)
    ppermute x16, waiting for transfers between devices, swapped(): lax.ppermute(value, axis, [(at, at ^ reach) for at in range(lax.axis_size...  30.7 us
    ppermute x16, starting transfers between devices, swapped(): lax.ppermute(value, axis, [(at, at ^ reach) for at in range(lax.axis_size...  27 us
    pallas_call x1, Pallas kernels, local(): call(factor_kernel, sizes, [(coarse + 3,) + tile] + [jax.ShapeDtypeStruct...  12.8 us
  transfers between devices with their start and end apart: 16, of which 16 were waited for; matrix products, arithmetic and copies ran while one was open for 0% of the time, Pallas kernels for 0%

profile of v10, /device:TPU:0, one launch (start us, length us, event | category | flops | bytes accessed | tf_op | source)
XLA Modules:
  0.0 76.1 jit_solution(3394824028588924710)
XLA Ops:
  0.6 0.7 fusion.3
  1.3 0.7 slice_bitcast_fusion
  2.1 3.0 %collective-permute-start = (f32[2,24,128]{2,1,0:T(8,128)S(1)}, f32[2,24,128]{2,1,0:T(8,128)S(1)}, u32[]{:S(2)}, u32[]{:S(2)}) collective-permute-start(f32[2,24,128]{2,1,0:T(8,128)S(1)} %pad_maximum_fusion.8), channel_id=1, source_target_pairs={{0,16},{8,24},{16,0},{24,8},{1,17},{9,25},{17,1},{25,9},{2,18},{10... | collective-permute-start | bytes 73736 | tf_op jit(solution)/shard_map/ppermute | solution.py:342
  5.1 1.8 %collective-permute-done = f32[2,24,128]{2,1,0:T(8,128)S(1)} collective-permute-done((f32[2,24,128]{2,1,0:T(8,128)S(1)}, f32[2,24,128]{2,1,0:T(8,128)S(1)}, u32[]{:S(2)}, u32[]{:S(2)}) %collective-permute-start) | collective-permute-done | bytes 24608 | tf_op jit(solution)/shard_map/ppermute | solution.py:342
  6.9 2.1 %collective-permute-start.1 = (f32[2,24,128]{2,1,0:T(8,128)S(1)}, f32[2,24,128]{2,1,0:T(8,128)S(1)}, u32[]{:S(2)}, u32[]{:S(2)}) collective-permute-start(f32[2,24,128]{2,1,0:T(8,128)S(1)} %pad_maximum_fusion.9), channel_id=1, source_target_pairs={{0,8},{8,0},{16,24},{24,16},{1,9},{9,1},{17,25},{25,17},{2,10},{10... | collective-permute-start | bytes 73736 | tf_op jit(solution)/shard_map/ppermute | solution.py:342
  9.0 1.8 %collective-permute-done.1 = f32[2,24,128]{2,1,0:T(8,128)S(1)} collective-permute-done((f32[2,24,128]{2,1,0:T(8,128)S(1)}, f32[2,24,128]{2,1,0:T(8,128)S(1)}, u32[]{:S(2)}, u32[]{:S(2)}) %collective-permute-start.1) | collective-permute-done | bytes 24608 | tf_op jit(solution)/shard_map/ppermute | solution.py:342
  10.8 3.2 %collective-permute-start.2 = (f32[2,24,128]{2,1,0:T(8,128)S(1)}, f32[2,24,128]{2,1,0:T(8,128)S(1)}, u32[]{:S(2)}, u32[]{:S(2)}) collective-permute-start(f32[2,24,128]{2,1,0:T(8,128)S(1)} %pad_maximum_fusion.10), channel_id=1, source_target_pairs={{0,4},{1,5},{2,6},{3,7},{4,0},{5,1},{6,2},{7,3},{8,12},{9,13},{10,... | collective-permute-start | bytes 73736 | tf_op jit(solution)/shard_map/ppermute | solution.py:342
  14.0 1.8 %collective-permute-done.2 = f32[2,24,128]{2,1,0:T(8,128)S(1)} collective-permute-done((f32[2,24,128]{2,1,0:T(8,128)S(1)}, f32[2,24,128]{2,1,0:T(8,128)S(1)}, u32[]{:S(2)}, u32[]{:S(2)}) %collective-permute-start.2) | collective-permute-done | bytes 24608 | tf_op jit(solution)/shard_map/ppermute | solution.py:342
  15.8 0.0 copy-start
  15.8 2.0 %collective-permute-start.3 = (f32[3,24,128]{2,1,0:T(8,128)S(1)}, f32[3,24,128]{2,1,0:T(8,128)S(1)}, u32[]{:S(2)}, u32[]{:S(2)}) collective-permute-start(f32[3,24,128]{2,1,0:T(8,128)S(1)} %pad_maximum_fusion.6), channel_id=1, source_target_pairs={{0,2},{1,3},{2,0},{3,1},{4,6},{5,7},{6,4},{7,5},{8,10},{9,11},{10,... | collective-permute-start | bytes 110600 | tf_op jit(solution)/shard_map/ppermute | solution.py:342
  17.8 0.0 copy-done
  17.8 2.0 %collective-permute-done.3 = f32[3,24,128]{2,1,0:T(8,128)S(1)} collective-permute-done((f32[3,24,128]{2,1,0:T(8,128)S(1)}, f32[3,24,128]{2,1,0:T(8,128)S(1)}, u32[]{:S(2)}, u32[]{:S(2)}) %collective-permute-start.3) | collective-permute-done | bytes 36896 | tf_op jit(solution)/shard_map/ppermute | solution.py:342
  19.8 0.0 copy-start.1
  19.9 0.1 collective-permute-start.4
  19.9 0.6 copy-done.1
  20.5 0.7 collective-permute-done.4
  21.2 12.8 %shard_map.59 = (f32[11,8,256]{2,1,0:T(8,128)S(1)}, bf16[256,768]{1,0:T(8,128)(2,1)S(1)}, bf16[256,768]{1,0:T(8,128)(2,1)S(1)}, bf16[256,256]{1,0:T(8,128)(2,1)S(1)}, bf16[256,256]{1,0:T(8,128)(2,1)S(1)}) custom-call(s32[1,4]{1,0:T(1,128)S(1)} %broadcast_select_fusion.1.nbr, s32[1]{0:T(128)} %bitcast.me, f32[1,24,128]{2,1,0:T(8,128)S(1)} %slice.222.before, ...), custom_call_target="tpu_custom_call" | custom-call | tf_op jit(solution)/shard_map/pallas_call | solution.py:394
  34.0 0.6 collective-permute-start.5
  34.6 0.9 %collective-permute-done.5 = f32[7,8,256]{2,1,0:T(8,128)S(1)} collective-permute-done((f32[7,8,256]{2,1,0:T(8,128)S(1)}, f32[7,8,256]{2,1,0:T(8,128)S(1)}, u32[]{:S(2)}, u32[]{:S(2)}) %collective-permute-start.5) | collective-permute-done | bytes 57376 | tf_op jit(solution)/shard_map/ppermute | solution.py:342
  35.6 2.6 %collective-permute-start.6 = (f32[6,8,256]{2,1,0:T(8,128)S(1)}, f32[6,8,256]{2,1,0:T(8,128)S(1)}, u32[]{:S(2)}, u32[]{:S(2)}) collective-permute-start(f32[6,8,256]{2,1,0:T(8,128)S(1)} %pad_maximum_fusion.2), channel_id=1, source_target_pairs={{0,2},{1,3},{2,0},{3,1},{4,6},{5,7},{6,4},{7,5},{8,10},{9,11},{10,... | collective-permute-start | bytes 147464 | tf_op jit(solution)/shard_map/ppermute | solution.py:342
  38.2 2.3 %collective-permute-done.6 = f32[6,8,256]{2,1,0:T(8,128)S(1)} collective-permute-done((f32[6,8,256]{2,1,0:T(8,128)S(1)}, f32[6,8,256]{2,1,0:T(8,128)S(1)}, u32[]{:S(2)}, u32[]{:S(2)}) %collective-permute-start.6) | collective-permute-done | bytes 49184 | tf_op jit(solution)/shard_map/ppermute | solution.py:342
  40.4 3.2 %collective-permute-start.7 = (f32[6,8,256]{2,1,0:T(8,128)S(1)}, f32[6,8,256]{2,1,0:T(8,128)S(1)}, u32[]{:S(2)}, u32[]{:S(2)}) collective-permute-start(f32[6,8,256]{2,1,0:T(8,128)S(1)} %pad_maximum_fusion.3), channel_id=1, source_target_pairs={{0,4},{1,5},{2,6},{3,7},{4,0},{5,1},{6,2},{7,3},{8,12},{9,13},{10,... | collective-permute-start | bytes 147464 | tf_op jit(solution)/shard_map/ppermute | solution.py:342
  43.6 2.4 %collective-permute-done.7 = f32[6,8,256]{2,1,0:T(8,128)S(1)} collective-permute-done((f32[6,8,256]{2,1,0:T(8,128)S(1)}, f32[6,8,256]{2,1,0:T(8,128)S(1)}, u32[]{:S(2)}, u32[]{:S(2)}) %collective-permute-start.7) | collective-permute-done | bytes 49184 | tf_op jit(solution)/shard_map/ppermute | solution.py:342
  46.0 1.6 %collective-permute-start.8 = (f32[6,8,256]{2,1,0:T(8,128)S(1)}, f32[6,8,256]{2,1,0:T(8,128)S(1)}, u32[]{:S(2)}, u32[]{:S(2)}) collective-permute-start(f32[6,8,256]{2,1,0:T(8,128)S(1)} %pad_maximum_fusion.4), channel_id=1, source_target_pairs={{0,8},{8,0},{16,24},{24,16},{1,9},{9,1},{17,25},{25,17},{2,10},{10... | collective-permute-start | bytes 147464 | tf_op jit(solution)/shard_map/ppermute | solution.py:342
  47.6 2.6 %collective-permute-done.8 = f32[6,8,256]{2,1,0:T(8,128)S(1)} collective-permute-done((f32[6,8,256]{2,1,0:T(8,128)S(1)}, f32[6,8,256]{2,1,0:T(8,128)S(1)}, u32[]{:S(2)}, u32[]{:S(2)}) %collective-permute-start.8) | collective-permute-done | bytes 49184 | tf_op jit(solution)/shard_map/ppermute | solution.py:342
  50.2 1.3 %collective-permute-start.9 = (f32[6,8,256]{2,1,0:T(8,128)S(1)}, f32[6,8,256]{2,1,0:T(8,128)S(1)}, u32[]{:S(2)}, u32[]{:S(2)}) collective-permute-start(f32[6,8,256]{2,1,0:T(8,128)S(1)} %pad_maximum_fusion.5), channel_id=1, source_target_pairs={{0,16},{8,24},{16,0},{24,8},{1,17},{9,25},{17,1},{25,9},{2,18},{10... | collective-permute-start | bytes 147464 | tf_op jit(solution)/shard_map/ppermute | solution.py:342
  51.5 2.9 %collective-permute-done.9 = f32[6,8,256]{2,1,0:T(8,128)S(1)} collective-permute-done((f32[6,8,256]{2,1,0:T(8,128)S(1)}, f32[6,8,256]{2,1,0:T(8,128)S(1)}, u32[]{:S(2)}, u32[]{:S(2)}) %collective-permute-start.9) | collective-permute-done | bytes 49184 | tf_op jit(solution)/shard_map/ppermute | solution.py:342
  54.4 0.0 collective-permute-start.10
  54.4 1.2 %collective-permute-done.10.other_rows = f32[4,8,256]{2,1,0:T(8,128)S(1)} collective-permute-done((f32[4,8,256]{2,1,0:T(8,128)S(1)}, f32[4,8,256]{2,1,0:T(8,128)S(1)}, u32[]{:S(2)}, u32[]{:S(2)}) %collective-permute-start.10) | collective-permute-done | bytes 32800 | tf_op jit(solution)/shard_map/ppermute | solution.py:342
  55.6 1.5 %shard_map.60 = (f32[10,8,256]{2,1,0:T(8,128)S(1)}, f32[2,8,256]{2,1,0:T(8,128)S(1)}, f32[8,256]{1,0:T(8,128)S(1)}, f32[8,128]{1,0:T(8,128)S(1)}) custom-call(s32[1,4]{1,0:T(1,128)S(1)} %broadcast_select_fusion.1.nbr, s32[1]{0:T(128)} %bitcast.me, f32[1,24,128]{2,1,0:T(8,128)S(1)} %slice.222.before, f32[8,24,128]{2,1,0:T(8,128)S(1)} %pad_maximum_fusion.table, ...), custom_call_target="tpu_custom_call" | custom-call | tf_op jit(solution)/shard_map/pallas_call | solution.py:412
  57.1 0.2 collective-permute-start.11
  57.3 1.1 %collective-permute-done.11 = f32[6,8,256]{2,1,0:T(8,128)S(1)} collective-permute-done((f32[6,8,256]{2,1,0:T(8,128)S(1)}, f32[6,8,256]{2,1,0:T(8,128)S(1)}, u32[]{:S(2)}, u32[]{:S(2)}) %collective-permute-start.11) | collective-permute-done | bytes 49184 | tf_op jit(solution)/shard_map/ppermute | solution.py:342
  58.4 1.6 %collective-permute-start.12 = (f32[4,8,256]{2,1,0:T(8,128)S(1)}, f32[4,8,256]{2,1,0:T(8,128)S(1)}, u32[]{:S(2)}, u32[]{:S(2)}) collective-permute-start(f32[4,8,256]{2,1,0:T(8,128)S(1)} %pad_maximum_fusion.7), channel_id=1, source_target_pairs={{0,2},{1,3},{2,0},{3,1},{4,6},{5,7},{6,4},{7,5},{8,10},{9,11},{10,... | collective-permute-start | bytes 98312 | tf_op jit(solution)/shard_map/ppermute | solution.py:342
  60.0 2.4 %collective-permute-done.12 = f32[4,8,256]{2,1,0:T(8,128)S(1)} collective-permute-done((f32[4,8,256]{2,1,0:T(8,128)S(1)}, f32[4,8,256]{2,1,0:T(8,128)S(1)}, u32[]{:S(2)}, u32[]{:S(2)}) %collective-permute-start.12) | collective-permute-done | bytes 32800 | tf_op jit(solution)/shard_map/ppermute | solution.py:342
  62.4 2.7 %collective-permute-start.13 = (f32[3,8,256]{2,1,0:T(8,128)S(1)}, f32[3,8,256]{2,1,0:T(8,128)S(1)}, u32[]{:S(2)}, u32[]{:S(2)}) collective-permute-start(f32[3,8,256]{2,1,0:T(8,128)S(1)} %pad_maximum_fusion.11), channel_id=1, source_target_pairs={{0,4},{1,5},{2,6},{3,7},{4,0},{5,1},{6,2},{7,3},{8,12},{9,13},{10,... | collective-permute-start | bytes 73736 | tf_op jit(solution)/shard_map/ppermute | solution.py:342
  65.1 2.1 %collective-permute-done.13 = f32[3,8,256]{2,1,0:T(8,128)S(1)} collective-permute-done((f32[3,8,256]{2,1,0:T(8,128)S(1)}, f32[3,8,256]{2,1,0:T(8,128)S(1)}, u32[]{:S(2)}, u32[]{:S(2)}) %collective-permute-start.13) | collective-permute-done | bytes 24608 | tf_op jit(solution)/shard_map/ppermute | solution.py:342
  67.2 1.7 %collective-permute-start.14 = (f32[3,8,256]{2,1,0:T(8,128)S(1)}, f32[3,8,256]{2,1,0:T(8,128)S(1)}, u32[]{:S(2)}, u32[]{:S(2)}) collective-permute-start(f32[3,8,256]{2,1,0:T(8,128)S(1)} %pad_maximum_fusion.12), channel_id=1, source_target_pairs={{0,8},{8,0},{16,24},{24,16},{1,9},{9,1},{17,25},{25,17},{2,10},{10... | collective-permute-start | bytes 73736 | tf_op jit(solution)/shard_map/ppermute | solution.py:342
  68.9 2.2 %collective-permute-done.14 = f32[3,8,256]{2,1,0:T(8,128)S(1)} collective-permute-done((f32[3,8,256]{2,1,0:T(8,128)S(1)}, f32[3,8,256]{2,1,0:T(8,128)S(1)}, u32[]{:S(2)}, u32[]{:S(2)}) %collective-permute-start.14) | collective-permute-done | bytes 24608 | tf_op jit(solution)/shard_map/ppermute | solution.py:342
  71.2 1.3 %collective-permute-start.15 = (f32[3,8,256]{2,1,0:T(8,128)S(1)}, f32[3,8,256]{2,1,0:T(8,128)S(1)}, u32[]{:S(2)}, u32[]{:S(2)}) collective-permute-start(f32[3,8,256]{2,1,0:T(8,128)S(1)} %pad_maximum_fusion.13), channel_id=1, source_target_pairs={{0,16},{8,24},{16,0},{24,8},{1,17},{9,25},{17,1},{25,9},{2,18},{10... | collective-permute-start | bytes 73736 | tf_op jit(solution)/shard_map/ppermute | solution.py:342
  72.5 2.6 %collective-permute-done.15 = f32[3,8,256]{2,1,0:T(8,128)S(1)} collective-permute-done((f32[3,8,256]{2,1,0:T(8,128)S(1)}, f32[3,8,256]{2,1,0:T(8,128)S(1)}, u32[]{:S(2)}, u32[]{:S(2)}) %collective-permute-start.15) | collective-permute-done | bytes 24608 | tf_op jit(solution)/shard_map/ppermute | solution.py:342
  75.1 1.0 %shard_map.61 = (f32[1,8,256]{2,1,0:T(8,128)}, f32[1,8,256]{2,1,0:T(8,128)}) custom-call(s32[1]{0:T(128)} %bitcast.me, f32[2,8,256]{2,1,0:T(8,128)S(1)} %slice_add_fusion.7.received, f32[1,8,256]{2,1,0:T(8,128)S(1)} %slice_select_fusion.6.shifted, f32[2,8,256]{2,1,0:T(8,128)S(1)} %get-tuple-element.17.images, f32[8,256]{1,0:T(8,128)S(1)} %get-tuple-element.18.residual, ...), custom_call_target="tpu_custom_call" | custom-call | tf_op jit(solution)/shard_map/pallas_call | solution.py:428
  (54 shorter events, 0.3 us)
Async XLA Ops:
  2.1 4.8 %collective-permute-start = (f32[2,24,128]{2,1,0:T(8,128)S(1)}, f32[2,24,128]{2,1,0:T(8,128)S(1)}, u32[]{:S(2)}, u32[]{:S(2)}) collective-permute-start(f32[2,24,128]{2,1,0:T(8,128)S(1)} %pad_maximum_fusion.8), channel_id=1, source_target_pairs={{0,16},{8,24},{16,0},{24,8},{1,17},{9,25},{17,1},{25,9},{2,18},{10... | collective-permute-start | bytes 73736 | tf_op jit(solution)/shard_map/ppermute | solution.py:342
  6.9 3.9 %collective-permute-start.1 = (f32[2,24,128]{2,1,0:T(8,128)S(1)}, f32[2,24,128]{2,1,0:T(8,128)S(1)}, u32[]{:S(2)}, u32[]{:S(2)}) collective-permute-start(f32[2,24,128]{2,1,0:T(8,128)S(1)} %pad_maximum_fusion.9), channel_id=1, source_target_pairs={{0,8},{8,0},{16,24},{24,16},{1,9},{9,1},{17,25},{25,17},{2,10},{10... | collective-permute-start | bytes 73736 | tf_op jit(solution)/shard_map/ppermute | solution.py:342
  10.8 5.0 %collective-permute-start.2 = (f32[2,24,128]{2,1,0:T(8,128)S(1)}, f32[2,24,128]{2,1,0:T(8,128)S(1)}, u32[]{:S(2)}, u32[]{:S(2)}) collective-permute-start(f32[2,24,128]{2,1,0:T(8,128)S(1)} %pad_maximum_fusion.10), channel_id=1, source_target_pairs={{0,4},{1,5},{2,6},{3,7},{4,0},{5,1},{6,2},{7,3},{8,12},{9,13},{10,... | collective-permute-start | bytes 73736 | tf_op jit(solution)/shard_map/ppermute | solution.py:342
  15.8 2.0 %copy-start = (f32[1,8,256]{2,1,0:T(8,128)S(1)}, f32[1,8,256]{2,1,0:T(8,128)}, u32[]{:S(2)}) copy-start(f32[1,8,256]{2,1,0:T(8,128)} %param.7) | copy-start | bytes 24580
  15.8 4.0 %collective-permute-start.3 = (f32[3,24,128]{2,1,0:T(8,128)S(1)}, f32[3,24,128]{2,1,0:T(8,128)S(1)}, u32[]{:S(2)}, u32[]{:S(2)}) collective-permute-start(f32[3,24,128]{2,1,0:T(8,128)S(1)} %pad_maximum_fusion.6), channel_id=1, source_target_pairs={{0,2},{1,3},{2,0},{3,1},{4,6},{5,7},{6,4},{7,5},{8,10},{9,11},{10,... | collective-permute-start | bytes 110600 | tf_op jit(solution)/shard_map/ppermute | solution.py:342
  19.8 0.7 copy-start.1
  19.9 1.3 %collective-permute-start.4 = (f32[5,24,128]{2,1,0:T(8,128)S(1)}, f32[5,24,128]{2,1,0:T(8,128)S(1)}, u32[]{:S(2)}, u32[]{:S(2)}) collective-permute-start(f32[5,24,128]{2,1,0:T(8,128)S(1)} %pad_maximum_fusion.1), channel_id=1, source_target_pairs={{0,1},{1,0},{2,3},{3,2},{4,5},{5,4},{6,7},{7,6},{8,9},{9,8},{10,11... | collective-permute-start | bytes 184328 | tf_op jit(solution)/shard_map/ppermute | solution.py:342
  34.0 1.5 %collective-permute-start.5 = (f32[7,8,256]{2,1,0:T(8,128)S(1)}, f32[7,8,256]{2,1,0:T(8,128)S(1)}, u32[]{:S(2)}, u32[]{:S(2)}) collective-permute-start(f32[7,8,256]{2,1,0:T(8,128)S(1)} %slice.177), channel_id=1, source_target_pairs={{0,1},{1,0},{2,3},{3,2},{4,5},{5,4},{6,7},{7,6},{8,9},{9,8},{10,11... | collective-permute-start | bytes 172040 | tf_op jit(solution)/shard_map/ppermute | solution.py:342
  35.6 4.9 %collective-permute-start.6 = (f32[6,8,256]{2,1,0:T(8,128)S(1)}, f32[6,8,256]{2,1,0:T(8,128)S(1)}, u32[]{:S(2)}, u32[]{:S(2)}) collective-permute-start(f32[6,8,256]{2,1,0:T(8,128)S(1)} %pad_maximum_fusion.2), channel_id=1, source_target_pairs={{0,2},{1,3},{2,0},{3,1},{4,6},{5,7},{6,4},{7,5},{8,10},{9,11},{10,... | collective-permute-start | bytes 147464 | tf_op jit(solution)/shard_map/ppermute | solution.py:342
  40.4 5.5 %collective-permute-start.7 = (f32[6,8,256]{2,1,0:T(8,128)S(1)}, f32[6,8,256]{2,1,0:T(8,128)S(1)}, u32[]{:S(2)}, u32[]{:S(2)}) collective-permute-start(f32[6,8,256]{2,1,0:T(8,128)S(1)} %pad_maximum_fusion.3), channel_id=1, source_target_pairs={{0,4},{1,5},{2,6},{3,7},{4,0},{5,1},{6,2},{7,3},{8,12},{9,13},{10,... | collective-permute-start | bytes 147464 | tf_op jit(solution)/shard_map/ppermute | solution.py:342
  46.0 4.2 %collective-permute-start.8 = (f32[6,8,256]{2,1,0:T(8,128)S(1)}, f32[6,8,256]{2,1,0:T(8,128)S(1)}, u32[]{:S(2)}, u32[]{:S(2)}) collective-permute-start(f32[6,8,256]{2,1,0:T(8,128)S(1)} %pad_maximum_fusion.4), channel_id=1, source_target_pairs={{0,8},{8,0},{16,24},{24,16},{1,9},{9,1},{17,25},{25,17},{2,10},{10... | collective-permute-start | bytes 147464 | tf_op jit(solution)/shard_map/ppermute | solution.py:342
  50.2 4.2 %collective-permute-start.9 = (f32[6,8,256]{2,1,0:T(8,128)S(1)}, f32[6,8,256]{2,1,0:T(8,128)S(1)}, u32[]{:S(2)}, u32[]{:S(2)}) collective-permute-start(f32[6,8,256]{2,1,0:T(8,128)S(1)} %pad_maximum_fusion.5), channel_id=1, source_target_pairs={{0,16},{8,24},{16,0},{24,8},{1,17},{9,25},{17,1},{25,9},{2,18},{10... | collective-permute-start | bytes 147464 | tf_op jit(solution)/shard_map/ppermute | solution.py:342
  54.4 1.2 %collective-permute-start.10 = (f32[4,8,256]{2,1,0:T(8,128)S(1)}, f32[4,8,256]{2,1,0:T(8,128)S(1)}, u32[]{:S(2)}, u32[]{:S(2)}) collective-permute-start(f32[4,8,256]{2,1,0:T(8,128)S(1)} %slice_add_fusion.1.rows), channel_id=1, source_target_pairs={{0,1},{1,0},{2,3},{3,2},{4,5},{5,4},{6,7},{7,6},{8,9},{9,8},{10,11... | collective-permute-start | bytes 98312 | tf_op jit(solution)/shard_map/ppermute | solution.py:342
  57.1 1.3 %collective-permute-start.11 = (f32[6,8,256]{2,1,0:T(8,128)S(1)}, f32[6,8,256]{2,1,0:T(8,128)S(1)}, u32[]{:S(2)}, u32[]{:S(2)}) collective-permute-start(f32[6,8,256]{2,1,0:T(8,128)S(1)} %concatenate.75), channel_id=1, source_target_pairs={{0,1},{1,0},{2,3},{3,2},{4,5},{5,4},{6,7},{7,6},{8,9},{9,8},{10,11... | collective-permute-start | bytes 147464 | tf_op jit(solution)/shard_map/ppermute | solution.py:342
  58.4 4.0 %collective-permute-start.12 = (f32[4,8,256]{2,1,0:T(8,128)S(1)}, f32[4,8,256]{2,1,0:T(8,128)S(1)}, u32[]{:S(2)}, u32[]{:S(2)}) collective-permute-start(f32[4,8,256]{2,1,0:T(8,128)S(1)} %pad_maximum_fusion.7), channel_id=1, source_target_pairs={{0,2},{1,3},{2,0},{3,1},{4,6},{5,7},{6,4},{7,5},{8,10},{9,11},{10,... | collective-permute-start | bytes 98312 | tf_op jit(solution)/shard_map/ppermute | solution.py:342
  62.4 4.8 %collective-permute-start.13 = (f32[3,8,256]{2,1,0:T(8,128)S(1)}, f32[3,8,256]{2,1,0:T(8,128)S(1)}, u32[]{:S(2)}, u32[]{:S(2)}) collective-permute-start(f32[3,8,256]{2,1,0:T(8,128)S(1)} %pad_maximum_fusion.11), channel_id=1, source_target_pairs={{0,4},{1,5},{2,6},{3,7},{4,0},{5,1},{6,2},{7,3},{8,12},{9,13},{10,... | collective-permute-start | bytes 73736 | tf_op jit(solution)/shard_map/ppermute | solution.py:342
  67.2 3.9 %collective-permute-start.14 = (f32[3,8,256]{2,1,0:T(8,128)S(1)}, f32[3,8,256]{2,1,0:T(8,128)S(1)}, u32[]{:S(2)}, u32[]{:S(2)}) collective-permute-start(f32[3,8,256]{2,1,0:T(8,128)S(1)} %pad_maximum_fusion.12), channel_id=1, source_target_pairs={{0,8},{8,0},{16,24},{24,16},{1,9},{9,1},{17,25},{25,17},{2,10},{10... | collective-permute-start | bytes 73736 | tf_op jit(solution)/shard_map/ppermute | solution.py:342
  71.2 3.9 %collective-permute-start.15 = (f32[3,8,256]{2,1,0:T(8,128)S(1)}, f32[3,8,256]{2,1,0:T(8,128)S(1)}, u32[]{:S(2)}, u32[]{:S(2)}) collective-permute-start(f32[3,8,256]{2,1,0:T(8,128)S(1)} %pad_maximum_fusion.13), channel_id=1, source_target_pairs={{0,16},{8,24},{16,0},{24,8},{1,17},{9,25},{17,1},{25,9},{2,18},{10... | collective-permute-start | bytes 73736 | tf_op jit(solution)/shard_map/ppermute | solution.py:342
